TPU v7x, 32 devices: a whole 2x2x4 slice. The times are simulated.
32 devices in a mesh: tm: 8 (over z, x), rows: 4 (over y, core).
Axes of the slice: x: 2, y: 2, z: 4, core: 2. Of those that a mesh axis runs over, the one named last changes fastest.
Arguments:
- video: bfloat16 [64, 32, 128, 128], P('tm', 'rows'), may hold values from -36 to 50
- conv_weight: bfloat16 [3, 3, 3, 128, 256], replicated, may hold values from -0.109375 to 0.109375
- norm_gain: float32 [256], replicated, may hold values from 0.5 to 1.5
- norm_bias: float32 [256], replicated, may hold values from -3 to 3
Outputs:
- patch_tokens: bfloat16 [16, 64, 64, 1024], P('rows', 'tm')
All inputs are finite; a program needn't handle non-finite values.
Results may differ from a plain program's by a relative error of at most 0.0049.
Values may be sent and summed in bfloat16 or wider, within the bound.
No kernel may reach another device: no remote copies, remote signals or barrier semaphores. Data moves between devices by JAX's collectives and lax.ppermute only.
A program may use at most 128 MiB of HBM per device.

v0:
```python
import jax
import jax.numpy as jnp
from jax import lax
from jax.sharding import PartitionSpec as P

GROUPS = 32


inv_root = 0.7071067811865476


def from_partner(block, axis, distance):
    count = lax.axis_size(axis)
    route = []
    for low in range(count):
        high = low | 1 << distance
        if high != low and high < count:
            route += [(low, high), (high, low)]
    return lax.ppermute(block, axis, route)


def shifted(block, axis, distance):
    devices = range(lax.axis_size(axis))
    route = [(i - distance, i) for i in devices if i - distance in devices]
    return lax.ppermute(block, axis, route)


def padded_2(cells, sides, width):
    for axis, dim in sides:
        count = lax.axis_size(axis)
        ends = count - 1
        head = lax.slice_in_dim(cells, 0, width, axis=dim)
        tail = lax.slice_in_dim(cells, cells.shape[dim] - width, cells.shape[dim], axis=dim)
        cells = jnp.concatenate(
            [
                lax.ppermute(tail, axis, [(i, (i + 1) % count) for i in range(ends)]),
                cells,
                lax.ppermute(head, axis, [((i + 1) % count, i) for i in range(ends)]),
            ],
            axis=dim,
        )
    return cells


def per_device(video, conv_weight, norm_gain, norm_bias):
    frames, height, width, channels = video.shape
    tm_count = lax.axis_size("tm")
    current = video.astype(jnp.float32)
    position = lax.axis_index("tm")
    for bit_number in range(3):
        partner = from_partner(current, "tm", bit_number)
        is_upper = position >> bit_number & 1 == 1
        current = jnp.where(
            is_upper, (partner - current) * inv_root, (current + partner) * inv_root
        )
    wavelet = current.astype(jnp.bfloat16)
    last_frames = wavelet[frames - 2 :]
    earlier = shifted(last_frames, "tm", 1)
    extended = jnp.concatenate([earlier, wavelet], axis=0)
    with_rows = padded_2(extended, (("rows", 1),), 1)
    padded = jnp.pad(with_rows, ((0, 0), (0, 0), (1, 1), (0, 0)))
    convolved = lax.conv_general_dilated(
        padded[None],
        conv_weight,
        (1, 1, 1),
        "VALID",
        dimension_numbers=("NDHWC", "DHWIO", "NDHWC"),
        preferred_element_type=jnp.float32,
    )[0]
    out_frames, out_height, out_width, out_channels = convolved.shape
    group_count = GROUPS
    groups = convolved.reshape(
        out_frames, out_height, out_width, group_count, out_channels // group_count
    )
    entries = float(
        out_frames
        * out_height
        * out_width
        * (out_channels // group_count)
        * tm_count
        * lax.axis_size("rows")
    )
    local_sums = jnp.sum(groups, axis=(0, 1, 2, 4))
    group_total = lax.psum(local_sums, ("tm", "rows"))
    group_mean = group_total / entries
    centered = groups - group_mean[:, None]
    squares = lax.psum(jnp.sum(centered * centered, axis=(0, 1, 2, 4)), ("tm", "rows"))
    variance = squares / entries
    normed = (centered / jnp.sqrt(variance + 1e-05)[:, None]).reshape(
        out_frames, out_height, out_width, out_channels
    )
    activated = jax.nn.silu(normed * norm_gain + norm_bias).astype(jnp.bfloat16)
    arranged = activated.reshape(
        out_frames, out_height // 2, 2, out_width // 2, 2, out_channels
    ).transpose(1, 3, 0, 2, 4, 5)
    arranged = arranged.reshape(out_height // 2, out_width // 2, out_frames, 4 * out_channels)
    return lax.all_to_all(arranged, "tm", split_axis=1, concat_axis=2, tiled=True)


def solution(mesh):
    placed = (P("tm", "rows", None, None), P(), P(), P())
    return jax.shard_map(
        per_device,
        mesh=mesh,
        in_specs=placed,
        out_specs=P("rows", "tm", None, None),
        check_vma=False,
    )
```

profile of v0, /device:TPU:0, one launch (start us, length us, event | category | flops | bytes accessed | tf_op | source)
XLA Modules:
  0.0 674.7 jit_solution(13683090357064641958)
XLA Ops:
  0.0 0.0 copy-start
  0.0 4.3 convert_element_type.12
  4.3 2.9 collective-permute-start
  7.2 90.9 %collective-permute-done = f32[8,8,128,128]{3,2,1,0:T(8,128)} collective-permute-done((f32[8,8,128,128]{3,2,1,0:T(8,128)}, f32[8,8,128,128]{3,2,1,0:T(8,128)}, u32[]{:S(2)}, u32[]{:S(2)}) %collective-permute-start) | collective-permute-done | bytes 4194336 | tf_op jit(solution)/shard_map/ppermute | solution.py:19
  98.1 5.9 multiply_select_fusion.1
  104.0 1.8 collective-permute-start.1
  105.8 90.2 %collective-permute-done.1 = f32[8,8,128,128]{3,2,1,0:T(8,128)} collective-permute-done((f32[8,8,128,128]{3,2,1,0:T(8,128)}, f32[8,8,128,128]{3,2,1,0:T(8,128)}, u32[]{:S(2)}, u32[]{:S(2)}) %collective-permute-start.1) | collective-permute-done | bytes 4194336 | tf_op jit(solution)/shard_map/ppermute | solution.py:19
  196.1 6.9 %multiply_select_fusion = f32[8,8,128,128]{3,2,1,0:T(8,128)} fusion(f32[8,8,128,128]{3,2,1,0:T(8,128)} %multiply_select_fusion.1, f32[8,8,128,128]{3,2,1,0:T(8,128)} %collective-permute-done.1, pred[]{:T(512)S(6)} %eq.10), kind=kLoop, calls=%fused_computation.15 | loop fusion | flops 5242880 | bytes 12582913 | tf_op jit(solution)/shard_map/jit(_where)/select_n | solution.py:53
  203.0 2.5 collective-permute-start.2
  205.5 179.4 %collective-permute-done.2 = f32[8,8,128,128]{3,2,1,0:T(8,128)} collective-permute-done((f32[8,8,128,128]{3,2,1,0:T(8,128)}, f32[8,8,128,128]{3,2,1,0:T(8,128)}, u32[]{:S(2)}, u32[]{:S(2)}) %collective-permute-start.2) | collective-permute-done | bytes 4194336 | tf_op jit(solution)/shard_map/ppermute | solution.py:19
  384.9 4.5 select_convert_fusion
  389.4 3.0 collective-permute-start.3
  392.5 10.2 %collective-permute-done.3 = bf16[2,8,128,128]{3,2,1,0:T(8,128)(2,1)S(1)} collective-permute-done((bf16[2,8,128,128]{3,2,1,0:T(8,128)(2,1)S(1)}, bf16[2,8,128,128]{3,2,1,0:T(8,128)(2,1)S(1)}, u32[]{:S(2)}, u32[]{:S(2)}) %collective-permute-start.3) | collective-permute-done | bytes 524320 | tf_op jit(solution)/shard_map/ppermute | solution.py:25
  402.7 0.1 pad_maximum_fusion.1
  402.8 1.3 collective-permute-start.4
  404.1 1.3 collective-permute-start.5
  405.4 0.0 collective-permute-done.4
  405.4 3.9 collective-permute-done.5
  409.4 2.1 fusion.13
  411.5 2.0 pad.5
  413.5 6.9 %reshape.19 = bf16[10,10,1,8,17,128]{5,4,3,1,0,2:T(8,128)(2,1)} reshape(bf16[10,10,1,136,128]{4,3,1,0,2:T(8,128)(2,1)} %pad.5) | data formatting | bytes 6963200 | tf_op jit(solution)/shard_map/conv_general_dilated | solution.py:62
  420.4 3.0 copy.29
  423.5 0.1 slice.15
  423.6 0.0 copy-done
  423.6 0.0 copy-done.3
  423.6 19.0 %select_reduce_fusion.1 = (f32[256]{0:T(256)S(1)}, f32[8,8,8,17,256]{4,2,3,1,0:T(8,128)}) fusion(pred[8,17]{0,1:T(8,128)(4,1)S(1)} %copy-done.3, bf16[3,3,3,128,256]{4,3,2,1,0:T(8,128)(2,1)S(1)} %copy-done, bf16[10,10,1,7,2,128]{5,3,4,1,0,2:T(8,128)(2,1)S(1)} %slice.15, bf16[10,10,1,8,17,128]{5,3,4,1,0,2:T(8,128)(2,1)S(1)} %copy.29), kind=kOutput, calls=%fused_computation.3 | convolution fusion | flops 15419842560 | bytes 14523528 | tf_op jit(solution)/shard_map/conv_general_dilated | solution.py:62
  442.7 0.1 reduce_sum.24
  442.8 0.1 reduce_sum.25
  442.9 46.1 %psum.14 = f32[32]{0:T(128)S(1)} all-reduce(f32[32]{0:T(128)S(1)} %reduce_sum.25), channel_id=1, replica_groups=mesh['tm'=8,'rows'=4] {'tm','rows'}, use_global_device_ids=true, to_apply=%region_2.3 | all-reduce | flops 32 | bytes 256 | tf_op jit(solution)/shard_map/psum | solution.py:84
  488.9 0.1 sub.31
  489.0 0.1 sub.32
  489.1 6.3 copy.30
  495.5 1.5 select_reduce_fusion
  497.0 4.1 slice.16
  501.1 0.1 reduce_sum.36
  501.2 0.1 reduce_sum.37
  501.3 0.0 copy-start.4
  501.3 0.0 copy-start.5
  501.3 11.5 %copy.31 = f32[8,8,1,128,256]{4,0,3,1,2:T(8,128)} copy(f32[8,8,1,128,256]{4,1,3,0,2:T(8,128)} %slice.16) | data formatting | bytes 16777216 | tf_op jit(solution)/shard_map/conv_general_dilated | solution.py:62
  512.8 41.6 %psum.15 = f32[32]{0:T(128)S(1)} all-reduce(f32[32]{0:T(128)S(1)} %reduce_sum.37), channel_id=1, replica_groups=mesh['tm'=8,'rows'=4] {'tm','rows'}, use_global_device_ids=true, to_apply=%region_5.6 | all-reduce | flops 32 | bytes 256 | tf_op jit(solution)/shard_map/psum | solution.py:87
  554.4 0.1 div.27
  554.4 0.1 div.28
  554.5 6.9 %fusion.5 = bf16[4,64,8,2,2,256]{5,1,4,3,0,2:T(8,128)(2,1)S(1)} fusion(f32[256]{0:T(256)S(1)} %copy-done.4, f32[256]{0:T(256)S(1)} %copy-done.5, f32[256]{0:T(256)S(1)} %div.28, f32[256]{0:T(256)S(1)} %sub.32, f32[8,4,2,64,2,256]{5,0,4,3,2,1:T(8,128)} %bitcast.27), kind=kLoop, calls=%fused_computation.17 | loop fusion | flops 18874368 | bytes 12587008 | tf_op jit(solution)/shard_map/transpose | solution.py:95
  561.4 6.4 copy.37
  567.8 7.7 %reshape.33 = bf16[4,64,8,1024]{3,2,0,1:T(8,128)(2,1)} reshape(bf16[4,64,8,2,2,256]{5,4,3,2,0,1:T(2,128)(2,1)} %copy.37) | data formatting | bytes 8388608 | tf_op jit(solution)/shard_map/reshape | solution.py:96
  575.5 96.8 %all_to_all.18 = bf16[4,64,8,1024]{3,2,0,1:T(8,128)(2,1)S(1)} all-to-all(bf16[4,64,8,1024]{3,2,0,1:T(8,128)(2,1)} %reshape.33), channel_id=1, replica_groups=mesh['tm'=8,'rows'=4] {'tm'}, dimensions={1} | all-to-all | bytes 8388608 | tf_op jit(solution)/shard_map/all_to_all | solution.py:97
  672.3 2.5 copy.52
  674.7 0.0 copy-done.1
  (9 shorter events, 0.1 us)
Async XLA Ops:
  0.0 423.6 %copy-start = (bf16[3,3,3,128,256]{4,3,2,1,0:T(8,128)(2,1)S(1)}, bf16[3,3,3,128,256]{4,3,2,1,0:T(8,128)(2,1)}, u32[]{:S(2)}) copy-start(bf16[3,3,3,128,256]{4,3,2,1,0:T(8,128)(2,1)} %param.5) | copy-start | bytes 5308420
  4.3 93.8 %collective-permute-start = (f32[8,8,128,128]{3,2,1,0:T(8,128)}, f32[8,8,128,128]{3,2,1,0:T(8,128)}, u32[]{:S(2)}, u32[]{:S(2)}) collective-permute-start(f32[8,8,128,128]{3,2,1,0:T(8,128)} %convert_element_type.12), channel_id=1, source_target_pairs={{0,4},{4,0},{8,12},{12,8},{16,20},{20,16},{24,28},{28,24},{1,5},{5... | collective-permute-start | bytes 12582920 | tf_op jit(solution)/shard_map/ppermute | solution.py:19
  104.0 92.1 %collective-permute-start.1 = (f32[8,8,128,128]{3,2,1,0:T(8,128)}, f32[8,8,128,128]{3,2,1,0:T(8,128)}, u32[]{:S(2)}, u32[]{:S(2)}) collective-permute-start(f32[8,8,128,128]{3,2,1,0:T(8,128)} %multiply_select_fusion.1), channel_id=1, source_target_pairs={{0,8},{8,0},{4,12},{12,4},{16,24},{24,16},{20,28},{28,20},{1,9},{9... | collective-permute-start | bytes 12582920 | tf_op jit(solution)/shard_map/ppermute | solution.py:19
  203.0 181.9 %collective-permute-start.2 = (f32[8,8,128,128]{3,2,1,0:T(8,128)}, f32[8,8,128,128]{3,2,1,0:T(8,128)}, u32[]{:S(2)}, u32[]{:S(2)}) collective-permute-start(f32[8,8,128,128]{3,2,1,0:T(8,128)} %multiply_select_fusion), channel_id=1, source_target_pairs={{0,16},{16,0},{4,20},{20,4},{8,24},{24,8},{12,28},{28,12},{1,17},{... | collective-permute-start | bytes 12582920 | tf_op jit(solution)/shard_map/ppermute | solution.py:19
  389.4 13.3 %collective-permute-start.3 = (bf16[2,8,128,128]{3,2,1,0:T(8,128)(2,1)S(1)}, bf16[2,8,128,128]{3,2,1,0:T(8,128)(2,1)S(1)}, u32[]{:S(2)}, u32[]{:S(2)}) collective-permute-start(bf16[2,8,128,128]{3,2,1,0:T(8,128)(2,1)S(1)} %slice.14), channel_id=1, source_target_pairs={{0,4},{4,8},{8,12},{12,16},{16,20},{20,24},{24,28},{1,5},{5,9},{9,... | collective-permute-start | bytes 1572872 | tf_op jit(solution)/shard_map/ppermute | solution.py:25
  402.8 2.6 collective-permute-start.4
  404.1 5.3 collective-permute-start.5
  420.4 3.2 copy-start.3
  489.1 6.4 copy-start.2
  501.3 53.3 %copy-start.4 = (f32[256]{0:T(256)S(1)}, f32[256]{0:T(256)}, u32[]{:S(2)}) copy-start(f32[256]{0:T(256)} %param.7) | copy-start | bytes 3076
  501.3 53.3 %copy-start.5 = (f32[256]{0:T(256)S(1)}, f32[256]{0:T(256)}, u32[]{:S(2)}) copy-start(f32[256]{0:T(256)} %param.6) | copy-start | bytes 3076
  672.3 2.5 copy-start.1
where the time goes:
time: 675 us
  waiting for transfers between devices  375 us (56%)
  blocking collectives  184 us (27%)
  local copies, waits for them, and re-layouts  51.1 us (8%)
  other arithmetic  32.4 us (5%)
  matrix products  19 us (3%)
  starting transfers between devices  12.9 us (2%)
    ppermute x3, waiting for transfers between devices, from_partner(): return lax.ppermute(block, axis, route)  361 us
    all_to_all x1, blocking collectives, per_device(): lax.all_to_all(arranged, 'tm', split_axis=1, concat_axis=2, tiled=True)  96.8 us
    psum x1, blocking collectives, per_device(): group_total = lax.psum(local_sums, ('tm', 'rows'))  46.1 us
    psum x1, blocking collectives, per_device(): lax.psum(jnp.sum(centered * centered, axis=(0, 1, 2, 4)), ('tm', 'rows'))  41.6 us
    conv_general_dilated x6, local copies, waits for them, and re-layouts, per_device(): lax.conv_general_dilated(padded[None], conv_weight, (1, 1, 1), 'VALID', d...  31.9 us
    conv_general_dilated x1, matrix products, per_device(): lax.conv_general_dilated(padded[None], conv_weight, (1, 1, 1), 'VALID', d...  19 us
    reshape x2, local copies, waits for them, and re-layouts, per_device(): arranged.reshape(out_height // 2, out_width // 2, out_frames, 4 * out_cha...  14.1 us
  transfers between devices with their start and end apart: 6, of which 5 were waited for; matrix products, arithmetic and copies ran while one was open for 0% of the time, Pallas kernels for 0%

commit v1 on v0

v1 whole, which is shorter than its diff:
```python
import functools

import jax
import jax.numpy as jnp
from jax import lax
from jax.experimental import pallas as pl
from jax.experimental.pallas import tpu as pltpu
from jax.sharding import PartitionSpec as P

GROUPS = 32
LEVELS = 3
TAPS = 3
inv_root = 0.7071067811865476
F32 = jnp.float32
BF16 = jnp.bfloat16
VMEM = pl.BlockSpec(memory_space=pltpu.VMEM)
SMEM = pl.BlockSpec(memory_space=pltpu.SMEM)
MIB = 1 << 20


def shape(dims, dtype):
    return jax.ShapeDtypeStruct(dims, dtype)


def on_core(body, outs, scalar, arrays, scratch=(), flops=0, limit=48):
    moved = sum(a.size * a.dtype.itemsize for a in arrays)
    moved += sum(o.size * jnp.dtype(o.dtype).itemsize for o in outs)
    return pl.pallas_call(
        body,
        out_shape=outs,
        in_specs=[SMEM] + [VMEM] * len(arrays),
        out_specs=[VMEM] * len(outs),
        scratch_shapes=list(scratch),
        compiler_params=pltpu.CompilerParams(vmem_limit_bytes=limit * MIB),
        cost_estimate=pl.CostEstimate(flops=flops, bytes_accessed=moved, transcendentals=0),
    )(scalar, *arrays)


def swap_bit(block, axis, bit):
    count = lax.axis_size(axis)
    return lax.ppermute(block, axis, [(i, i ^ (1 << bit)) for i in range(count)])


def bit_of(me, bit):
    return (me >> bit) & 1


class High:
    def __init__(self, count, width):
        self.bits = count.bit_length() - 1
        self.width = width
        self.order = list(range(self.bits))[::-1]
        self.columns = width // count

    def start(self, me, holder, bit, mine):
        top = self.bits if holder is None else holder
        low = max(bit, 0)
        at = sum(bit_of(me, m) * (self.width >> (self.bits - m)) for m in range(low + (0 if mine else 1), top))
        if not mine:
            at = at + (1 - bit_of(me, bit)) * (self.width >> (self.bits - bit))
        return at

    def length(self, bit):
        return (self.width >> (self.bits - bit)) + 2

    def view(self, ref, holder, source, at, size):
        return ref[pl.ds(at, size)] if holder is None else ref[source, pl.ds(at, size)]

    def sent_shape(self, bit):
        return (1 << (self.bits - 1 - bit), self.length(bit))

    def put(self, out, source, value):
        out[source] = value


class Low:
    def __init__(self, count, width):
        self.count = count
        self.bits = count.bit_length() - 1
        self.width = width
        self.order = list(range(self.bits))
        self.columns = width // count

    def start(self, me, holder, bit, mine):
        bottom = 0 if holder is None else holder + 1
        top = self.bits if mine else bit
        at = sum(bit_of(me, m) * (self.count >> (m + 1)) for m in range(bottom, top))
        if not mine:
            at = at + (1 - bit_of(me, bit)) * (self.count >> (bit + 1))
        return at

    def view(self, ref, holder, source, at, size):
        return ref[pl.ds(at, size)] if holder is None else ref[source, pl.ds(at, size)]

    def length(self, bit):
        return self.count >> (bit + 1)

    def sent_shape(self, bit):
        return (1 << bit, self.length(bit), self.columns + 2)

    def put(self, out, source, value):
        out[source] = value


def sources_of(plan, upto):
    held = [(None, 0, 0)]
    for bit in plan.order[:upto]:
        held += [(bit, i, mask ^ (1 << bit)) for i, (_, _, mask) in enumerate(list(held))]
    return held


def split_body(plan, me_ref, first, second, own, sent, *spare):
    me = me_ref[0]
    width = first.shape[2]
    rows = jnp.swapaxes(jnp.concatenate([first[:, 0], second[:, 0]], 0), 0, 1)
    edge = jnp.zeros((1,) + rows.shape[1:], BF16)
    wide = spare[0] if spare else own
    wide[0:1] = edge
    wide[1 : width + 1] = rows
    wide[width + 1 : width + 2] = edge
    bit = plan.order[0]
    if spare:
        for d in range(plan.count):
            place = sum(((d >> m) & 1) * (plan.count >> (m + 1)) for m in range(plan.bits))
            own[place] = wide[d * plan.columns : (d + 1) * plan.columns + 2]
    sent[0] = own[pl.ds(plan.start(me, None, bit, False), plan.length(bit))]


def split_rows(plan, me, video, pair):
    frames, _, width, channels = video.shape
    low = isinstance(plan, Low)
    bit = plan.order[0]
    own = (plan.count, plan.columns + 2) if low else (width + 2,)
    tail = (2 * frames, channels)
    return pl.pallas_call(
        functools.partial(split_body, plan),
        grid=(1,),
        out_shape=[shape(own + tail, BF16), shape(plan.sent_shape(bit) + tail, BF16)],
        in_specs=[
            SMEM,
            pl.BlockSpec((frames, 1, width, channels), lambda g, h=pair[0]: (0, h, 0, 0)),
            pl.BlockSpec((frames, 1, width, channels), lambda g, h=pair[1]: (0, h, 0, 0)),
        ],
        out_specs=[VMEM, VMEM],
        scratch_shapes=[pltpu.VMEM((width + 2,) + tail, BF16)] if low else [],
        compiler_params=pltpu.CompilerParams(vmem_limit_bytes=24 * MIB),
    )(me, video, video)


def part_body(plan, step, me_ref, *refs):
    me = me_ref[0]
    out = refs[-1]
    holders = dict(zip([None] + plan.order[:step], refs))
    bit = plan.order[step]
    for place, (holder, source, _) in enumerate(sources_of(plan, step)):
        at = plan.start(me, holder, bit, False)
        plan.put(out, place, plan.view(holders[holder], holder, source, at, plan.length(bit)))


def transpose_blocks(plan, me, own, sent):
    got = []
    tail = own.shape[-2:]
    for step, bit in enumerate(plan.order):
        if step:
            outs = [shape(plan.sent_shape(bit) + tail, BF16)]
            (sent,) = on_core(functools.partial(part_body, plan, step), outs, me, [own] + got, limit=24)
        got.append(swap_bit(sent, "tm", bit))
    return [own] + got


def gather(plan, me, refs, blocks):
    holders = dict(zip([None] + plan.order, refs))
    size = plan.columns + 2
    for holder, source, mask in sources_of(plan, plan.bits):
        ref = holders[holder]
        at = plan.start(me, holder, -1, True)
        if isinstance(plan, High):
            value = plan.view(ref, holder, source, at, size)
        else:
            value = ref[at] if holder is None else ref[source, at]
        blocks[me ^ mask] = value


def widen(wide, row, column, cells):
    channels = cells.shape[1]
    frame = lax.broadcasted_iota(jnp.int32, cells.shape, 0)
    for tap in range(TAPS):
        back = TAPS - 1 - tap
        moved = cells
        if back:
            moved = jnp.where(frame < back, 0.0, pltpu.roll(cells, back, 0))
        wide[row, column, :, tap * channels : (tap + 1) * channels] = moved.astype(BF16)


def wavelet_rows(blocks, wide, plain=None):
    count, columns, both, _ = blocks.shape
    frames = both // 2

    def column(i, _):
        values = [blocks[b, i].astype(F32) for b in range(count)]
        for level in range(LEVELS):
            span = 1 << level
            later = list(values)
            for b in range(count):
                if not b & span:
                    later[b] = (values[b] + values[b + span]) * inv_root
                    later[b + span] = (values[b] - values[b + span]) * inv_root
            values = later
        for row in range(2):
            cells = jnp.concatenate([v[row * frames : (row + 1) * frames] for v in values], 0)
            widen(wide, row, i, cells)
            if plain is not None:
                plain[row, i] = cells.astype(BF16)
        return 0

    lax.fori_loop(0, columns, column, 0)


def outer_body(plan, me_ref, *refs):
    *held, wide, plain, blocks = refs
    gather(plan, me_ref[0], held, blocks)
    wavelet_rows(blocks, wide, plain)


def taps(w_ref, terms, before=None):
    columns = terms[0][0].shape[1] - 2
    left, right = [], []
    for wide, row, i in terms:
        for j in range(TAPS):
            cells = wide[row, pl.ds(j, columns)]
            left.append(cells.reshape(-1, cells.shape[-1]))
            right += [w_ref[k, i, j] for k in range(TAPS)]
    total = jnp.dot(
        jnp.concatenate(left, -1), jnp.concatenate(right, 0), preferred_element_type=F32
    )
    if before is not None:
        total = total + before
    return total


def row_sums(total):
    mean = jnp.sum(total, 0, keepdims=True) * (1.0 / total.shape[0])
    apart = total - mean
    return mean, jnp.sum(apart * apart, 0, keepdims=True)


def finish(total, out, sums, row):
    out[row] = total.reshape(out.shape[1:])
    mean, squares = row_sums(total)
    sums[row, 0:1] = mean
    sums[row, 1:2] = squares


def keep(total, out, row):
    out[row] = total.reshape(out.shape[1:])


def flat(ref, row):
    return ref[row].reshape(-1, ref.shape[-1])


def stage_a(plan, me_ref, w_ref, outer, above, below, *refs):
    *held, done, part1, part2, sums, wide, halo, blocks = refs
    gather(plan, me_ref[0], held, blocks)
    wavelet_rows(blocks, wide)

    def column(i, _):
        widen(halo, 0, i, above[i].astype(F32))
        widen(halo, 1, i, below[i].astype(F32))
        return 0

    lax.fori_loop(0, above.shape[0], column, 0)
    finish(taps(w_ref, [(halo, 0, 0), (outer, 0, 1), (wide, 0, 2)]), done, sums, 0)
    finish(taps(w_ref, [(wide, 1, 0), (outer, 1, 1), (halo, 1, 2)]), done, sums, 1)
    keep(taps(w_ref, [(outer, 0, 0), (wide, 0, 1)]), part1, 0)
    keep(taps(w_ref, [(wide, 1, 1), (outer, 1, 2)]), part1, 1)
    keep(taps(w_ref, [(wide, 0, 0)]), part2, 0)
    keep(taps(w_ref, [(wide, 1, 2)]), part2, 1)


def stage_b(plan, me_ref, w_ref, part1, part2, *refs):
    *held, done, next2, part3, sums, wide, blocks = refs
    gather(plan, me_ref[0], held, blocks)
    wavelet_rows(blocks, wide)
    finish(taps(w_ref, [(wide, 0, 2)], flat(part1, 0)), done, sums, 0)
    finish(taps(w_ref, [(wide, 1, 0)], flat(part1, 1)), done, sums, 1)
    keep(taps(w_ref, [(wide, 0, 1)], flat(part2, 0)), next2, 0)
    keep(taps(w_ref, [(wide, 1, 1)], flat(part2, 1)), next2, 1)
    keep(taps(w_ref, [(wide, 0, 0)]), part3, 0)
    keep(taps(w_ref, [(wide, 1, 2)]), part3, 1)


def stage_c(plan, me_ref, w_ref, part2, part3, sums_a, sums_b, *refs):
    *held, done2, done3, message, sums, wide, blocks = refs
    gather(plan, me_ref[0], held, blocks)
    wavelet_rows(blocks, wide)
    finish(taps(w_ref, [(wide, 0, 2)], flat(part2, 0)), done2, sums, 0)
    finish(taps(w_ref, [(wide, 1, 0)], flat(part2, 1)), done2, sums, 1)
    finish(taps(w_ref, [(wide, 0, 1), (wide, 1, 2)], flat(part3, 0)), done3, sums.at[2:4], 0)
    finish(taps(w_ref, [(wide, 0, 0), (wide, 1, 1)], flat(part3, 1)), done3, sums.at[2:4], 1)
    rows = [sums[r] for r in range(4)]
    rows += [s[r] for s in (sums_a, sums_b) for r in range(2)]
    entries = wide.shape[2] * (wide.shape[1] - 2)
    mean = sum(r[0:1] for r in rows) * (1.0 / len(rows))
    squares = sum(r[1:2] + entries * (r[0:1] - mean) * (r[0:1] - mean) for r in rows)
    lanes = message.shape[-1]
    parts = [v[:, c : c + lanes] for v in (mean, squares) for c in range(0, mean.shape[1], lanes)]
    packed = jnp.concatenate(parts + [jnp.zeros((8 - len(parts), lanes), F32)], 0)
    message[...] = jnp.broadcast_to(packed[None], message.shape)


def over_group(values, size):
    lanes = values.shape[-1]
    lane = lax.broadcasted_iota(jnp.int32, values.shape, values.ndim - 1)
    step = 1
    while step < size:
        axis = values.ndim - 1
        down = pltpu.roll(values, step, axis)
        up = pltpu.roll(values, lanes - step, axis)
        values = values + jnp.where((lane & step) != 0, down, up)
        step *= 2
    return values


def norm_body(entries, size, all_ref, gain_ref, bias_ref, *refs):
    *rows, out, affine = refs

    @pl.when(pl.program_id(0) == 0)
    def _():
        devices = all_ref.shape[0]
        half = gain_ref.shape[0]
        means = all_ref[:, 0:half]
        mean = jnp.sum(means, 0) * (1.0 / devices)
        apart = means - mean[None]
        squares = jnp.sum(all_ref[:, half : 2 * half] + entries * apart * apart, 0)
        group_mean = over_group(mean, size) * (1.0 / size)
        apart = mean - group_mean
        group = over_group(squares + (entries * devices) * apart * apart, size)
        variance = group * (1.0 / (entries * devices * size))
        scale = (0.5 * gain_ref[...]) / jnp.sqrt(variance + 1e-05)
        for p in range(half):
            lanes = slice(p * scale.shape[1], (p + 1) * scale.shape[1])
            affine[0:1, lanes] = group_mean[p : p + 1]
            affine[1:2, lanes] = scale[p : p + 1]
            affine[2:3, lanes] = 0.5 * bias_ref[p : p + 1]

    mean, scale, bias = affine[0:1], affine[1:2], affine[2:3]
    channels = mean.shape[1]
    height = 2 * len(rows)
    for h in range(height):
        ref, place = (rows[h], 0) if h < len(rows) else (rows[height - 1 - h], 1)
        for w in range(ref.shape[1]):
            half_v = (ref[place, w] - mean) * scale + bias
            value = half_v + half_v * jnp.tanh(half_v)
            lanes = (h % 2 * 2 + w % 2) * channels
            out[h // 2, w // 2, :, lanes : lanes + channels] = value.astype(BF16)


def per_device(video, conv_weight, norm_gain, norm_bias):
    frames, height, width, channels = video.shape
    outputs = conv_weight.shape[-1]
    count = lax.axis_size("tm")
    strips = lax.axis_size("rows")
    devices = count * strips
    columns = width // count
    time = frames * count
    me = lax.axis_index("tm").astype(jnp.int32).reshape(1)
    high, low = High(count, width), Low(count, width)

    def gathered(plan, pair):
        return transpose_blocks(plan, me, *split_rows(plan, me, video, pair))

    held0 = gathered(high, (0, 7))
    held1 = gathered(high, (1, 6))
    held2 = gathered(low, (2, 5))
    held3 = gathered(low, (3, 4))

    blocks = pltpu.VMEM((count, columns + 2, 2 * frames, channels), BF16)
    wide = (2, columns + 2, time, TAPS * channels)
    wide_spare = pltpu.VMEM(wide, BF16)
    row_pair = shape((2, columns, time, outputs), F32)
    pair_sums = shape((2, 2, outputs), F32)
    tap_flops = 2 * columns * time * TAPS * TAPS * channels * outputs

    outer, plain = on_core(
        functools.partial(outer_body, high),
        [shape(wide, BF16), shape((2, columns + 2, time, channels), BF16)],
        me,
        held0,
        [blocks],
    )
    down = [(i, i + 1) for i in range(strips - 1)]
    up = [(i + 1, i) for i in range(strips - 1)]
    above = lax.ppermute(plain[1], "rows", down)
    below = lax.ppermute(plain[0], "rows", up)
    done0, part1, part2, sums_a = on_core(
        functools.partial(stage_a, high),
        [row_pair, row_pair, row_pair, pair_sums],
        me,
        [conv_weight, outer, above, below] + held1,
        [wide_spare, wide_spare, blocks],
        flops=12 * tap_flops,
    )
    done1, part2, part3, sums_b = on_core(
        functools.partial(stage_b, low),
        [row_pair, row_pair, row_pair, pair_sums],
        me,
        [conv_weight, part1, part2] + held2,
        [wide_spare, blocks],
        flops=6 * tap_flops,
    )
    done2, done3, message = on_core(
        functools.partial(stage_c, low),
        [row_pair, row_pair, shape((devices, 8, 128), F32)],
        me,
        [conv_weight, part2, part3, sums_a, sums_b] + held3,
        [pltpu.VMEM((4, 2, outputs), F32), wide_spare, blocks],
        flops=6 * tap_flops,
    )
    messages = lax.all_to_all(message, ("tm", "rows"), 0, 0, tiled=True)

    steps = columns // 2 // min(2, columns // 2)
    block = columns // steps
    rows_spec = pl.BlockSpec((2, block, time, outputs), lambda g: (0, g, 0, 0))
    return pl.pallas_call(
        functools.partial(norm_body, float(height * columns * time), outputs // GROUPS),
        grid=(steps,),
        out_shape=shape((height // 2, columns // 2, time, 4 * outputs), BF16),
        in_specs=[VMEM, VMEM, VMEM] + [rows_spec] * 4,
        out_specs=pl.BlockSpec((height // 2, block // 2, time, 4 * outputs), lambda g: (0, g, 0, 0)),
        scratch_shapes=[pltpu.VMEM((8, outputs), F32)],
        compiler_params=pltpu.CompilerParams(vmem_limit_bytes=40 * MIB),
    )(messages, norm_gain.reshape(-1, 128), norm_bias.reshape(-1, 128), done0, done1, done2, done3)


def solution(mesh):
    placed = (P("tm", "rows", None, None), P(), P(), P())
    return jax.shard_map(
        per_device,
        mesh=mesh,
        in_specs=placed,
        out_specs=P("rows", "tm", None, None),
        check_vma=False,
    )
```

time: 675 us -> 110 us (0.16)
  waiting for transfers between devices: 375 us -> 37.3 us
  blocking collectives: 184 us -> 13.1 us
  local copies, waits for them, and re-layouts: 51.1 us -> 3.24 us
  Pallas kernels: 0 us -> 34.5 us
  other arithmetic: 32.4 us -> 0 us
  matrix products: 19 us -> 0 us
  starting transfers between devices: 12.9 us -> 22.1 us
    ppermute x6 -> x14, waiting for transfers between devices: 375 us -> 37.3 us  [the longest x12 37.3 us: swap_bit(): return lax.ppermute(block, axis, [(i, i ^ 1 << bit) for i in range(count)])]
    psum x2 -> x0, blocking collectives: 87.6 us -> none  [the longest x1 46.1 us: per_device(): group_total = lax.psum(local_sums, ('tm', 'rows'))]
    all_to_all x1, blocking collectives: 96.8 us -> 13.1 us  [per_device(): messages = lax.all_to_all(message, ('tm', 'rows'), 0, 0, tiled=True)]
    pallas_call x0 -> x17, Pallas kernels: none -> 34.5 us  [the longest x12 28.9 us: on_core(): pl.pallas_call(body, out_shape=outs, in_specs=[SMEM] + [VMEM] * len(array...]
    conv_general_dilated x6 -> x0, local copies, waits for them, and re-layouts: 31.9 us -> none  [per_device(): lax.conv_general_dilated(padded[None], conv_weight, (1, 1, 1), 'VALID', d...]
    conv_general_dilated x1 -> x0, matrix products: 19 us -> none  [per_device(): lax.conv_general_dilated(padded[None], conv_weight, (1, 1, 1), 'VALID', d...]
    reshape x2 -> x0, local copies, waits for them, and re-layouts: 14.1 us -> none  [per_device(): arranged.reshape(out_height // 2, out_width // 2, out_frames, 4 * out_cha...]
    select_n x2 -> x0, other arithmetic: 12.8 us -> none  [per_device(): jnp.where(is_upper, (partner - current) * inv_root, (current + partner) *...]
  transfers between devices with their start and end apart: 6 -> 14, of which waited for: 5 -> 8; matrix products, arithmetic and copies ran while one was open for 0% -> 0% of each run, Pallas kernels for 0% -> 19%
where the time goes in v1:
time: 110 us
  waiting for transfers between devices  37.3 us (34%)
  Pallas kernels  34.5 us (31%)
  starting transfers between devices  22.1 us (20%)
  blocking collectives  13.1 us (12%)
  local copies, waits for them, and re-layouts  3.24 us (3%)
    ppermute x12, waiting for transfers between devices, swap_bit(): return lax.ppermute(block, axis, [(i, i ^ 1 << bit) for i in range(count)])  37.3 us
    pallas_call x12, Pallas kernels, on_core(): pl.pallas_call(body, out_shape=outs, in_specs=[SMEM] + [VMEM] * len(array...  28.9 us
    ppermute x12, starting transfers between devices, swap_bit(): return lax.ppermute(block, axis, [(i, i ^ 1 << bit) for i in range(count)])  19.2 us
    all_to_all x1, blocking collectives, per_device(): messages = lax.all_to_all(message, ('tm', 'rows'), 0, 0, tiled=True)  13.1 us
    pallas_call x1, Pallas kernels, per_device(): pl.pallas_call(functools.partial(norm_body, float(height * columns * time...  4.24 us
    unnamed x14, local copies, waits for them, and re-layouts  3.2 us
  transfers between devices with their start and end apart: 14, of which 8 were waited for; matrix products, arithmetic and copies ran while one was open for 0% of the time, Pallas kernels for 19%

profile of v1, /device:TPU:0, one launch (start us, length us, event | category | flops | bytes accessed | tf_op | source)
XLA Modules:
  0.0 110.2 jit_solution(10174185270187348510)
XLA Ops:
  0.0 1.6 %copy-done = bf16[8,8,128,128]{3,2,1,0:T(8,128)(2,1)S(1)} copy-done((bf16[8,8,128,128]{3,2,1,0:T(8,128)(2,1)S(1)}, bf16[8,8,128,128]{3,2,1,0:T(8,128)(2,1)}, u32[]{:S(2)}) %copy-start) | copy-done | bytes 2097176
  1.6 0.3 shard_map.46
  1.9 4.1 %collective-permute-start = (bf16[1,66,16,128]{3,2,1,0:T(8,128)(2,1)S(1)}, bf16[1,66,16,128]{3,2,1,0:T(8,128)(2,1)S(1)}, u32[]{:S(2)}, u32[]{:S(2)}) collective-permute-start(bf16[1,66,16,128]{3,2,1,0:T(8,128)(2,1)S(1)} %get-tuple-element.27), channel_id=1, source_target_pairs={{0,16},{4,20},{8,24},{12,28},{16,0},{20,4},{24,8},{28,12},{1,17},{... | collective-permute-start | bytes 811016 | tf_op jit(solution)/shard_map/ppermute | solution.py:41
  6.0 12.3 %collective-permute-done.refs_1_ = bf16[1,66,16,128]{3,2,1,0:T(8,128)(2,1)S(1)} collective-permute-done((bf16[1,66,16,128]{3,2,1,0:T(8,128)(2,1)S(1)}, bf16[1,66,16,128]{3,2,1,0:T(8,128)(2,1)S(1)}, u32[]{:S(2)}, u32[]{:S(2)}) %collective-permute-start) | collective-permute-done | bytes 270368 | tf_op jit(solution)/shard_map/ppermute | solution.py:41
  18.3 0.8 collective-permute-start.1
  19.0 0.0 copy-done.1
  19.0 0.3 shard_map.50
  19.3 3.4 %collective-permute-start.5 = (bf16[1,66,16,128]{3,2,1,0:T(8,128)(2,1)S(1)}, bf16[1,66,16,128]{3,2,1,0:T(8,128)(2,1)S(1)}, u32[]{:S(2)}, u32[]{:S(2)}) collective-permute-start(bf16[1,66,16,128]{3,2,1,0:T(8,128)(2,1)S(1)} %get-tuple-element.31), channel_id=1, source_target_pairs={{0,16},{4,20},{8,24},{12,28},{16,0},{20,4},{24,8},{28,12},{1,17},{... | collective-permute-start | bytes 811016 | tf_op jit(solution)/shard_map/ppermute | solution.py:41
  22.8 0.4 shard_map.54
  23.2 1.6 %collective-permute-start.8 = (bf16[1,4,18,16,128]{4,3,2,1,0:T(8,128)(2,1)S(1)}, bf16[1,4,18,16,128]{4,3,2,1,0:T(8,128)(2,1)S(1)}, u32[]{:S(2)}, u32[]{:S(2)}) collective-permute-start(bf16[1,4,18,16,128]{4,3,2,1,0:T(8,128)(2,1)S(1)} %get-tuple-element.35), channel_id=1, source_target_pairs={{0,4},{4,0},{8,12},{12,8},{16,20},{20,16},{24,28},{28,24},{1,5},{5... | collective-permute-start | bytes 884744 | tf_op jit(solution)/shard_map/ppermute | solution.py:41
  24.7 0.4 shard_map.58
  25.1 0.6 collective-permute-start.11
  25.7 5.9 %collective-permute-done.1.refs_2_ = bf16[2,34,16,128]{3,2,1,0:T(8,128)(2,1)S(1)} collective-permute-done((bf16[2,34,16,128]{3,2,1,0:T(8,128)(2,1)S(1)}, bf16[2,34,16,128]{3,2,1,0:T(8,128)(2,1)S(1)}, u32[]{:S(2)}, u32[]{:S(2)}) %collective-permute-start.1) | collective-permute-done | bytes 278560 | tf_op jit(solution)/shard_map/ppermute | solution.py:41
  31.6 1.3 %collective-permute-start.2 = (bf16[4,18,16,128]{3,2,1,0:T(8,128)(2,1)S(1)}, bf16[4,18,16,128]{3,2,1,0:T(8,128)(2,1)S(1)}, u32[]{:S(2)}, u32[]{:S(2)}) collective-permute-start(bf16[4,18,16,128]{3,2,1,0:T(8,128)(2,1)S(1)} %shard_map.48), channel_id=1, source_target_pairs={{0,4},{4,0},{8,12},{12,8},{16,20},{20,16},{24,28},{28,24},{1,5},{5... | collective-permute-start | bytes 884744 | tf_op jit(solution)/shard_map/ppermute | solution.py:41
  32.9 2.1 %collective-permute-done.5.refs_1_ = bf16[1,66,16,128]{3,2,1,0:T(8,128)(2,1)S(1)} collective-permute-done((bf16[1,66,16,128]{3,2,1,0:T(8,128)(2,1)S(1)}, bf16[1,66,16,128]{3,2,1,0:T(8,128)(2,1)S(1)}, u32[]{:S(2)}, u32[]{:S(2)}) %collective-permute-start.5) | collective-permute-done | bytes 270368 | tf_op jit(solution)/shard_map/ppermute | solution.py:41
  35.0 0.2 collective-permute-start.6
  35.2 0.0 collective-permute-done.8.refs_1_
  35.3 1.9 %collective-permute-start.9 = (bf16[2,2,18,16,128]{4,3,2,1,0:T(8,128)(2,1)S(1)}, bf16[2,2,18,16,128]{4,3,2,1,0:T(8,128)(2,1)S(1)}, u32[]{:S(2)}, u32[]{:S(2)}) collective-permute-start(bf16[2,2,18,16,128]{4,3,2,1,0:T(8,128)(2,1)S(1)} %shard_map.55), channel_id=1, source_target_pairs={{0,8},{4,12},{8,0},{12,4},{16,24},{20,28},{24,16},{28,20},{1,9},{5... | collective-permute-start | bytes 884744 | tf_op jit(solution)/shard_map/ppermute | solution.py:41
  37.2 2.3 %collective-permute-done.11.refs_1_ = bf16[1,4,18,16,128]{4,3,2,1,0:T(8,128)(2,1)S(1)} collective-permute-done((bf16[1,4,18,16,128]{4,3,2,1,0:T(8,128)(2,1)S(1)}, bf16[1,4,18,16,128]{4,3,2,1,0:T(8,128)(2,1)S(1)}, u32[]{:S(2)}, u32[]{:S(2)}) %collective-permute-start.11) | collective-permute-done | bytes 294944 | tf_op jit(solution)/shard_map/ppermute | solution.py:41
  39.5 0.1 collective-permute-start.12
  39.6 5.1 %collective-permute-done.6.refs_2_ = bf16[2,34,16,128]{3,2,1,0:T(8,128)(2,1)S(1)} collective-permute-done((bf16[2,34,16,128]{3,2,1,0:T(8,128)(2,1)S(1)}, bf16[2,34,16,128]{3,2,1,0:T(8,128)(2,1)S(1)}, u32[]{:S(2)}, u32[]{:S(2)}) %collective-permute-start.6) | collective-permute-done | bytes 278560 | tf_op jit(solution)/shard_map/ppermute | solution.py:41
  44.7 1.6 %collective-permute-start.7 = (bf16[4,18,16,128]{3,2,1,0:T(8,128)(2,1)S(1)}, bf16[4,18,16,128]{3,2,1,0:T(8,128)(2,1)S(1)}, u32[]{:S(2)}, u32[]{:S(2)}) collective-permute-start(bf16[4,18,16,128]{3,2,1,0:T(8,128)(2,1)S(1)} %shard_map.52), channel_id=1, source_target_pairs={{0,4},{4,0},{8,12},{12,8},{16,20},{20,16},{24,28},{28,24},{1,5},{5... | collective-permute-start | bytes 884744 | tf_op jit(solution)/shard_map/ppermute | solution.py:41
  46.2 0.0 collective-permute-done.2.refs_3_
  46.2 0.7 shard_map.49
  47.0 0.0 copy-start.6
  47.1 1.4 %collective-permute-start.3 = (bf16[18,64,128]{2,1,0:T(8,128)(2,1)S(1)}, bf16[18,64,128]{2,1,0:T(8,128)(2,1)S(1)}, u32[]{:S(2)}, u32[]{:S(2)}) collective-permute-start(bf16[18,64,128]{2,1,0:T(8,128)(2,1)S(1)} %get-tuple-element.48), channel_id=1, source_target_pairs={{0,1},{1,2},{2,3},{4,5},{5,6},{6,7},{8,9},{9,10},{10,11},{12,13},{... | collective-permute-start | bytes 884744 | tf_op jit(solution)/shard_map/ppermute | solution.py:394
  48.5 1.5 %collective-permute-start.4 = (bf16[18,64,128]{2,1,0:T(8,128)(2,1)S(1)}, bf16[18,64,128]{2,1,0:T(8,128)(2,1)S(1)}, u32[]{:S(2)}, u32[]{:S(2)}) collective-permute-start(bf16[18,64,128]{2,1,0:T(8,128)(2,1)S(1)} %get-tuple-element.47), channel_id=1, source_target_pairs={{1,0},{2,1},{3,2},{5,4},{6,5},{7,6},{9,8},{10,9},{11,10},{13,12},{... | collective-permute-start | bytes 884744 | tf_op jit(solution)/shard_map/ppermute | solution.py:395
  50.0 1.0 collective-permute-done.9.refs_2_
  51.0 1.0 collective-permute-start.10
  52.0 2.1 %collective-permute-done.12.refs_2_ = bf16[2,2,18,16,128]{4,3,2,1,0:T(8,128)(2,1)S(1)} collective-permute-done((bf16[2,2,18,16,128]{4,3,2,1,0:T(8,128)(2,1)S(1)}, bf16[2,2,18,16,128]{4,3,2,1,0:T(8,128)(2,1)S(1)}, u32[]{:S(2)}, u32[]{:S(2)}) %collective-permute-start.12) | collective-permute-done | bytes 294944 | tf_op jit(solution)/shard_map/ppermute | solution.py:41
  54.2 2.6 %collective-permute-start.13 = (bf16[4,1,18,16,128]{4,3,2,1,0:T(8,128)(2,1)S(1)}, bf16[4,1,18,16,128]{4,3,2,1,0:T(8,128)(2,1)S(1)}, u32[]{:S(2)}, u32[]{:S(2)}) collective-permute-start(bf16[4,1,18,16,128]{4,3,2,1,0:T(8,128)(2,1)S(1)} %shard_map.60), channel_id=1, source_target_pairs={{0,16},{4,20},{8,24},{12,28},{16,0},{20,4},{24,8},{28,12},{1,17},{... | collective-permute-start | bytes 884744 | tf_op jit(solution)/shard_map/ppermute | solution.py:41
  56.7 0.0 collective-permute-done.7.refs_3_
  56.7 0.0 collective-permute-done.3.above
  56.7 0.0 collective-permute-done.4.below
  56.8 0.0 copy-done.6
  56.8 10.6 %shard_map.53 = (f32[2,16,64,256]{3,2,1,0:T(8,128)}, f32[2,16,64,256]{3,2,1,0:T(8,128)}, f32[2,16,64,256]{3,2,1,0:T(8,128)}, f32[2,2,256]{2,1,0:T(2,128)S(1)}) custom-call(s32[1]{0:T(128)} %bitcast.me_ref, bf16[3,3,3,128,256]{4,3,2,1,0:T(8,128)(2,1)S(1)} %copy-done.6, bf16[2,18,64,384]{3,2,1,0:T(8,128)(2,1)S(1)} %get-tuple-element.28.outer, ...), custom_call_target="tpu_custom_call" | custom-call | flops 7247757312 | bytes 11800576 | tf_op jit(solution)/shard_map/pallas_call | solution.py:28
  67.3 6.5 %collective-permute-done.10.refs_3_ = bf16[4,1,18,16,128]{4,3,2,1,0:T(8,128)(2,1)S(1)} collective-permute-done((bf16[4,1,18,16,128]{4,3,2,1,0:T(8,128)(2,1)S(1)}, bf16[4,1,18,16,128]{4,3,2,1,0:T(8,128)(2,1)S(1)}, u32[]{:S(2)}, u32[]{:S(2)}) %collective-permute-start.10) | collective-permute-done | bytes 294944 | tf_op jit(solution)/shard_map/ppermute | solution.py:41
  73.9 8.8 %shard_map.57 = (f32[2,16,64,256]{3,2,1,0:T(8,128)S(1)}, f32[2,16,64,256]{3,2,1,0:T(8,128)}, f32[2,16,64,256]{3,2,1,0:T(8,128)}, f32[2,2,256]{2,1,0:T(2,128)S(1)}) custom-call(s32[1]{0:T(128)} %bitcast.me_ref, bf16[3,3,3,128,256]{4,3,2,1,0:T(8,128)(2,1)S(1)} %copy-done.6, f32[2,16,64,256]{3,2,1,0:T(8,128)} %get-tuple-element.32.part1, ...), custom_call_target="tpu_custom_call" | custom-call | flops 3623878656 | bytes 13733888 | tf_op jit(solution)/shard_map/pallas_call | solution.py:28
  82.6 0.0 collective-permute-done.13.refs_3_
  82.7 0.0 copy-start.5
  82.7 8.7 %shard_map.61 = (f32[2,16,64,256]{3,2,1,0:T(8,128)S(1)}, f32[2,16,64,256]{3,2,1,0:T(8,128)}, f32[32,8,128]{2,1,0:T(8,128)S(1)}) custom-call(s32[1]{0:T(128)} %bitcast.me_ref, bf16[3,3,3,128,256]{4,3,2,1,0:T(8,128)(2,1)S(1)} %copy-done.6, f32[2,16,64,256]{3,2,1,0:T(8,128)} %get-tuple-element.36.part2, f32[2,16,64,256]{3,2,1,0:T(8,128)} %get-tuple-element.37.part3, ...), custom_call_target="tpu_custom_call" | custom-call | flops 3623878656 | bytes 11771904 | tf_op jit(solution)/shard_map/pallas_call | solution.py:28
  91.3 13.1 %all_to_all.5.all_ref = f32[32,8,128]{2,1,0:T(8,128)S(1)} all-to-all(f32[32,8,128]{2,1,0:T(8,128)S(1)} %get-tuple-element.42), channel_id=1, replica_groups=mesh['tm'=8,'rows'=4] {'tm','rows'}, dimensions={0} | all-to-all | bytes 262144 | tf_op jit(solution)/shard_map/all_to_all | solution.py:420
  104.4 0.0 copy-done.2
  104.4 0.0 copy-done.4
  104.4 0.0 copy-done.5
  104.4 0.0 copy-start.3
  104.4 1.6 %copy-done.3 = f32[2,16,64,256]{3,2,1,0:T(8,128)S(1)} copy-done((f32[2,16,64,256]{3,2,1,0:T(8,128)S(1)}, f32[2,16,64,256]{3,2,1,0:T(8,128)}, u32[]{:S(2)}) %copy-start.3) | copy-done | bytes 2097176
  106.0 4.2 %shard_map.62 = bf16[4,8,64,1024]{3,2,1,0:T(8,128)(2,1)} custom-call(f32[32,8,128]{2,1,0:T(8,128)S(1)} %all_to_all.5.all_ref, f32[2,128]{1,0:T(2,128)S(1)} %bitcast.7, f32[2,128]{1,0:T(2,128)S(1)} %bitcast.8, f32[2,16,64,256]{3,2,1,0:T(8,128)S(1)} %copy-done.2, f32[2,16,64,256]{3,2,1,0:T(8,128)S(1)} %get-tuple-element.44.refs_1_, ...), custom_call_target="tpu_custom_call" | custom-call | tf_op jit(solution)/shard_map/pallas_call | solution.py:425
  (13 shorter events, 0.2 us)
Async XLA Ops:
  0.0 1.6 %copy-start = (bf16[8,8,128,128]{3,2,1,0:T(8,128)(2,1)S(1)}, bf16[8,8,128,128]{3,2,1,0:T(8,128)(2,1)}, u32[]{:S(2)}) copy-start(bf16[8,8,128,128]{3,2,1,0:T(8,128)(2,1)} %second.7) | copy-start | bytes 6291460
  1.6 17.5 %copy-start.1 = (bf16[8,8,128,128]{3,2,1,0:T(8,128)(2,1)S(1)}, bf16[8,8,128,128]{3,2,1,0:T(8,128)(2,1)}, u32[]{:S(2)}) copy-start(bf16[8,8,128,128]{3,2,1,0:T(8,128)(2,1)} %second.7) | copy-start | bytes 6291460
  1.9 16.4 %collective-permute-start = (bf16[1,66,16,128]{3,2,1,0:T(8,128)(2,1)S(1)}, bf16[1,66,16,128]{3,2,1,0:T(8,128)(2,1)S(1)}, u32[]{:S(2)}, u32[]{:S(2)}) collective-permute-start(bf16[1,66,16,128]{3,2,1,0:T(8,128)(2,1)S(1)} %get-tuple-element.27), channel_id=1, source_target_pairs={{0,16},{4,20},{8,24},{12,28},{16,0},{20,4},{24,8},{28,12},{1,17},{... | collective-permute-start | bytes 811016 | tf_op jit(solution)/shard_map/ppermute | solution.py:41
  18.3 13.3 %collective-permute-start.1 = (bf16[2,34,16,128]{3,2,1,0:T(8,128)(2,1)S(1)}, bf16[2,34,16,128]{3,2,1,0:T(8,128)(2,1)S(1)}, u32[]{:S(2)}, u32[]{:S(2)}) collective-permute-start(bf16[2,34,16,128]{3,2,1,0:T(8,128)(2,1)S(1)} %shard_map.47), channel_id=1, source_target_pairs={{0,8},{4,12},{8,0},{12,4},{16,24},{20,28},{24,16},{28,20},{1,9},{5... | collective-permute-start | bytes 835592 | tf_op jit(solution)/shard_map/ppermute | solution.py:41
  19.3 15.7 %collective-permute-start.5 = (bf16[1,66,16,128]{3,2,1,0:T(8,128)(2,1)S(1)}, bf16[1,66,16,128]{3,2,1,0:T(8,128)(2,1)S(1)}, u32[]{:S(2)}, u32[]{:S(2)}) collective-permute-start(bf16[1,66,16,128]{3,2,1,0:T(8,128)(2,1)S(1)} %get-tuple-element.31), channel_id=1, source_target_pairs={{0,16},{4,20},{8,24},{12,28},{16,0},{20,4},{24,8},{28,12},{1,17},{... | collective-permute-start | bytes 811016 | tf_op jit(solution)/shard_map/ppermute | solution.py:41
  23.2 12.1 %collective-permute-start.8 = (bf16[1,4,18,16,128]{4,3,2,1,0:T(8,128)(2,1)S(1)}, bf16[1,4,18,16,128]{4,3,2,1,0:T(8,128)(2,1)S(1)}, u32[]{:S(2)}, u32[]{:S(2)}) collective-permute-start(bf16[1,4,18,16,128]{4,3,2,1,0:T(8,128)(2,1)S(1)} %get-tuple-element.35), channel_id=1, source_target_pairs={{0,4},{4,0},{8,12},{12,8},{16,20},{20,16},{24,28},{28,24},{1,5},{5... | collective-permute-start | bytes 884744 | tf_op jit(solution)/shard_map/ppermute | solution.py:41
  25.1 14.4 %collective-permute-start.11 = (bf16[1,4,18,16,128]{4,3,2,1,0:T(8,128)(2,1)S(1)}, bf16[1,4,18,16,128]{4,3,2,1,0:T(8,128)(2,1)S(1)}, u32[]{:S(2)}, u32[]{:S(2)}) collective-permute-start(bf16[1,4,18,16,128]{4,3,2,1,0:T(8,128)(2,1)S(1)} %get-tuple-element.41), channel_id=1, source_target_pairs={{0,4},{4,0},{8,12},{12,8},{16,20},{20,16},{24,28},{28,24},{1,5},{5... | collective-permute-start | bytes 884744 | tf_op jit(solution)/shard_map/ppermute | solution.py:41
  31.6 14.6 %collective-permute-start.2 = (bf16[4,18,16,128]{3,2,1,0:T(8,128)(2,1)S(1)}, bf16[4,18,16,128]{3,2,1,0:T(8,128)(2,1)S(1)}, u32[]{:S(2)}, u32[]{:S(2)}) collective-permute-start(bf16[4,18,16,128]{3,2,1,0:T(8,128)(2,1)S(1)} %shard_map.48), channel_id=1, source_target_pairs={{0,4},{4,0},{8,12},{12,8},{16,20},{20,16},{24,28},{28,24},{1,5},{5... | collective-permute-start | bytes 884744 | tf_op jit(solution)/shard_map/ppermute | solution.py:41
  35.0 9.7 %collective-permute-start.6 = (bf16[2,34,16,128]{3,2,1,0:T(8,128)(2,1)S(1)}, bf16[2,34,16,128]{3,2,1,0:T(8,128)(2,1)S(1)}, u32[]{:S(2)}, u32[]{:S(2)}) collective-permute-start(bf16[2,34,16,128]{3,2,1,0:T(8,128)(2,1)S(1)} %shard_map.51), channel_id=1, source_target_pairs={{0,8},{4,12},{8,0},{12,4},{16,24},{20,28},{24,16},{28,20},{1,9},{5... | collective-permute-start | bytes 835592 | tf_op jit(solution)/shard_map/ppermute | solution.py:41
  35.3 15.7 %collective-permute-start.9 = (bf16[2,2,18,16,128]{4,3,2,1,0:T(8,128)(2,1)S(1)}, bf16[2,2,18,16,128]{4,3,2,1,0:T(8,128)(2,1)S(1)}, u32[]{:S(2)}, u32[]{:S(2)}) collective-permute-start(bf16[2,2,18,16,128]{4,3,2,1,0:T(8,128)(2,1)S(1)} %shard_map.55), channel_id=1, source_target_pairs={{0,8},{4,12},{8,0},{12,4},{16,24},{20,28},{24,16},{28,20},{1,9},{5... | collective-permute-start | bytes 884744 | tf_op jit(solution)/shard_map/ppermute | solution.py:41
  39.5 14.6 %collective-permute-start.12 = (bf16[2,2,18,16,128]{4,3,2,1,0:T(8,128)(2,1)S(1)}, bf16[2,2,18,16,128]{4,3,2,1,0:T(8,128)(2,1)S(1)}, u32[]{:S(2)}, u32[]{:S(2)}) collective-permute-start(bf16[2,2,18,16,128]{4,3,2,1,0:T(8,128)(2,1)S(1)} %shard_map.59), channel_id=1, source_target_pairs={{0,8},{4,12},{8,0},{12,4},{16,24},{20,28},{24,16},{28,20},{1,9},{5... | collective-permute-start | bytes 884744 | tf_op jit(solution)/shard_map/ppermute | solution.py:41
  44.7 12.1 %collective-permute-start.7 = (bf16[4,18,16,128]{3,2,1,0:T(8,128)(2,1)S(1)}, bf16[4,18,16,128]{3,2,1,0:T(8,128)(2,1)S(1)}, u32[]{:S(2)}, u32[]{:S(2)}) collective-permute-start(bf16[4,18,16,128]{3,2,1,0:T(8,128)(2,1)S(1)} %shard_map.52), channel_id=1, source_target_pairs={{0,4},{4,0},{8,12},{12,8},{16,20},{20,16},{24,28},{28,24},{1,5},{5... | collective-permute-start | bytes 884744 | tf_op jit(solution)/shard_map/ppermute | solution.py:41
  47.0 9.8 %copy-start.6 = (bf16[3,3,3,128,256]{4,3,2,1,0:T(8,128)(2,1)S(1)}, bf16[3,3,3,128,256]{4,3,2,1,0:T(8,128)(2,1)}, u32[]{:S(2)}) copy-start(bf16[3,3,3,128,256]{4,3,2,1,0:T(8,128)(2,1)} %w_ref.5) | copy-start | bytes 5308420
  47.1 9.7 %collective-permute-start.3 = (bf16[18,64,128]{2,1,0:T(8,128)(2,1)S(1)}, bf16[18,64,128]{2,1,0:T(8,128)(2,1)S(1)}, u32[]{:S(2)}, u32[]{:S(2)}) collective-permute-start(bf16[18,64,128]{2,1,0:T(8,128)(2,1)S(1)} %get-tuple-element.48), channel_id=1, source_target_pairs={{0,1},{1,2},{2,3},{4,5},{5,6},{6,7},{8,9},{9,10},{10,11},{12,13},{... | collective-permute-start | bytes 884744 | tf_op jit(solution)/shard_map/ppermute | solution.py:394
  48.5 8.2 %collective-permute-start.4 = (bf16[18,64,128]{2,1,0:T(8,128)(2,1)S(1)}, bf16[18,64,128]{2,1,0:T(8,128)(2,1)S(1)}, u32[]{:S(2)}, u32[]{:S(2)}) collective-permute-start(bf16[18,64,128]{2,1,0:T(8,128)(2,1)S(1)} %get-tuple-element.47), channel_id=1, source_target_pairs={{1,0},{2,1},{3,2},{5,4},{6,5},{7,6},{9,8},{10,9},{11,10},{13,12},{... | collective-permute-start | bytes 884744 | tf_op jit(solution)/shard_map/ppermute | solution.py:395
  51.0 22.8 %collective-permute-start.10 = (bf16[4,1,18,16,128]{4,3,2,1,0:T(8,128)(2,1)S(1)}, bf16[4,1,18,16,128]{4,3,2,1,0:T(8,128)(2,1)S(1)}, u32[]{:S(2)}, u32[]{:S(2)}) collective-permute-start(bf16[4,1,18,16,128]{4,3,2,1,0:T(8,128)(2,1)S(1)} %shard_map.56), channel_id=1, source_target_pairs={{0,16},{4,20},{8,24},{12,28},{16,0},{20,4},{24,8},{28,12},{1,17},{... | collective-permute-start | bytes 884744 | tf_op jit(solution)/shard_map/ppermute | solution.py:41
  54.2 28.5 %collective-permute-start.13 = (bf16[4,1,18,16,128]{4,3,2,1,0:T(8,128)(2,1)S(1)}, bf16[4,1,18,16,128]{4,3,2,1,0:T(8,128)(2,1)S(1)}, u32[]{:S(2)}, u32[]{:S(2)}) collective-permute-start(bf16[4,1,18,16,128]{4,3,2,1,0:T(8,128)(2,1)S(1)} %shard_map.60), channel_id=1, source_target_pairs={{0,16},{4,20},{8,24},{12,28},{16,0},{20,4},{24,8},{28,12},{1,17},{... | collective-permute-start | bytes 884744 | tf_op jit(solution)/shard_map/ppermute | solution.py:41
  82.7 21.8 %copy-start.2 = (f32[2,16,64,256]{3,2,1,0:T(8,128)S(1)}, f32[2,16,64,256]{3,2,1,0:T(8,128)}, u32[]{:S(2)}) copy-start(f32[2,16,64,256]{3,2,1,0:T(8,128)} %get-tuple-element.43.refs_0_) | copy-start | bytes 6291460
  82.7 21.8 %copy-start.4 = (f32[256]{0:T(256)S(1)}, f32[256]{0:T(256)}, u32[]{:S(2)}) copy-start(f32[256]{0:T(256)} %param.6) | copy-start | bytes 3076
  82.7 21.8 %copy-start.5 = (f32[256]{0:T(256)S(1)}, f32[256]{0:T(256)}, u32[]{:S(2)}) copy-start(f32[256]{0:T(256)} %param.7) | copy-start | bytes 3076
  104.4 1.6 %copy-start.3 = (f32[2,16,64,256]{3,2,1,0:T(8,128)S(1)}, f32[2,16,64,256]{3,2,1,0:T(8,128)}, u32[]{:S(2)}) copy-start(f32[2,16,64,256]{3,2,1,0:T(8,128)} %get-tuple-element.46.refs_3_) | copy-start | bytes 6291460

commit v2 on v1

v2 whole, which is shorter than its diff:
```python
import functools

import jax
import jax.numpy as jnp
from jax import lax
from jax.experimental import pallas as pl
from jax.experimental.pallas import tpu as pltpu
from jax.sharding import PartitionSpec as P

GROUPS = 32
LEVELS = 3
TAPS = 3
inv_root = 0.7071067811865476
F32 = jnp.float32
BF16 = jnp.bfloat16
VMEM = pl.BlockSpec(memory_space=pltpu.VMEM)
SMEM = pl.BlockSpec(memory_space=pltpu.SMEM)
HBM = pl.BlockSpec(memory_space=pltpu.HBM)
MIB = 1 << 20
MARK = jax.ShapeDtypeStruct((8, 128), jnp.float32)


def shape(dims, dtype):
    return jax.ShapeDtypeStruct(dims, dtype)


def handing_on(body, inputs):
    def wrapped(me_ref, before, *refs):
        refs[inputs][...] = jnp.zeros_like(before)
        body(me_ref, *refs[:inputs], *refs[inputs + 1 :])

    return wrapped


def on_core(body, outs, scalar, arrays, scratch=(), limit=28, specs=None):
    mark, *given = pl.pallas_call(
        handing_on(body, len(arrays)),
        out_shape=[MARK] + outs,
        in_specs=[SMEM, VMEM] + (specs or [VMEM] * len(arrays)),
        out_specs=[VMEM] + [VMEM] * len(outs),
        scratch_shapes=list(scratch),
        compiler_params=pltpu.CompilerParams(vmem_limit_bytes=limit * MIB),
        cost_estimate=pl.CostEstimate(flops=0, bytes_accessed=0, transcendentals=0),
    )(*scalar, *arrays)
    return (scalar[0], mark), *given


def swap(block, mask):
    count = lax.axis_size("tm")
    return lax.ppermute(block, "tm", [(i, i ^ mask) for i in range(count)])


def combined(bits):
    masks = [0]
    for bit in bits:
        masks += [m | 1 << bit for m in masks]
    return masks[1:]


class Trip:
    def __init__(self, rows, groups):
        self.rows = rows
        self.groups = [g for g in groups if g]
        self.count = 1 << sum(len(g) for g in self.groups)
        self.place = {(0, m): None for m in range(self.count)}
        self.arrays = []
        self.steps = 0

    def leaving(self):
        group = sum(1 << b for b in self.groups[self.steps])
        past = sum(1 << b for g in self.groups[: self.steps] for b in g)
        held = sorted(k for k in self.place if not k[1] & past)
        return {m: [k for k in held if k[1] & group == m] for m in combined(self.groups[self.steps])}

    def swap(self, blocks):
        for (mask, wanted), block in zip(self.leaving().items(), blocks):
            got = lax.ppermute(block, "tm", [(i, i ^ mask) for i in range(self.count)])
            for i, (source, dest) in enumerate(wanted):
                self.place[(source ^ mask, dest ^ mask)] = (len(self.arrays), i)
            self.arrays.append(got)
        self.steps += 1

    def step(self, me, after=()):
        places = [[self.place[k] for k in wanted] for wanted in self.leaving().values()]

        def body(me_ref, *refs):
            for out, chosen in zip(refs[-len(places) :], places):
                for i, (array, at) in enumerate(chosen):
                    out[i] = refs[array][at]

        outs = [shape((len(p),) + self.arrays[0].shape[1:], BF16) for p in places]
        me, *blocks = on_core(body, outs, me, self.arrays + list(after), limit=24)
        self.swap(blocks)
        return me

    def gather(self, me, refs, blocks):
        for source in range(self.count):
            array, at = self.place[(source, 0)]
            blocks[me ^ source] = refs[array][at]


def part_body(trips, me_ref, video, *refs):
    *outs, wide = refs
    width = video.shape[2]
    columns = width // trips[0].count
    for i, trip in enumerate(trips):
        cells = jnp.swapaxes(jnp.concatenate([video[:, h] for h in trip.rows], 0), 0, 1)
        edge = jnp.zeros((1,) + cells.shape[1:], BF16)
        wide[0:1] = edge
        wide[1 : width + 1] = cells
        wide[width + 1 : width + 2] = edge
        for _, masks in trip.first:
            out = outs.pop(0)
            for place, mask in enumerate(masks):
                out[place] = wide[pl.ds((me_ref[0] ^ mask) * columns, columns + 2)]


def part_rows(me, video, trips):
    frames, _, width, channels = video.shape
    count = trips[0].count
    tail = (width // count + 2, 2 * frames, channels)
    outs = []
    for trip in trips:
        leaving = trip.leaving()
        away = [k[1] for wanted in leaving.values() for k in wanted]
        kept = [m for m in range(count) if m not in away]
        trip.first = [(0, kept)] + [(m, [k[1] for k in wanted]) for m, wanted in leaving.items()]
        trip.place.update({(0, m): (0, i) for i, m in enumerate(kept)})
        outs += [shape((len(masks),) + tail, BF16) for _, masks in trip.first]
    body = functools.partial(part_body, trips)
    scratch = [pltpu.VMEM((width + 2, 2 * frames, channels), BF16)]
    me, *parts = on_core(body, outs, me, [video], scratch, limit=24)
    for trip in trips:
        trip.arrays.append(parts.pop(0))
        trip.swap([parts.pop(0) for _ in trip.first[1:]])
    return me


def widen(wide, row, column, cells):
    channels = cells.shape[1]
    frame = lax.broadcasted_iota(jnp.int32, cells.shape, 0)
    for tap in range(TAPS):
        back = TAPS - 1 - tap
        moved = cells
        if back:
            moved = jnp.where(frame < back, 0.0, pltpu.roll(cells, back, 0))
        wide[row, column, :, tap * channels : (tap + 1) * channels] = moved.astype(BF16)


def wavelet_rows(blocks, wide, plain=None):
    count, columns = blocks.shape[:2]
    rows = wide.shape[0]
    frames = blocks.shape[2] // rows

    def column(i, _):
        values = [blocks[b, i].astype(F32) for b in range(count)]
        for level in range(LEVELS):
            span = 1 << level
            later = list(values)
            for b in range(count):
                if not b & span:
                    later[b] = (values[b] + values[b + span]) * inv_root
                    later[b + span] = (values[b] - values[b + span]) * inv_root
            values = later
        for row in range(rows):
            cells = jnp.concatenate([v[row * frames : (row + 1) * frames] for v in values], 0)
            widen(wide, row, i, cells)
            if plain is not None:
                plain[row, i] = cells.astype(BF16)
        return 0

    lax.fori_loop(0, columns, column, 0)


def outer_body(trip, me_ref, *refs):
    *held, wide, plain, blocks = refs
    trip.gather(me_ref[0], held, blocks)
    wavelet_rows(blocks, wide, plain)


def taps(w_ref, terms, before=None):
    columns = terms[0][0].shape[1] - 2
    left, right = [], []
    for wide, row, i in terms:
        for j in range(TAPS):
            cells = wide[row, pl.ds(j, columns)]
            left.append(cells.reshape(-1, cells.shape[-1]))
            right += [w_ref[k, i, j] for k in range(TAPS)]
    total = jnp.dot(
        jnp.concatenate(left, -1), jnp.concatenate(right, 0), preferred_element_type=F32
    )
    if before is not None:
        total = total + before
    return total


def row_sums(total):
    mean = jnp.sum(total, 0, keepdims=True) * (1.0 / total.shape[0])
    apart = total - mean
    return mean, jnp.sum(apart * apart, 0, keepdims=True)


def finish(total, out, sums, row):
    out[row] = total.reshape(out.shape[1:])
    mean, squares = row_sums(total)
    sums[row, 0:1] = mean
    sums[row, 1:2] = squares


def keep(total, out, row):
    out[row] = total.reshape(out.shape[1:])


def flat(ref, row):
    return ref[row].reshape(-1, ref.shape[-1])


def stage_a(trip, me_ref, w_ref, outer, *refs):
    *held, part0, part1, part2, wide, blocks = refs
    trip.gather(me_ref[0], held, blocks)
    wavelet_rows(blocks, wide)
    keep(taps(w_ref, [(outer, 0, 1), (wide, 0, 2)]), part0, 0)
    keep(taps(w_ref, [(wide, 1, 0), (outer, 1, 1)]), part0, 1)
    keep(taps(w_ref, [(outer, 0, 0), (wide, 0, 1)]), part1, 0)
    keep(taps(w_ref, [(wide, 1, 1), (outer, 1, 2)]), part1, 1)
    keep(taps(w_ref, [(wide, 0, 0)]), part2, 0)
    keep(taps(w_ref, [(wide, 1, 2)]), part2, 1)


def stage_b(trip, me_ref, w_ref, above, below, part0, part1, part2, *refs):
    *held, done0, done1, next2, part3, sums, wide, halo, blocks = refs
    trip.gather(me_ref[0], held, blocks)
    wavelet_rows(blocks, wide)

    def column(i, _):
        widen(halo, 0, i, above[i].astype(F32))
        widen(halo, 1, i, below[i].astype(F32))
        return 0

    lax.fori_loop(0, above.shape[0], column, 0)
    finish(taps(w_ref, [(wide, 0, 2)], flat(part1, 0)), done1, sums.at[2:4], 0)
    finish(taps(w_ref, [(wide, 1, 0)], flat(part1, 1)), done1, sums.at[2:4], 1)
    keep(taps(w_ref, [(wide, 0, 1)], flat(part2, 0)), next2, 0)
    keep(taps(w_ref, [(wide, 1, 1)], flat(part2, 1)), next2, 1)
    keep(taps(w_ref, [(wide, 0, 0)]), part3, 0)
    keep(taps(w_ref, [(wide, 1, 2)]), part3, 1)
    finish(taps(w_ref, [(halo, 0, 0)], flat(part0, 0)), done0, sums, 0)
    finish(taps(w_ref, [(halo, 1, 2)], flat(part0, 1)), done0, sums, 1)


def stage_c(trip, me_ref, w_ref, part2, part3, earlier, *refs):
    *held, done2, done3, message, sums, wide, blocks = refs
    trip.gather(me_ref[0], held, blocks)
    wavelet_rows(blocks, wide)
    finish(taps(w_ref, [(wide, 0, 2)], flat(part2, 0)), done2, sums, 0)
    finish(taps(w_ref, [(wide, 1, 0)], flat(part2, 1)), done2, sums, 1)
    finish(taps(w_ref, [(wide, 0, 1), (wide, 1, 2)], flat(part3, 0)), done3, sums.at[2:4], 0)
    finish(taps(w_ref, [(wide, 0, 0), (wide, 1, 1)], flat(part3, 1)), done3, sums.at[2:4], 1)
    rows = [sums[r] for r in range(4)]
    rows += [earlier[r] for r in range(4)]
    entries = wide.shape[2] * (wide.shape[1] - 2)
    mean = sum(r[0:1] for r in rows) * (1.0 / len(rows))
    squares = sum(r[1:2] + entries * (r[0:1] - mean) * (r[0:1] - mean) for r in rows)
    lanes = message.shape[-1]
    parts = [v[:, c : c + lanes] for v in (mean, squares) for c in range(0, mean.shape[1], lanes)]
    packed = jnp.concatenate(parts + [jnp.zeros((8 - len(parts), lanes), F32)], 0)
    message[...] = jnp.broadcast_to(packed[None], message.shape)


def over_group(values, size):
    lanes = values.shape[-1]
    lane = lax.broadcasted_iota(jnp.int32, values.shape, values.ndim - 1)
    step = 1
    while step < size:
        axis = values.ndim - 1
        down = pltpu.roll(values, step, axis)
        up = pltpu.roll(values, lanes - step, axis)
        values = values + jnp.where((lane & step) != 0, down, up)
        step *= 2
    return values


def norm_body(entries, size, all_ref, gain_ref, bias_ref, *refs):
    *rows, out, affine = refs

    @pl.when(pl.program_id(0) == 0)
    def _():
        devices = all_ref.shape[0]
        half = gain_ref.shape[0]
        means = all_ref[:, 0:half]
        mean = jnp.sum(means, 0) * (1.0 / devices)
        apart = means - mean[None]
        squares = jnp.sum(all_ref[:, half : 2 * half] + entries * apart * apart, 0)
        group_mean = over_group(mean, size) * (1.0 / size)
        apart = mean - group_mean
        group = over_group(squares + (entries * devices) * apart * apart, size)
        variance = group * (1.0 / (entries * devices * size))
        scale = (0.5 * gain_ref[...]) / jnp.sqrt(variance + 1e-05)
        for p in range(half):
            lanes = slice(p * scale.shape[1], (p + 1) * scale.shape[1])
            affine[0:1, lanes] = group_mean[p : p + 1]
            affine[1:2, lanes] = scale[p : p + 1]
            affine[2:3, lanes] = 0.5 * bias_ref[p : p + 1]

    mean, scale, bias = affine[0:1], affine[1:2], affine[2:3]
    channels = mean.shape[1]
    height = 2 * len(rows)
    for h in range(height):
        ref, place = (rows[h], 0) if h < len(rows) else (rows[height - 1 - h], 1)
        for w in range(ref.shape[1]):
            half_v = (ref[place, w] - mean) * scale + bias
            value = half_v + half_v * jnp.tanh(half_v)
            lanes = (h % 2 * 2 + w % 2) * channels
            out[h // 2, w // 2, :, lanes : lanes + channels] = value.astype(BF16)


def per_device(video, conv_weight, norm_gain, norm_bias):
    frames, height, width, channels = video.shape
    outputs = conv_weight.shape[-1]
    count = lax.axis_size("tm")
    strips = lax.axis_size("rows")
    devices = count * strips
    columns = width // count
    time = frames * count
    me = lax.axis_index("tm").astype(jnp.int32).reshape(1)
    me = (me, jnp.zeros(MARK.shape, MARK.dtype))
    bits = count.bit_length() - 1
    top, rest = bits - 1, list(range(1, bits - 1))
    outer_trip = Trip((0, 7), [[top], [0] + rest])
    third_trip = Trip((2, 5), [[0], [top], rest])
    second_trip = Trip((1, 6), [[0], rest, [top]])
    inner_trip = Trip((3, 4), [rest, [0], [top]])
    trips = [outer_trip, third_trip, second_trip, inner_trip]
    me = part_rows(me, video, trips)
    for trip in (outer_trip, third_trip, second_trip, inner_trip, third_trip, second_trip, inner_trip):
        me = trip.step(me)

    def blocks(rows):
        return pltpu.VMEM((count, columns + 2, rows * frames, channels), BF16)

    def wide(rows):
        return (rows, columns + 2, time, TAPS * channels)

    row_pair = shape((2, columns, time, outputs), F32)
    four_sums = shape((4, 2, outputs), F32)

    me, outer, plain = on_core(
        functools.partial(outer_body, outer_trip),
        [shape(wide(2), BF16), shape((2, columns + 2, time, channels), BF16)],
        me,
        outer_trip.arrays,
        [blocks(2)],
    )
    down = [(i, i + 1) for i in range(strips - 1)]
    up = [(i + 1, i) for i in range(strips - 1)]
    above = lax.ppermute(plain[1], "rows", down)
    below = lax.ppermute(plain[0], "rows", up)
    me, part0, part1, part2 = on_core(
        functools.partial(stage_a, second_trip),
        [row_pair, row_pair, row_pair],
        me,
        [conv_weight, outer] + second_trip.arrays,
        [pltpu.VMEM(wide(2), BF16), blocks(2)],
    )
    me, done0, done1, part2, part3, sums = on_core(
        functools.partial(stage_b, third_trip),
        [row_pair, row_pair, row_pair, row_pair, four_sums],
        me,
        [conv_weight, above, below, part0, part1, part2] + third_trip.arrays,
        [pltpu.VMEM(wide(2), BF16), pltpu.VMEM(wide(2), BF16), blocks(2)],
    )
    me, done2, done3, message = on_core(
        functools.partial(stage_c, inner_trip),
        [row_pair, row_pair, shape((devices, 8, 128), F32)],
        me,
        [conv_weight, part2, part3, sums] + inner_trip.arrays,
        [pltpu.VMEM((4, 2, outputs), F32), pltpu.VMEM(wide(2), BF16), blocks(2)],
    )
    messages = lax.all_to_all(message, ("tm", "rows"), 0, 0, tiled=True)

    steps = columns // 2 // min(2, columns // 2)
    block = columns // steps
    rows_spec = pl.BlockSpec((2, block, time, outputs), lambda g: (0, g, 0, 0))
    return pl.pallas_call(
        functools.partial(norm_body, float(height * columns * time), outputs // GROUPS),
        grid=(steps,),
        out_shape=shape((height // 2, columns // 2, time, 4 * outputs), BF16),
        in_specs=[VMEM, VMEM, VMEM] + [rows_spec] * 4,
        out_specs=pl.BlockSpec((height // 2, block // 2, time, 4 * outputs), lambda g: (0, g, 0, 0)),
        scratch_shapes=[pltpu.VMEM((8, outputs), F32)],
        compiler_params=pltpu.CompilerParams(vmem_limit_bytes=40 * MIB),
    )(messages, norm_gain.reshape(-1, 128), norm_bias.reshape(-1, 128), done0, done1, done2, done3)


def solution(mesh):
    placed = (P("tm", "rows", None, None), P(), P(), P())
    return jax.shard_map(
        per_device,
        mesh=mesh,
        in_specs=placed,
        out_specs=P("rows", "tm", None, None),
        check_vma=False,
    )
```

time: 110 us -> 91.4 us (0.83)
  Pallas kernels: 34.5 us -> 26 us
  waiting for transfers between devices: 37.3 us -> 30 us
  local copies, waits for them, and re-layouts: 3.24 us -> 1.65 us
    pallas_call x16 -> x12, Pallas kernels: 30.2 us -> 21.7 us  [on_core(): pl.pallas_call(handing_on(body, len(arrays)), out_shape=[MARK] + outs, in...]
    ppermute x12 -> x13, waiting for transfers between devices: 37.3 us -> 30 us  [swap(): got = lax.ppermute(block, 'tm', [(i, i ^ mask) for i in range(self.count)])]
    ppermute x12 -> x13, starting transfers between devices: 19.2 us -> 16.7 us  [swap(): got = lax.ppermute(block, 'tm', [(i, i ^ mask) for i in range(self.count)])]
    ppermute x1, starting transfers between devices: 1.44 us -> 3.23 us  [per_device(): above = lax.ppermute(plain[1], 'rows', down)]
    unnamed x14 -> x8, local copies, waits for them, and re-layouts: 3.2 us -> 1.6 us
  transfers between devices with their start and end apart: 14 -> 15, of which waited for: 8 -> 7; matrix products, arithmetic and copies ran while one was open for 0% -> 0% of each run, Pallas kernels for 19% -> 17%
where the time goes in v2:
time: 91.4 us; the launch traced here: 91.2 us
  waiting for transfers between devices  30 us (33%)
  Pallas kernels  26 us (28%)
  starting transfers between devices  21.3 us (23%)
  blocking collectives  12.1 us (13%)
  local copies, waits for them, and re-layouts  1.65 us (2%)
    ppermute x13, waiting for transfers between devices, swap(): got = lax.ppermute(block, 'tm', [(i, i ^ mask) for i in range(self.count)])  30 us
    pallas_call x12, Pallas kernels, on_core(): pl.pallas_call(handing_on(body, len(arrays)), out_shape=[MARK] + outs, in...  21.7 us
    ppermute x13, starting transfers between devices, swap(): got = lax.ppermute(block, 'tm', [(i, i ^ mask) for i in range(self.count)])  16.7 us
    all_to_all x1, blocking collectives, per_device(): messages = lax.all_to_all(message, ('tm', 'rows'), 0, 0, tiled=True)  12.1 us
    pallas_call x1, Pallas kernels, per_device(): pl.pallas_call(functools.partial(norm_body, float(height * columns * time...  4.24 us
    ppermute x1, starting transfers between devices, per_device(): above = lax.ppermute(plain[1], 'rows', down)  3.23 us
  transfers between devices with their start and end apart: 15, of which 7 were waited for; matrix products, arithmetic and copies ran while one was open for 0% of the time, Pallas kernels for 17%

profile of v2, /device:TPU:0, one launch (start us, length us, event | category | flops | bytes accessed | tf_op | source)
XLA Modules:
  0.0 91.2 jit_solution(2822450502635002925)
XLA Ops:
  0.0 0.0 copy-start.1
  0.0 1.6 %copy-done.1 = bf16[8,8,128,128]{3,2,1,0:T(8,128)(2,1)S(1)} copy-done((bf16[8,8,128,128]{3,2,1,0:T(8,128)(2,1)S(1)}, bf16[8,8,128,128]{3,2,1,0:T(8,128)(2,1)}, u32[]{:S(2)}) %copy-start.1) | copy-done | bytes 2097176
  1.6 1.2 %shard_map.46 = (f32[8,128]{1,0:T(8,128)S(1)}, bf16[4,18,16,128]{3,2,1,0:T(8,128)(2,1)S(1)}, bf16[4,18,16,128]{3,2,1,0:T(8,128)(2,1)S(1)}, bf16[4,18,16,128]{3,2...) custom-call(s32[1]{0:T(128)} %bitcast.me_ref, ...), custom_call_target="tpu_custom_call" | custom-call | tf_op jit(solution)/shard_map/pallas_call | solution.py:36
  2.8 4.1 %collective-permute-start = (bf16[4,18,16,128]{3,2,1,0:T(8,128)(2,1)S(1)}, bf16[4,18,16,128]{3,2,1,0:T(8,128)(2,1)S(1)}, u32[]{:S(2)}, u32[]{:S(2)}) collective-permute-start(bf16[4,18,16,128]{3,2,1,0:T(8,128)(2,1)S(1)} %get-tuple-element.48), channel_id=1, source_target_pairs={{0,16},{4,20},{8,24},{12,28},{16,0},{20,4},{24,8},{28,12},{1,17},{... | collective-permute-start | bytes 884744 | tf_op jit(solution)/shard_map/ppermute | solution.py:77
  6.9 1.5 %collective-permute-start.1 = (bf16[4,18,16,128]{3,2,1,0:T(8,128)(2,1)S(1)}, bf16[4,18,16,128]{3,2,1,0:T(8,128)(2,1)S(1)}, u32[]{:S(2)}, u32[]{:S(2)}) collective-permute-start(bf16[4,18,16,128]{3,2,1,0:T(8,128)(2,1)S(1)} %get-tuple-element.51), channel_id=1, source_target_pairs={{0,4},{4,0},{8,12},{12,8},{16,20},{20,16},{24,28},{28,24},{1,5},{5... | collective-permute-start | bytes 884744 | tf_op jit(solution)/shard_map/ppermute | solution.py:77
  8.4 0.5 collective-permute-start.2
  8.9 1.6 %collective-permute-start.3 = (bf16[4,18,16,128]{3,2,1,0:T(8,128)(2,1)S(1)}, bf16[4,18,16,128]{3,2,1,0:T(8,128)(2,1)S(1)}, u32[]{:S(2)}, u32[]{:S(2)}) collective-permute-start(bf16[4,18,16,128]{3,2,1,0:T(8,128)(2,1)S(1)} %get-tuple-element.57), channel_id=1, source_target_pairs={{0,8},{4,12},{8,0},{12,4},{16,24},{20,28},{24,16},{28,20},{1,9},{5... | collective-permute-start | bytes 884744 | tf_op jit(solution)/shard_map/ppermute | solution.py:77
  10.5 9.8 %collective-permute-done.refs_1_ = bf16[4,18,16,128]{3,2,1,0:T(8,128)(2,1)S(1)} collective-permute-done((bf16[4,18,16,128]{3,2,1,0:T(8,128)(2,1)S(1)}, bf16[4,18,16,128]{3,2,1,0:T(8,128)(2,1)S(1)}, u32[]{:S(2)}, u32[]{:S(2)}) %collective-permute-start) | collective-permute-done | bytes 294944 | tf_op jit(solution)/shard_map/ppermute | solution.py:77
  20.3 0.0 collective-permute-done.1.refs_1_.refs_7_
  20.4 0.1 collective-permute-start.4
  20.5 1.2 %collective-permute-done.2.refs_1_.refs_3_ = bf16[4,18,16,128]{3,2,1,0:T(8,128)(2,1)S(1)} collective-permute-done((bf16[4,18,16,128]{3,2,1,0:T(8,128)(2,1)S(1)}, bf16[4,18,16,128]{3,2,1,0:T(8,128)(2,1)S(1)}, u32[]{:S(2)}, u32[]{:S(2)}) %collective-permute-start.2) | collective-permute-done | bytes 294944 | tf_op jit(solution)/shard_map/ppermute | solution.py:77
  21.7 3.0 %collective-permute-start.5 = (bf16[4,18,16,128]{3,2,1,0:T(8,128)(2,1)S(1)}, bf16[4,18,16,128]{3,2,1,0:T(8,128)(2,1)S(1)}, u32[]{:S(2)}, u32[]{:S(2)}) collective-permute-start(bf16[4,18,16,128]{3,2,1,0:T(8,128)(2,1)S(1)} %get-tuple-element.61), channel_id=1, source_target_pairs={{0,8},{4,12},{8,0},{12,4},{16,24},{20,28},{24,16},{28,20},{1,9},{5... | collective-permute-start | bytes 884744 | tf_op jit(solution)/shard_map/ppermute | solution.py:77
  24.6 0.0 collective-permute-done.3.refs_1_.refs_5_
  24.7 1.6 %collective-permute-start.6 = (bf16[4,18,16,128]{3,2,1,0:T(8,128)(2,1)S(1)}, bf16[4,18,16,128]{3,2,1,0:T(8,128)(2,1)S(1)}, u32[]{:S(2)}, u32[]{:S(2)}) collective-permute-start(bf16[4,18,16,128]{3,2,1,0:T(8,128)(2,1)S(1)} %get-tuple-element.63), channel_id=1, source_target_pairs={{0,4},{4,0},{8,12},{12,8},{16,20},{20,16},{24,28},{28,24},{1,5},{5... | collective-permute-start | bytes 884744 | tf_op jit(solution)/shard_map/ppermute | solution.py:77
  26.2 0.5 collective-permute-start.7
  26.8 0.0 collective-permute-start.8
  26.8 9.1 %collective-permute-done.4.refs_2_.refs_8_ = bf16[4,18,16,128]{3,2,1,0:T(8,128)(2,1)S(1)} collective-permute-done((bf16[4,18,16,128]{3,2,1,0:T(8,128)(2,1)S(1)}, bf16[4,18,16,128]{3,2,1,0:T(8,128)(2,1)S(1)}, u32[]{:S(2)}, u32[]{:S(2)}) %collective-permute-start.4) | collective-permute-done | bytes 294944 | tf_op jit(solution)/shard_map/ppermute | solution.py:77
  35.9 0.0 collective-permute-start.9
  35.9 0.0 copy-start
  36.0 1.1 %collective-permute-done.5.refs_2_.refs_4_ = bf16[4,18,16,128]{3,2,1,0:T(8,128)(2,1)S(1)} collective-permute-done((bf16[4,18,16,128]{3,2,1,0:T(8,128)(2,1)S(1)}, bf16[4,18,16,128]{3,2,1,0:T(8,128)(2,1)S(1)}, u32[]{:S(2)}, u32[]{:S(2)}) %collective-permute-start.5) | collective-permute-done | bytes 294944 | tf_op jit(solution)/shard_map/ppermute | solution.py:77
  37.1 1.7 %collective-permute-start.10 = (bf16[4,18,16,128]{3,2,1,0:T(8,128)(2,1)S(1)}, bf16[4,18,16,128]{3,2,1,0:T(8,128)(2,1)S(1)}, u32[]{:S(2)}, u32[]{:S(2)}) collective-permute-start(bf16[4,18,16,128]{3,2,1,0:T(8,128)(2,1)S(1)} %get-tuple-element.70), channel_id=1, source_target_pairs={{0,16},{4,20},{8,24},{12,28},{16,0},{20,4},{24,8},{28,12},{1,17},{... | collective-permute-start | bytes 884744 | tf_op jit(solution)/shard_map/ppermute | solution.py:77
  38.8 0.0 collective-permute-done.6.refs_2_.refs_6_
  38.8 2.1 %collective-permute-start.13 = (bf16[4,18,16,128]{3,2,1,0:T(8,128)(2,1)S(1)}, bf16[4,18,16,128]{3,2,1,0:T(8,128)(2,1)S(1)}, u32[]{:S(2)}, u32[]{:S(2)}) collective-permute-start(bf16[4,18,16,128]{3,2,1,0:T(8,128)(2,1)S(1)} %get-tuple-element.76), channel_id=1, source_target_pairs={{0,8},{4,12},{8,0},{12,4},{16,24},{20,28},{24,16},{28,20},{1,9},{5... | collective-permute-start | bytes 884744 | tf_op jit(solution)/shard_map/ppermute | solution.py:77
  41.0 0.0 collective-permute-done.7.refs_2_
  41.0 4.1 %collective-permute-done.8.refs_3_ = bf16[2,18,16,128]{3,2,1,0:T(8,128)(2,1)S(1)} collective-permute-done((bf16[2,18,16,128]{3,2,1,0:T(8,128)(2,1)S(1)}, bf16[2,18,16,128]{3,2,1,0:T(8,128)(2,1)S(1)}, u32[]{:S(2)}, u32[]{:S(2)}) %collective-permute-start.8) | collective-permute-done | bytes 147488 | tf_op jit(solution)/shard_map/ppermute | solution.py:77
  45.1 4.4 %collective-permute-done.9.refs_4_ = bf16[2,18,16,128]{3,2,1,0:T(8,128)(2,1)S(1)} collective-permute-done((bf16[2,18,16,128]{3,2,1,0:T(8,128)(2,1)S(1)}, bf16[2,18,16,128]{3,2,1,0:T(8,128)(2,1)S(1)}, u32[]{:S(2)}, u32[]{:S(2)}) %collective-permute-start.9) | collective-permute-done | bytes 147488 | tf_op jit(solution)/shard_map/ppermute | solution.py:77
  49.5 0.7 shard_map.54
  50.3 1.3 %collective-permute-start.12 = (bf16[18,64,128]{2,1,0:T(8,128)(2,1)S(1)}, bf16[18,64,128]{2,1,0:T(8,128)(2,1)S(1)}, u32[]{:S(2)}, u32[]{:S(2)}) collective-permute-start(bf16[18,64,128]{2,1,0:T(8,128)(2,1)S(1)} %get-tuple-element.87), channel_id=1, source_target_pairs={{1,0},{2,1},{3,2},{5,4},{6,5},{7,6},{9,8},{10,9},{11,10},{13,12},{... | collective-permute-start | bytes 884744 | tf_op jit(solution)/shard_map/ppermute | solution.py:357
  51.6 3.2 %collective-permute-start.11 = (bf16[18,64,128]{2,1,0:T(8,128)(2,1)S(1)}, bf16[18,64,128]{2,1,0:T(8,128)(2,1)S(1)}, u32[]{:S(2)}, u32[]{:S(2)}) collective-permute-start(bf16[18,64,128]{2,1,0:T(8,128)(2,1)S(1)} %get-tuple-element.88), channel_id=1, source_target_pairs={{0,1},{1,2},{2,3},{4,5},{5,6},{6,7},{8,9},{9,10},{10,11},{12,13},{... | collective-permute-start | bytes 884744 | tf_op jit(solution)/shard_map/ppermute | solution.py:356
  54.9 0.1 collective-permute-start.14
  54.9 0.0 collective-permute-done.10.refs_5_
  55.0 0.0 copy-done
  55.0 7.2 %shard_map.55 = (f32[8,128]{1,0:T(8,128)S(1)}, f32[2,16,64,256]{3,2,1,0:T(8,128)S(1)}, f32[2,16,64,256]{3,2,1,0:T(8,128)S(1)}, f32[2,16,64,256]{3,2,1,0:T(8,128)S(1)}) custom-call(s32[1]{0:T(128)} %bitcast.me_ref, f32[8,128]{1,0:T(8,128)S(1)} %get-tuple-element.68.before, bf16[3,3,3,128,256]{4,3,2,1,0:T(8,128)(2,1)S(1)} %copy-done, ...), custom_call_target="tpu_custom_call" | custom-call | tf_op jit(solution)/shard_map/pallas_call | solution.py:36
  62.1 0.0 collective-permute-done.13.refs_9_
  62.1 0.0 collective-permute-done.12.refs_2_
  62.1 0.0 collective-permute-done.11.refs_1_
  62.2 7.3 %shard_map.56 = (f32[8,128]{1,0:T(8,128)S(1)}, f32[2,16,64,256]{3,2,1,0:T(8,128)S(1)}, f32[2,16,64,256]{3,2,1,0:T(8,128)S(1)}, f32[2,16,64,256]{3,2,1,0:T(8,128)...) custom-call(s32[1]{0:T(128)} %bitcast.me_ref, f32[8,128]{1,0:T(8,128)S(1)} %get-tuple-element.71.before, ...), custom_call_target="tpu_custom_call" | custom-call | tf_op jit(solution)/shard_map/pallas_call | solution.py:36
  69.5 0.2 collective-permute-done.14.refs_7_
  69.6 0.0 copy-start.2
  69.6 0.0 copy-start.3
  69.6 5.2 %shard_map.57 = (f32[8,128]{1,0:T(8,128)}, f32[2,16,64,256]{3,2,1,0:T(8,128)S(1)}, f32[2,16,64,256]{3,2,1,0:T(8,128)S(1)}, f32[32,8,128]{2,1,0:T(8,128)S(1)}) custom-call(s32[1]{0:T(128)} %bitcast.me_ref, f32[8,128]{1,0:T(8,128)S(1)} %get-tuple-element.77.before, bf16[3,3,3,128,256]{4,3,2,1,0:T(8,128)(2,1)S(1)} %copy-done, ...), custom_call_target="tpu_custom_call" | custom-call | tf_op jit(solution)/shard_map/pallas_call | solution.py:36
  74.8 12.1 %all_to_all.5.all_ref = f32[32,8,128]{2,1,0:T(8,128)S(1)} all-to-all(f32[32,8,128]{2,1,0:T(8,128)S(1)} %get-tuple-element.82), channel_id=1, replica_groups=mesh['tm'=8,'rows'=4] {'tm','rows'}, dimensions={0} | all-to-all | bytes 262144 | tf_op jit(solution)/shard_map/all_to_all | solution.py:379
  86.9 0.0 copy-done.2
  87.0 0.0 copy-done.3
  87.0 4.2 %shard_map.58 = bf16[4,8,64,1024]{3,2,1,0:T(8,128)(2,1)} custom-call(f32[32,8,128]{2,1,0:T(8,128)S(1)} %all_to_all.5.all_ref, f32[2,128]{1,0:T(2,128)S(1)} %bitcast.7, f32[2,128]{1,0:T(2,128)S(1)} %bitcast.8, f32[2,16,64,256]{3,2,1,0:T(8,128)S(1)} %get-tuple-element.83.refs_0_, f32[2,16,64,256]{3,2,1,0:T(8,128)S(1)} %get-tuple-element.84.refs_1_, ...), custom_call_target="tpu_custom_call" | custom-call | tf_op jit(solution)/shard_map/pallas_call | solution.py:384
  (9 shorter events, 0.2 us)
Async XLA Ops:
  0.0 1.6 %copy-start.1 = (bf16[8,8,128,128]{3,2,1,0:T(8,128)(2,1)S(1)}, bf16[8,8,128,128]{3,2,1,0:T(8,128)(2,1)}, u32[]{:S(2)}) copy-start(bf16[8,8,128,128]{3,2,1,0:T(8,128)(2,1)} %refs_0_.4) | copy-start | bytes 6291460
  2.8 17.5 %collective-permute-start = (bf16[4,18,16,128]{3,2,1,0:T(8,128)(2,1)S(1)}, bf16[4,18,16,128]{3,2,1,0:T(8,128)(2,1)S(1)}, u32[]{:S(2)}, u32[]{:S(2)}) collective-permute-start(bf16[4,18,16,128]{3,2,1,0:T(8,128)(2,1)S(1)} %get-tuple-element.48), channel_id=1, source_target_pairs={{0,16},{4,20},{8,24},{12,28},{16,0},{20,4},{24,8},{28,12},{1,17},{... | collective-permute-start | bytes 884744 | tf_op jit(solution)/shard_map/ppermute | solution.py:77
  6.9 13.5 %collective-permute-start.1 = (bf16[4,18,16,128]{3,2,1,0:T(8,128)(2,1)S(1)}, bf16[4,18,16,128]{3,2,1,0:T(8,128)(2,1)S(1)}, u32[]{:S(2)}, u32[]{:S(2)}) collective-permute-start(bf16[4,18,16,128]{3,2,1,0:T(8,128)(2,1)S(1)} %get-tuple-element.51), channel_id=1, source_target_pairs={{0,4},{4,0},{8,12},{12,8},{16,20},{20,16},{24,28},{28,24},{1,5},{5... | collective-permute-start | bytes 884744 | tf_op jit(solution)/shard_map/ppermute | solution.py:77
  8.4 13.3 %collective-permute-start.2 = (bf16[4,18,16,128]{3,2,1,0:T(8,128)(2,1)S(1)}, bf16[4,18,16,128]{3,2,1,0:T(8,128)(2,1)S(1)}, u32[]{:S(2)}, u32[]{:S(2)}) collective-permute-start(bf16[4,18,16,128]{3,2,1,0:T(8,128)(2,1)S(1)} %get-tuple-element.54), channel_id=1, source_target_pairs={{0,4},{4,0},{8,12},{12,8},{16,20},{20,16},{24,28},{28,24},{1,5},{5... | collective-permute-start | bytes 884744 | tf_op jit(solution)/shard_map/ppermute | solution.py:77
  8.9 15.7 %collective-permute-start.3 = (bf16[4,18,16,128]{3,2,1,0:T(8,128)(2,1)S(1)}, bf16[4,18,16,128]{3,2,1,0:T(8,128)(2,1)S(1)}, u32[]{:S(2)}, u32[]{:S(2)}) collective-permute-start(bf16[4,18,16,128]{3,2,1,0:T(8,128)(2,1)S(1)} %get-tuple-element.57), channel_id=1, source_target_pairs={{0,8},{4,12},{8,0},{12,4},{16,24},{20,28},{24,16},{28,20},{1,9},{5... | collective-permute-start | bytes 884744 | tf_op jit(solution)/shard_map/ppermute | solution.py:77
  20.4 15.5 %collective-permute-start.4 = (bf16[4,18,16,128]{3,2,1,0:T(8,128)(2,1)S(1)}, bf16[4,18,16,128]{3,2,1,0:T(8,128)(2,1)S(1)}, u32[]{:S(2)}, u32[]{:S(2)}) collective-permute-start(bf16[4,18,16,128]{3,2,1,0:T(8,128)(2,1)S(1)} %get-tuple-element.59), channel_id=1, source_target_pairs={{0,16},{4,20},{8,24},{12,28},{16,0},{20,4},{24,8},{28,12},{1,17},{... | collective-permute-start | bytes 884744 | tf_op jit(solution)/shard_map/ppermute | solution.py:77
  21.7 15.4 %collective-permute-start.5 = (bf16[4,18,16,128]{3,2,1,0:T(8,128)(2,1)S(1)}, bf16[4,18,16,128]{3,2,1,0:T(8,128)(2,1)S(1)}, u32[]{:S(2)}, u32[]{:S(2)}) collective-permute-start(bf16[4,18,16,128]{3,2,1,0:T(8,128)(2,1)S(1)} %get-tuple-element.61), channel_id=1, source_target_pairs={{0,8},{4,12},{8,0},{12,4},{16,24},{20,28},{24,16},{28,20},{1,9},{5... | collective-permute-start | bytes 884744 | tf_op jit(solution)/shard_map/ppermute | solution.py:77
  24.7 14.2 %collective-permute-start.6 = (bf16[4,18,16,128]{3,2,1,0:T(8,128)(2,1)S(1)}, bf16[4,18,16,128]{3,2,1,0:T(8,128)(2,1)S(1)}, u32[]{:S(2)}, u32[]{:S(2)}) collective-permute-start(bf16[4,18,16,128]{3,2,1,0:T(8,128)(2,1)S(1)} %get-tuple-element.63), channel_id=1, source_target_pairs={{0,4},{4,0},{8,12},{12,8},{16,20},{20,16},{24,28},{28,24},{1,5},{5... | collective-permute-start | bytes 884744 | tf_op jit(solution)/shard_map/ppermute | solution.py:77
  26.2 14.7 %collective-permute-start.7 = (bf16[2,18,16,128]{3,2,1,0:T(8,128)(2,1)S(1)}, bf16[2,18,16,128]{3,2,1,0:T(8,128)(2,1)S(1)}, u32[]{:S(2)}, u32[]{:S(2)}) collective-permute-start(bf16[2,18,16,128]{3,2,1,0:T(8,128)(2,1)S(1)} %get-tuple-element.65), channel_id=1, source_target_pairs={{0,4},{4,0},{8,12},{12,8},{16,20},{20,16},{24,28},{28,24},{1,5},{5... | collective-permute-start | bytes 442376 | tf_op jit(solution)/shard_map/ppermute | solution.py:77
  26.8 18.3 %collective-permute-start.8 = (bf16[2,18,16,128]{3,2,1,0:T(8,128)(2,1)S(1)}, bf16[2,18,16,128]{3,2,1,0:T(8,128)(2,1)S(1)}, u32[]{:S(2)}, u32[]{:S(2)}) collective-permute-start(bf16[2,18,16,128]{3,2,1,0:T(8,128)(2,1)S(1)} %get-tuple-element.66), channel_id=1, source_target_pairs={{0,8},{4,12},{8,0},{12,4},{16,24},{20,28},{24,16},{28,20},{1,9},{5... | collective-permute-start | bytes 442376 | tf_op jit(solution)/shard_map/ppermute | solution.py:77
  35.9 13.6 %collective-permute-start.9 = (bf16[2,18,16,128]{3,2,1,0:T(8,128)(2,1)S(1)}, bf16[2,18,16,128]{3,2,1,0:T(8,128)(2,1)S(1)}, u32[]{:S(2)}, u32[]{:S(2)}) collective-permute-start(bf16[2,18,16,128]{3,2,1,0:T(8,128)(2,1)S(1)} %get-tuple-element.67), channel_id=1, source_target_pairs={{0,12},{4,8},{8,4},{12,0},{16,28},{20,24},{24,20},{28,16},{1,13},{... | collective-permute-start | bytes 442376 | tf_op jit(solution)/shard_map/ppermute | solution.py:77
  35.9 19.0 %copy-start = (bf16[3,3,3,128,256]{4,3,2,1,0:T(8,128)(2,1)S(1)}, bf16[3,3,3,128,256]{4,3,2,1,0:T(8,128)(2,1)}, u32[]{:S(2)}) copy-start(bf16[3,3,3,128,256]{4,3,2,1,0:T(8,128)(2,1)} %refs_0_.7) | copy-start | bytes 5308420
  37.1 17.8 %collective-permute-start.10 = (bf16[4,18,16,128]{3,2,1,0:T(8,128)(2,1)S(1)}, bf16[4,18,16,128]{3,2,1,0:T(8,128)(2,1)S(1)}, u32[]{:S(2)}, u32[]{:S(2)}) collective-permute-start(bf16[4,18,16,128]{3,2,1,0:T(8,128)(2,1)S(1)} %get-tuple-element.70), channel_id=1, source_target_pairs={{0,16},{4,20},{8,24},{12,28},{16,0},{20,4},{24,8},{28,12},{1,17},{... | collective-permute-start | bytes 884744 | tf_op jit(solution)/shard_map/ppermute | solution.py:77
  38.8 23.3 %collective-permute-start.13 = (bf16[4,18,16,128]{3,2,1,0:T(8,128)(2,1)S(1)}, bf16[4,18,16,128]{3,2,1,0:T(8,128)(2,1)S(1)}, u32[]{:S(2)}, u32[]{:S(2)}) collective-permute-start(bf16[4,18,16,128]{3,2,1,0:T(8,128)(2,1)S(1)} %get-tuple-element.76), channel_id=1, source_target_pairs={{0,8},{4,12},{8,0},{12,4},{16,24},{20,28},{24,16},{28,20},{1,9},{5... | collective-permute-start | bytes 884744 | tf_op jit(solution)/shard_map/ppermute | solution.py:77
  50.3 11.8 %collective-permute-start.12 = (bf16[18,64,128]{2,1,0:T(8,128)(2,1)S(1)}, bf16[18,64,128]{2,1,0:T(8,128)(2,1)S(1)}, u32[]{:S(2)}, u32[]{:S(2)}) collective-permute-start(bf16[18,64,128]{2,1,0:T(8,128)(2,1)S(1)} %get-tuple-element.87), channel_id=1, source_target_pairs={{1,0},{2,1},{3,2},{5,4},{6,5},{7,6},{9,8},{10,9},{11,10},{13,12},{... | collective-permute-start | bytes 884744 | tf_op jit(solution)/shard_map/ppermute | solution.py:357
  51.6 10.5 %collective-permute-start.11 = (bf16[18,64,128]{2,1,0:T(8,128)(2,1)S(1)}, bf16[18,64,128]{2,1,0:T(8,128)(2,1)S(1)}, u32[]{:S(2)}, u32[]{:S(2)}) collective-permute-start(bf16[18,64,128]{2,1,0:T(8,128)(2,1)S(1)} %get-tuple-element.88), channel_id=1, source_target_pairs={{0,1},{1,2},{2,3},{4,5},{5,6},{6,7},{8,9},{9,10},{10,11},{12,13},{... | collective-permute-start | bytes 884744 | tf_op jit(solution)/shard_map/ppermute | solution.py:356
  54.9 14.8 %collective-permute-start.14 = (bf16[4,18,16,128]{3,2,1,0:T(8,128)(2,1)S(1)}, bf16[4,18,16,128]{3,2,1,0:T(8,128)(2,1)S(1)}, u32[]{:S(2)}, u32[]{:S(2)}) collective-permute-start(bf16[4,18,16,128]{3,2,1,0:T(8,128)(2,1)S(1)} %get-tuple-element.81), channel_id=1, source_target_pairs={{0,16},{4,20},{8,24},{12,28},{16,0},{20,4},{24,8},{28,12},{1,17},{... | collective-permute-start | bytes 884744 | tf_op jit(solution)/shard_map/ppermute | solution.py:77
  69.6 17.3 %copy-start.2 = (f32[256]{0:T(256)S(1)}, f32[256]{0:T(256)}, u32[]{:S(2)}) copy-start(f32[256]{0:T(256)} %param.6) | copy-start | bytes 3076
  69.6 17.3 %copy-start.3 = (f32[256]{0:T(256)S(1)}, f32[256]{0:T(256)}, u32[]{:S(2)}) copy-start(f32[256]{0:T(256)} %param.7) | copy-start | bytes 3076

commit v3 on v2

--- a/solution.py
+++ b/solution.py
@@ -54,7 +54,7 @@
     masks = [0]
     for bit in bits:
         masks += [m | 1 << bit for m in masks]
-    return masks[1:]
+    return masks[:0:-1]
 
 
 class Trip:
@@ -215,20 +215,27 @@
     return ref[row].reshape(-1, ref.shape[-1])
 
 
-def stage_a(trip, me_ref, w_ref, outer, *refs):
-    *held, part0, part1, part2, wide, blocks = refs
+def stage_o(me_ref, w_ref, outer, part0, part1):
+    keep(taps(w_ref, [(outer, 0, 1)]), part0, 0)
+    keep(taps(w_ref, [(outer, 1, 1)]), part0, 1)
+    keep(taps(w_ref, [(outer, 0, 0)]), part1, 0)
+    keep(taps(w_ref, [(outer, 1, 2)]), part1, 1)
+
+
+def stage_a(trip, me_ref, w_ref, part1, *refs):
+    *held, next1, part2, part3, wide, blocks = refs
     trip.gather(me_ref[0], held, blocks)
     wavelet_rows(blocks, wide)
-    keep(taps(w_ref, [(outer, 0, 1), (wide, 0, 2)]), part0, 0)
-    keep(taps(w_ref, [(wide, 1, 0), (outer, 1, 1)]), part0, 1)
-    keep(taps(w_ref, [(outer, 0, 0), (wide, 0, 1)]), part1, 0)
-    keep(taps(w_ref, [(wide, 1, 1), (outer, 1, 2)]), part1, 1)
-    keep(taps(w_ref, [(wide, 0, 0)]), part2, 0)
-    keep(taps(w_ref, [(wide, 1, 2)]), part2, 1)
+    keep(taps(w_ref, [(wide, 0, 2)], flat(part1, 0)), next1, 0)
+    keep(taps(w_ref, [(wide, 1, 0)], flat(part1, 1)), next1, 1)
+    keep(taps(w_ref, [(wide, 0, 1)]), part2, 0)
+    keep(taps(w_ref, [(wide, 1, 1)]), part2, 1)
+    keep(taps(w_ref, [(wide, 0, 0)]), part3, 0)
+    keep(taps(w_ref, [(wide, 1, 2)]), part3, 1)
 
 
 def stage_b(trip, me_ref, w_ref, above, below, part0, part1, part2, *refs):
-    *held, done0, done1, next2, part3, sums, wide, halo, blocks = refs
+    *held, done0, done1, next2, sums, wide, halo, blocks = refs
     trip.gather(me_ref[0], held, blocks)
     wavelet_rows(blocks, wide)
 
@@ -238,14 +245,25 @@
         return 0
 
     lax.fori_loop(0, above.shape[0], column, 0)
-    finish(taps(w_ref, [(wide, 0, 2)], flat(part1, 0)), done1, sums.at[2:4], 0)
-    finish(taps(w_ref, [(wide, 1, 0)], flat(part1, 1)), done1, sums.at[2:4], 1)
-    keep(taps(w_ref, [(wide, 0, 1)], flat(part2, 0)), next2, 0)
-    keep(taps(w_ref, [(wide, 1, 1)], flat(part2, 1)), next2, 1)
-    keep(taps(w_ref, [(wide, 0, 0)]), part3, 0)
-    keep(taps(w_ref, [(wide, 1, 2)]), part3, 1)
-    finish(taps(w_ref, [(halo, 0, 0)], flat(part0, 0)), done0, sums, 0)
-    finish(taps(w_ref, [(halo, 1, 2)], flat(part0, 1)), done0, sums, 1)
+    finish(taps(w_ref, [(halo, 0, 0), (wide, 0, 2)], flat(part0, 0)), done0, sums, 0)
+    finish(taps(w_ref, [(wide, 1, 0), (halo, 1, 2)], flat(part0, 1)), done0, sums, 1)
+    finish(taps(w_ref, [(wide, 0, 1)], flat(part1, 0)), done1, sums.at[2:4], 0)
+    finish(taps(w_ref, [(wide, 1, 1)], flat(part1, 1)), done1, sums.at[2:4], 1)
+    keep(taps(w_ref, [(wide, 0, 0)], flat(part2, 0)), next2, 0)
+    keep(taps(w_ref, [(wide, 1, 2)], flat(part2, 1)), next2, 1)
+
+
+def over_group(values, size):
+    lanes = values.shape[-1]
+    lane = lax.broadcasted_iota(jnp.int32, values.shape, values.ndim - 1)
+    step = 1
+    while step < size:
+        axis = values.ndim - 1
+        down = pltpu.roll(values, step, axis)
+        up = pltpu.roll(values, lanes - step, axis)
+        values = values + jnp.where((lane & step) != 0, down, up)
+        step *= 2
+    return values
 
 
 def stage_c(trip, me_ref, w_ref, part2, part3, earlier, *refs):
@@ -262,22 +280,18 @@
     mean = sum(r[0:1] for r in rows) * (1.0 / len(rows))
     squares = sum(r[1:2] + entries * (r[0:1] - mean) * (r[0:1] - mean) for r in rows)
     lanes = message.shape[-1]
-    parts = [v[:, c : c + lanes] for v in (mean, squares) for c in range(0, mean.shape[1], lanes)]
-    packed = jnp.concatenate(parts + [jnp.zeros((8 - len(parts), lanes), F32)], 0)
+    halves = range(0, mean.shape[1], lanes)
+    mean = jnp.concatenate([mean[:, c : c + lanes] for c in halves], 0)
+    squares = jnp.concatenate([squares[:, c : c + lanes] for c in halves], 0)
+    size = mean.size // GROUPS
+    group_mean = over_group(mean, size) * (1.0 / size)
+    apart = mean - group_mean
+    group = over_group(squares + (entries * len(rows)) * apart * apart, size)
+    slot = lax.broadcasted_iota(jnp.int32, (1, lanes), 1) % size
+    packed = jnp.zeros((1, lanes), F32)
+    for i, value in enumerate([group_mean[0:1], group_mean[1:2], group[0:1], group[1:2]]):
+        packed = jnp.where(slot == i, value, packed)
     message[...] = jnp.broadcast_to(packed[None], message.shape)
-
-
-def over_group(values, size):
-    lanes = values.shape[-1]
-    lane = lax.broadcasted_iota(jnp.int32, values.shape, values.ndim - 1)
-    step = 1
-    while step < size:
-        axis = values.ndim - 1
-        down = pltpu.roll(values, step, axis)
-        up = pltpu.roll(values, lanes - step, axis)
-        values = values + jnp.where((lane & step) != 0, down, up)
-        step *= 2
-    return values
 
 
 def norm_body(entries, size, all_ref, gain_ref, bias_ref, *refs):
@@ -286,15 +300,19 @@
     @pl.when(pl.program_id(0) == 0)
     def _():
         devices = all_ref.shape[0]
+        given = all_ref[:, 0]
         half = gain_ref.shape[0]
-        means = all_ref[:, 0:half]
-        mean = jnp.sum(means, 0) * (1.0 / devices)
-        apart = means - mean[None]
-        squares = jnp.sum(all_ref[:, half : 2 * half] + entries * apart * apart, 0)
-        group_mean = over_group(mean, size) * (1.0 / size)
-        apart = mean - group_mean
-        group = over_group(squares + (entries * devices) * apart * apart, size)
-        variance = group * (1.0 / (entries * devices * size))
+        total = jnp.sum(given, 0, keepdims=True)
+        apart = given - total * (1.0 / devices)
+        spread = jnp.sum(apart * apart, 0, keepdims=True)
+        slot = lax.broadcasted_iota(jnp.int32, total.shape, 1) % size
+
+        def of(values, i):
+            return over_group(jnp.where(slot == i, values, 0.0), size)
+
+        group_mean = jnp.concatenate([of(total, p) for p in range(half)], 0) * (1.0 / devices)
+        squares = [of(total, half + p) + (entries * size) * of(spread, p) for p in range(half)]
+        variance = jnp.concatenate(squares, 0) * (1.0 / (entries * devices * size))
         scale = (0.5 * gain_ref[...]) / jnp.sqrt(variance + 1e-05)
         for p in range(half):
             lanes = slice(p * scale.shape[1], (p + 1) * scale.shape[1])
@@ -307,8 +325,8 @@
     height = 2 * len(rows)
     for h in range(height):
         ref, place = (rows[h], 0) if h < len(rows) else (rows[height - 1 - h], 1)
-        for w in range(ref.shape[1]):
-            half_v = (ref[place, w] - mean) * scale + bias
+        for w in range(2 * out.shape[1]):
+            half_v = (ref[place, pl.program_id(0) * (2 * out.shape[1]) + w] - mean) * scale + bias
             value = half_v + half_v * jnp.tanh(half_v)
             lanes = (h % 2 * 2 + w % 2) * channels
             out[h // 2, w // 2, :, lanes : lanes + channels] = value.astype(BF16)
@@ -328,11 +346,11 @@
     top, rest = bits - 1, list(range(1, bits - 1))
     outer_trip = Trip((0, 7), [[top], [0] + rest])
     third_trip = Trip((2, 5), [[0], [top], rest])
-    second_trip = Trip((1, 6), [[0], rest, [top]])
-    inner_trip = Trip((3, 4), [rest, [0], [top]])
+    second_trip = Trip((1, 6), [rest, [0], [top]])
+    inner_trip = Trip((3, 4), [[0], rest + [top]])
     trips = [outer_trip, third_trip, second_trip, inner_trip]
     me = part_rows(me, video, trips)
-    for trip in (outer_trip, third_trip, second_trip, inner_trip, third_trip, second_trip, inner_trip):
+    for trip in (outer_trip, third_trip, second_trip, third_trip, second_trip):
         me = trip.step(me)
 
     def blocks(rows):
@@ -355,23 +373,25 @@
     up = [(i + 1, i) for i in range(strips - 1)]
     above = lax.ppermute(plain[1], "rows", down)
     below = lax.ppermute(plain[0], "rows", up)
-    me, part0, part1, part2 = on_core(
-        functools.partial(stage_a, second_trip),
+    me, part0, part1 = on_core(stage_o, [row_pair, row_pair], me, [conv_weight, outer])
+    me = inner_trip.step(me)
+    me, part1, part2, part3 = on_core(
+        functools.partial(stage_a, third_trip),
         [row_pair, row_pair, row_pair],
         me,
-        [conv_weight, outer] + second_trip.arrays,
+        [conv_weight, part1] + third_trip.arrays,
         [pltpu.VMEM(wide(2), BF16), blocks(2)],
     )
-    me, done0, done1, part2, part3, sums = on_core(
-        functools.partial(stage_b, third_trip),
-        [row_pair, row_pair, row_pair, row_pair, four_sums],
+    me, done0, done1, part2, sums = on_core(
+        functools.partial(stage_b, second_trip),
+        [row_pair, row_pair, row_pair, four_sums],
         me,
-        [conv_weight, above, below, part0, part1, part2] + third_trip.arrays,
+        [conv_weight, above, below, part0, part1, part2] + second_trip.arrays,
         [pltpu.VMEM(wide(2), BF16), pltpu.VMEM(wide(2), BF16), blocks(2)],
     )
     me, done2, done3, message = on_core(
         functools.partial(stage_c, inner_trip),
-        [row_pair, row_pair, shape((devices, 8, 128), F32)],
+        [row_pair, row_pair, shape((devices, 1, 128), F32)],
         me,
         [conv_weight, part2, part3, sums] + inner_trip.arrays,
         [pltpu.VMEM((4, 2, outputs), F32), pltpu.VMEM(wide(2), BF16), blocks(2)],
@@ -380,12 +400,11 @@
 
     steps = columns // 2 // min(2, columns // 2)
     block = columns // steps
-    rows_spec = pl.BlockSpec((2, block, time, outputs), lambda g: (0, g, 0, 0))
     return pl.pallas_call(
         functools.partial(norm_body, float(height * columns * time), outputs // GROUPS),
         grid=(steps,),
         out_shape=shape((height // 2, columns // 2, time, 4 * outputs), BF16),
-        in_specs=[VMEM, VMEM, VMEM] + [rows_spec] * 4,
+        in_specs=[VMEM] * 7,
         out_specs=pl.BlockSpec((height // 2, block // 2, time, 4 * outputs), lambda g: (0, g, 0, 0)),
         scratch_shapes=[pltpu.VMEM((8, outputs), F32)],
         compiler_params=pltpu.CompilerParams(vmem_limit_bytes=40 * MIB),

time: 91.4 us -> 86.3 us (0.944)
  waiting for transfers between devices: 30 us -> 21.4 us
  starting transfers between devices: 21.3 us -> 24.9 us
    ppermute x13 -> x14, waiting for transfers between devices: 30 us -> 21.4 us  [swap(): got = lax.ppermute(block, 'tm', [(i, i ^ mask) for i in range(self.count)])]
    ppermute x13 -> x14, starting transfers between devices: 16.7 us -> 20.4 us  [swap(): got = lax.ppermute(block, 'tm', [(i, i ^ mask) for i in range(self.count)])]
  transfers between devices with their start and end apart: 15 -> 16, of which waited for: 7 -> 5; matrix products, arithmetic and copies ran while one was open for 0% -> 0% of each run, Pallas kernels for 17% -> 18%
where the time goes in v3:
time: 86.3 us; the launch traced here: 86.1 us
  Pallas kernels  26 us (30%)
  starting transfers between devices  24.9 us (29%)
  waiting for transfers between devices  21.4 us (25%)
  blocking collectives  11.9 us (14%)
  local copies, waits for them, and re-layouts  1.65 us (2%)
    pallas_call x12, Pallas kernels, on_core(): pl.pallas_call(handing_on(body, len(arrays)), out_shape=[MARK] + outs, in...  22.5 us
    ppermute x14, waiting for transfers between devices, swap(): got = lax.ppermute(block, 'tm', [(i, i ^ mask) for i in range(self.count)])  21.4 us
    ppermute x14, starting transfers between devices, swap(): got = lax.ppermute(block, 'tm', [(i, i ^ mask) for i in range(self.count)])  20.4 us
    all_to_all x1, blocking collectives, per_device(): messages = lax.all_to_all(message, ('tm', 'rows'), 0, 0, tiled=True)  11.9 us
    pallas_call x1, Pallas kernels, per_device(): pl.pallas_call(functools.partial(norm_body, float(height * columns * time...  3.57 us
    ppermute x1, starting transfers between devices, per_device(): above = lax.ppermute(plain[1], 'rows', down)  3.23 us
  transfers between devices with their start and end apart: 16, of which 5 were waited for; matrix products, arithmetic and copies ran while one was open for 0% of the time, Pallas kernels for 18%

profile of v3, /device:TPU:0, one launch (start us, length us, event | category | flops | bytes accessed | tf_op | source)
XLA Modules:
  0.0 86.1 jit_solution(17381336270715132269)
XLA Ops:
  0.0 0.0 copy-start.1
  0.0 1.6 %copy-done.1 = bf16[8,8,128,128]{3,2,1,0:T(8,128)(2,1)S(1)} copy-done((bf16[8,8,128,128]{3,2,1,0:T(8,128)(2,1)S(1)}, bf16[8,8,128,128]{3,2,1,0:T(8,128)(2,1)}, u32[]{:S(2)}) %copy-start.1) | copy-done | bytes 2097176
  1.6 1.2 %shard_map.46 = (f32[8,128]{1,0:T(8,128)S(1)}, bf16[4,18,16,128]{3,2,1,0:T(8,128)(2,1)S(1)}, bf16[4,18,16,128]{3,2,1,0:T(8,128)(2,1)S(1)}, bf16[4,18,16,128]{3,2...) custom-call(s32[1]{0:T(128)} %bitcast.me_ref, ...), custom_call_target="tpu_custom_call" | custom-call | tf_op jit(solution)/shard_map/pallas_call | solution.py:36
  2.8 4.1 %collective-permute-start = (bf16[4,18,16,128]{3,2,1,0:T(8,128)(2,1)S(1)}, bf16[4,18,16,128]{3,2,1,0:T(8,128)(2,1)S(1)}, u32[]{:S(2)}, u32[]{:S(2)}) collective-permute-start(bf16[4,18,16,128]{3,2,1,0:T(8,128)(2,1)S(1)} %get-tuple-element.50), channel_id=1, source_target_pairs={{0,16},{4,20},{8,24},{12,28},{16,0},{20,4},{24,8},{28,12},{1,17},{... | collective-permute-start | bytes 884744 | tf_op jit(solution)/shard_map/ppermute | solution.py:77
  6.9 1.5 %collective-permute-start.1 = (bf16[4,18,16,128]{3,2,1,0:T(8,128)(2,1)S(1)}, bf16[4,18,16,128]{3,2,1,0:T(8,128)(2,1)S(1)}, u32[]{:S(2)}, u32[]{:S(2)}) collective-permute-start(bf16[4,18,16,128]{3,2,1,0:T(8,128)(2,1)S(1)} %get-tuple-element.53), channel_id=1, source_target_pairs={{0,4},{4,0},{8,12},{12,8},{16,20},{20,16},{24,28},{28,24},{1,5},{5... | collective-permute-start | bytes 884744 | tf_op jit(solution)/shard_map/ppermute | solution.py:77
  8.4 1.6 %collective-permute-start.2 = (bf16[4,18,16,128]{3,2,1,0:T(8,128)(2,1)S(1)}, bf16[4,18,16,128]{3,2,1,0:T(8,128)(2,1)S(1)}, u32[]{:S(2)}, u32[]{:S(2)}) collective-permute-start(bf16[4,18,16,128]{3,2,1,0:T(8,128)(2,1)S(1)} %get-tuple-element.56), channel_id=1, source_target_pairs={{0,8},{4,12},{8,0},{12,4},{16,24},{20,28},{24,16},{28,20},{1,9},{5... | collective-permute-start | bytes 884744 | tf_op jit(solution)/shard_map/ppermute | solution.py:77
  9.9 10.4 %collective-permute-done.refs_1_ = bf16[4,18,16,128]{3,2,1,0:T(8,128)(2,1)S(1)} collective-permute-done((bf16[4,18,16,128]{3,2,1,0:T(8,128)(2,1)S(1)}, bf16[4,18,16,128]{3,2,1,0:T(8,128)(2,1)S(1)}, u32[]{:S(2)}, u32[]{:S(2)}) %collective-permute-start) | collective-permute-done | bytes 294944 | tf_op jit(solution)/shard_map/ppermute | solution.py:77
  20.3 0.0 collective-permute-done.1.refs_1_.refs_3_
  20.4 0.1 collective-permute-start.3
  20.5 1.3 %collective-permute-done.2.refs_1_.refs_7_ = bf16[4,18,16,128]{3,2,1,0:T(8,128)(2,1)S(1)} collective-permute-done((bf16[4,18,16,128]{3,2,1,0:T(8,128)(2,1)S(1)}, bf16[4,18,16,128]{3,2,1,0:T(8,128)(2,1)S(1)}, u32[]{:S(2)}, u32[]{:S(2)}) %collective-permute-start.2) | collective-permute-done | bytes 294944 | tf_op jit(solution)/shard_map/ppermute | solution.py:77
  21.7 0.0 copy-start
  21.8 0.6 collective-permute-start.4
  22.4 3.7 %collective-permute-start.5 = (bf16[2,18,16,128]{3,2,1,0:T(8,128)(2,1)S(1)}, bf16[2,18,16,128]{3,2,1,0:T(8,128)(2,1)S(1)}, u32[]{:S(2)}, u32[]{:S(2)}) collective-permute-start(bf16[2,18,16,128]{3,2,1,0:T(8,128)(2,1)S(1)} %get-tuple-element.62), channel_id=1, source_target_pairs={{0,12},{4,8},{8,4},{12,0},{16,28},{20,24},{24,20},{28,16},{1,13},{... | collective-permute-start | bytes 442376 | tf_op jit(solution)/shard_map/ppermute | solution.py:77
  26.1 0.0 collective-permute-start.6
  26.1 1.4 %collective-permute-start.7 = (bf16[2,18,16,128]{3,2,1,0:T(8,128)(2,1)S(1)}, bf16[2,18,16,128]{3,2,1,0:T(8,128)(2,1)S(1)}, u32[]{:S(2)}, u32[]{:S(2)}) collective-permute-start(bf16[2,18,16,128]{3,2,1,0:T(8,128)(2,1)S(1)} %get-tuple-element.64), channel_id=1, source_target_pairs={{0,4},{4,0},{8,12},{12,8},{16,20},{20,16},{24,28},{28,24},{1,5},{5... | collective-permute-start | bytes 442376 | tf_op jit(solution)/shard_map/ppermute | solution.py:77
  27.5 8.4 %collective-permute-done.3.refs_2_.refs_4_ = bf16[4,18,16,128]{3,2,1,0:T(8,128)(2,1)S(1)} collective-permute-done((bf16[4,18,16,128]{3,2,1,0:T(8,128)(2,1)S(1)}, bf16[4,18,16,128]{3,2,1,0:T(8,128)(2,1)S(1)}, u32[]{:S(2)}, u32[]{:S(2)}) %collective-permute-start.3) | collective-permute-done | bytes 294944 | tf_op jit(solution)/shard_map/ppermute | solution.py:77
  35.9 1.2 %collective-permute-start.8 = (bf16[4,18,16,128]{3,2,1,0:T(8,128)(2,1)S(1)}, bf16[4,18,16,128]{3,2,1,0:T(8,128)(2,1)S(1)}, u32[]{:S(2)}, u32[]{:S(2)}) collective-permute-start(bf16[4,18,16,128]{3,2,1,0:T(8,128)(2,1)S(1)} %get-tuple-element.69), channel_id=1, source_target_pairs={{0,4},{4,0},{8,12},{12,8},{16,20},{20,16},{24,28},{28,24},{1,5},{5... | collective-permute-start | bytes 884744 | tf_op jit(solution)/shard_map/ppermute | solution.py:77
  37.2 0.0 collective-permute-done.4.refs_2_.refs_8_
  37.2 0.1 collective-permute-start.12
  37.3 0.0 collective-permute-done.5.refs_2_
  37.3 1.7 %collective-permute-start.9 = (bf16[4,18,16,128]{3,2,1,0:T(8,128)(2,1)S(1)}, bf16[4,18,16,128]{3,2,1,0:T(8,128)(2,1)S(1)}, u32[]{:S(2)}, u32[]{:S(2)}) collective-permute-start(bf16[4,18,16,128]{3,2,1,0:T(8,128)(2,1)S(1)} %get-tuple-element.72), channel_id=1, source_target_pairs={{0,8},{4,12},{8,0},{12,4},{16,24},{20,28},{24,16},{28,20},{1,9},{5... | collective-permute-start | bytes 884744 | tf_op jit(solution)/shard_map/ppermute | solution.py:77
  39.0 0.0 collective-permute-done.6.refs_3_
  39.0 0.0 collective-permute-done.7.refs_4_
  39.0 0.7 shard_map.52
  39.8 1.3 %collective-permute-start.11 = (bf16[18,64,128]{2,1,0:T(8,128)(2,1)S(1)}, bf16[18,64,128]{2,1,0:T(8,128)(2,1)S(1)}, u32[]{:S(2)}, u32[]{:S(2)}) collective-permute-start(bf16[18,64,128]{2,1,0:T(8,128)(2,1)S(1)} %get-tuple-element.91), channel_id=1, source_target_pairs={{1,0},{2,1},{3,2},{5,4},{6,5},{7,6},{9,8},{10,9},{11,10},{13,12},{... | collective-permute-start | bytes 884744 | tf_op jit(solution)/shard_map/ppermute | solution.py:375
  41.1 3.2 %collective-permute-start.10 = (bf16[18,64,128]{2,1,0:T(8,128)(2,1)S(1)}, bf16[18,64,128]{2,1,0:T(8,128)(2,1)S(1)}, u32[]{:S(2)}, u32[]{:S(2)}) collective-permute-start(bf16[18,64,128]{2,1,0:T(8,128)(2,1)S(1)} %get-tuple-element.92), channel_id=1, source_target_pairs={{0,1},{1,2},{2,3},{4,5},{5,6},{6,7},{8,9},{9,10},{10,11},{12,13},{... | collective-permute-start | bytes 884744 | tf_op jit(solution)/shard_map/ppermute | solution.py:374
  44.4 0.0 copy-done
  44.4 2.9 %shard_map.53 = (f32[8,128]{1,0:T(8,128)S(1)}, f32[2,16,64,256]{3,2,1,0:T(8,128)S(1)}, f32[2,16,64,256]{3,2,1,0:T(8,128)S(1)}) custom-call(s32[1]{0:T(128)} %bitcast.me_ref, f32[8,128]{1,0:T(8,128)S(1)} %get-tuple-element.65.before, bf16[3,3,3,128,256]{4,3,2,1,0:T(8,128)(2,1)S(1)} %copy-done, bf16[2,18,64,384]{3,2,1,0:T(8,128)(2,1)S(1)} %get-tuple-element.66.refs_1_), custom_call_target="tpu_custom_call" | custom-call | tf_op jit(solution)/shard_map/pallas_call | solution.py:36
  47.3 0.0 collective-permute-done.8.refs_1_.refs_5_
  47.3 2.7 %collective-permute-start.13 = (bf16[2,18,16,128]{3,2,1,0:T(8,128)(2,1)S(1)}, bf16[2,18,16,128]{3,2,1,0:T(8,128)(2,1)S(1)}, u32[]{:S(2)}, u32[]{:S(2)}) collective-permute-start(bf16[2,18,16,128]{3,2,1,0:T(8,128)(2,1)S(1)} %get-tuple-element.83), channel_id=1, source_target_pairs={{0,24},{4,28},{8,16},{12,20},{16,8},{20,12},{24,0},{28,4},{1,25},{... | collective-permute-start | bytes 442376 | tf_op jit(solution)/shard_map/ppermute | solution.py:77
  50.0 1.3 %collective-permute-done.12.refs_9_ = bf16[4,18,16,128]{3,2,1,0:T(8,128)(2,1)S(1)} collective-permute-done((bf16[4,18,16,128]{3,2,1,0:T(8,128)(2,1)S(1)}, bf16[4,18,16,128]{3,2,1,0:T(8,128)(2,1)S(1)}, u32[]{:S(2)}, u32[]{:S(2)}) %collective-permute-start.12) | collective-permute-done | bytes 294944 | tf_op jit(solution)/shard_map/ppermute | solution.py:77
  51.3 0.0 collective-permute-start.14
  51.3 0.1 collective-permute-done.9.refs_5_
  51.4 1.7 %collective-permute-start.15 = (bf16[2,18,16,128]{3,2,1,0:T(8,128)(2,1)S(1)}, bf16[2,18,16,128]{3,2,1,0:T(8,128)(2,1)S(1)}, u32[]{:S(2)}, u32[]{:S(2)}) collective-permute-start(bf16[2,18,16,128]{3,2,1,0:T(8,128)(2,1)S(1)} %get-tuple-element.85), channel_id=1, source_target_pairs={{0,8},{4,12},{8,0},{12,4},{16,24},{20,28},{24,16},{28,20},{1,9},{5... | collective-permute-start | bytes 442376 | tf_op jit(solution)/shard_map/ppermute | solution.py:77
  53.0 5.0 %shard_map.55 = (f32[8,128]{1,0:T(8,128)S(1)}, f32[2,16,64,256]{3,2,1,0:T(8,128)S(1)}, f32[2,16,64,256]{3,2,1,0:T(8,128)S(1)}, f32[2,16,64,256]{3,2,1,0:T(8,128)S(1)}) custom-call(s32[1]{0:T(128)} %bitcast.me_ref, f32[8,128]{1,0:T(8,128)S(1)} %get-tuple-element.70.before, bf16[3,3,3,128,256]{4,3,2,1,0:T(8,128)(2,1)S(1)} %copy-done, ...), custom_call_target="tpu_custom_call" | custom-call | tf_op jit(solution)/shard_map/pallas_call | solution.py:36
  58.0 0.0 collective-permute-done.11.refs_2_
  58.1 0.0 collective-permute-done.10.refs_1_
  58.1 6.9 %shard_map.56 = (f32[8,128]{1,0:T(8,128)S(1)}, f32[2,16,64,256]{3,2,1,0:T(8,128)S(1)}, f32[2,16,64,256]{3,2,1,0:T(8,128)S(1)}, f32[2,16,64,256]{3,2,1,0:T(8,128)S(1)}, f32[4,2,256]{2,1,0:T(2,128)S(1)}) custom-call(s32[1]{0:T(128)} %bitcast.me_ref, f32[8,128]{1,0:T(8,128)S(1)} %get-tuple-element.73.before, bf16[3,3,3,128,256]{4,3,2,1,0:T(8,128)(2,1)S(1)} %copy-done, ...), custom_call_target="tpu_custom_call" | custom-call | tf_op jit(solution)/shard_map/pallas_call | solution.py:36
  64.9 0.0 collective-permute-done.13.refs_6_
  64.9 0.0 collective-permute-done.14.refs_7_
  65.0 0.0 collective-permute-done.15.refs_8_
  65.0 0.0 copy-start.2
  65.0 0.0 copy-start.3
  65.0 5.7 %shard_map.57 = (f32[8,128]{1,0:T(8,128)}, f32[2,16,64,256]{3,2,1,0:T(8,128)S(1)}, f32[2,16,64,256]{3,2,1,0:T(8,128)S(1)}, f32[32,1,128]{2,1,0:T(1,128)S(1)}) custom-call(s32[1]{0:T(128)} %bitcast.me_ref, f32[8,128]{1,0:T(8,128)S(1)} %get-tuple-element.79.before, bf16[3,3,3,128,256]{4,3,2,1,0:T(8,128)(2,1)S(1)} %copy-done, ...), custom_call_target="tpu_custom_call" | custom-call | tf_op jit(solution)/shard_map/pallas_call | solution.py:36
  70.7 11.9 %all_to_all.5.all_ref = f32[32,1,128]{2,1,0:T(1,128)S(1)} all-to-all(f32[32,1,128]{2,1,0:T(1,128)S(1)} %get-tuple-element.86), channel_id=1, replica_groups=mesh['tm'=8,'rows'=4] {'tm','rows'}, dimensions={0} | all-to-all | bytes 32768 | tf_op jit(solution)/shard_map/all_to_all | solution.py:399
  82.5 0.0 copy-done.2
  82.5 0.0 copy-done.3
  82.5 3.6 %shard_map.58 = bf16[4,8,64,1024]{3,2,1,0:T(8,128)(2,1)} custom-call(f32[32,1,128]{2,1,0:T(1,128)S(1)} %all_to_all.5.all_ref, f32[2,128]{1,0:T(2,128)S(1)} %bitcast.7, f32[2,128]{1,0:T(2,128)S(1)} %bitcast.8, f32[2,16,64,256]{3,2,1,0:T(8,128)S(1)} %get-tuple-element.87.refs_0_, f32[2,16,64,256]{3,2,1,0:T(8,128)S(1)} %get-tuple-element.88.refs_1_, ...), custom_call_target="tpu_custom_call" | custom-call | tf_op jit(solution)/shard_map/pallas_call | solution.py:403
  (8 shorter events, 0.2 us)
Async XLA Ops:
  0.0 1.6 %copy-start.1 = (bf16[8,8,128,128]{3,2,1,0:T(8,128)(2,1)S(1)}, bf16[8,8,128,128]{3,2,1,0:T(8,128)(2,1)}, u32[]{:S(2)}) copy-start(bf16[8,8,128,128]{3,2,1,0:T(8,128)(2,1)} %refs_0_.5) | copy-start | bytes 6291460
  2.8 17.5 %collective-permute-start = (bf16[4,18,16,128]{3,2,1,0:T(8,128)(2,1)S(1)}, bf16[4,18,16,128]{3,2,1,0:T(8,128)(2,1)S(1)}, u32[]{:S(2)}, u32[]{:S(2)}) collective-permute-start(bf16[4,18,16,128]{3,2,1,0:T(8,128)(2,1)S(1)} %get-tuple-element.50), channel_id=1, source_target_pairs={{0,16},{4,20},{8,24},{12,28},{16,0},{20,4},{24,8},{28,12},{1,17},{... | collective-permute-start | bytes 884744 | tf_op jit(solution)/shard_map/ppermute | solution.py:77
  6.9 13.5 %collective-permute-start.1 = (bf16[4,18,16,128]{3,2,1,0:T(8,128)(2,1)S(1)}, bf16[4,18,16,128]{3,2,1,0:T(8,128)(2,1)S(1)}, u32[]{:S(2)}, u32[]{:S(2)}) collective-permute-start(bf16[4,18,16,128]{3,2,1,0:T(8,128)(2,1)S(1)} %get-tuple-element.53), channel_id=1, source_target_pairs={{0,4},{4,0},{8,12},{12,8},{16,20},{20,16},{24,28},{28,24},{1,5},{5... | collective-permute-start | bytes 884744 | tf_op jit(solution)/shard_map/ppermute | solution.py:77
  8.4 13.3 %collective-permute-start.2 = (bf16[4,18,16,128]{3,2,1,0:T(8,128)(2,1)S(1)}, bf16[4,18,16,128]{3,2,1,0:T(8,128)(2,1)S(1)}, u32[]{:S(2)}, u32[]{:S(2)}) collective-permute-start(bf16[4,18,16,128]{3,2,1,0:T(8,128)(2,1)S(1)} %get-tuple-element.56), channel_id=1, source_target_pairs={{0,8},{4,12},{8,0},{12,4},{16,24},{20,28},{24,16},{28,20},{1,9},{5... | collective-permute-start | bytes 884744 | tf_op jit(solution)/shard_map/ppermute | solution.py:77
  20.4 15.5 %collective-permute-start.3 = (bf16[4,18,16,128]{3,2,1,0:T(8,128)(2,1)S(1)}, bf16[4,18,16,128]{3,2,1,0:T(8,128)(2,1)S(1)}, u32[]{:S(2)}, u32[]{:S(2)}) collective-permute-start(bf16[4,18,16,128]{3,2,1,0:T(8,128)(2,1)S(1)} %get-tuple-element.58), channel_id=1, source_target_pairs={{0,16},{4,20},{8,24},{12,28},{16,0},{20,4},{24,8},{28,12},{1,17},{... | collective-permute-start | bytes 884744 | tf_op jit(solution)/shard_map/ppermute | solution.py:77
  21.7 22.6 %copy-start = (bf16[3,3,3,128,256]{4,3,2,1,0:T(8,128)(2,1)S(1)}, bf16[3,3,3,128,256]{4,3,2,1,0:T(8,128)(2,1)}, u32[]{:S(2)}) copy-start(bf16[3,3,3,128,256]{4,3,2,1,0:T(8,128)(2,1)} %refs_0_.9) | copy-start | bytes 5308420
  21.8 15.4 %collective-permute-start.4 = (bf16[4,18,16,128]{3,2,1,0:T(8,128)(2,1)S(1)}, bf16[4,18,16,128]{3,2,1,0:T(8,128)(2,1)S(1)}, u32[]{:S(2)}, u32[]{:S(2)}) collective-permute-start(bf16[4,18,16,128]{3,2,1,0:T(8,128)(2,1)S(1)} %get-tuple-element.60), channel_id=1, source_target_pairs={{0,4},{4,0},{8,12},{12,8},{16,20},{20,16},{24,28},{28,24},{1,5},{5... | collective-permute-start | bytes 884744 | tf_op jit(solution)/shard_map/ppermute | solution.py:77
  22.4 14.9 %collective-permute-start.5 = (bf16[2,18,16,128]{3,2,1,0:T(8,128)(2,1)S(1)}, bf16[2,18,16,128]{3,2,1,0:T(8,128)(2,1)S(1)}, u32[]{:S(2)}, u32[]{:S(2)}) collective-permute-start(bf16[2,18,16,128]{3,2,1,0:T(8,128)(2,1)S(1)} %get-tuple-element.62), channel_id=1, source_target_pairs={{0,12},{4,8},{8,4},{12,0},{16,28},{20,24},{24,20},{28,16},{1,13},{... | collective-permute-start | bytes 442376 | tf_op jit(solution)/shard_map/ppermute | solution.py:77
  26.1 12.9 %collective-permute-start.6 = (bf16[2,18,16,128]{3,2,1,0:T(8,128)(2,1)S(1)}, bf16[2,18,16,128]{3,2,1,0:T(8,128)(2,1)S(1)}, u32[]{:S(2)}, u32[]{:S(2)}) collective-permute-start(bf16[2,18,16,128]{3,2,1,0:T(8,128)(2,1)S(1)} %get-tuple-element.63), channel_id=1, source_target_pairs={{0,8},{4,12},{8,0},{12,4},{16,24},{20,28},{24,16},{28,20},{1,9},{5... | collective-permute-start | bytes 442376 | tf_op jit(solution)/shard_map/ppermute | solution.py:77
  26.1 12.9 %collective-permute-start.7 = (bf16[2,18,16,128]{3,2,1,0:T(8,128)(2,1)S(1)}, bf16[2,18,16,128]{3,2,1,0:T(8,128)(2,1)S(1)}, u32[]{:S(2)}, u32[]{:S(2)}) collective-permute-start(bf16[2,18,16,128]{3,2,1,0:T(8,128)(2,1)S(1)} %get-tuple-element.64), channel_id=1, source_target_pairs={{0,4},{4,0},{8,12},{12,8},{16,20},{20,16},{24,28},{28,24},{1,5},{5... | collective-permute-start | bytes 442376 | tf_op jit(solution)/shard_map/ppermute | solution.py:77
  35.9 11.4 %collective-permute-start.8 = (bf16[4,18,16,128]{3,2,1,0:T(8,128)(2,1)S(1)}, bf16[4,18,16,128]{3,2,1,0:T(8,128)(2,1)S(1)}, u32[]{:S(2)}, u32[]{:S(2)}) collective-permute-start(bf16[4,18,16,128]{3,2,1,0:T(8,128)(2,1)S(1)} %get-tuple-element.69), channel_id=1, source_target_pairs={{0,4},{4,0},{8,12},{12,8},{16,20},{20,16},{24,28},{28,24},{1,5},{5... | collective-permute-start | bytes 884744 | tf_op jit(solution)/shard_map/ppermute | solution.py:77
  37.2 14.1 %collective-permute-start.12 = (bf16[4,18,16,128]{3,2,1,0:T(8,128)(2,1)S(1)}, bf16[4,18,16,128]{3,2,1,0:T(8,128)(2,1)S(1)}, u32[]{:S(2)}, u32[]{:S(2)}) collective-permute-start(bf16[4,18,16,128]{3,2,1,0:T(8,128)(2,1)S(1)} %get-tuple-element.78), channel_id=1, source_target_pairs={{0,16},{4,20},{8,24},{12,28},{16,0},{20,4},{24,8},{28,12},{1,17},{... | collective-permute-start | bytes 884744 | tf_op jit(solution)/shard_map/ppermute | solution.py:77
  37.3 14.1 %collective-permute-start.9 = (bf16[4,18,16,128]{3,2,1,0:T(8,128)(2,1)S(1)}, bf16[4,18,16,128]{3,2,1,0:T(8,128)(2,1)S(1)}, u32[]{:S(2)}, u32[]{:S(2)}) collective-permute-start(bf16[4,18,16,128]{3,2,1,0:T(8,128)(2,1)S(1)} %get-tuple-element.72), channel_id=1, source_target_pairs={{0,8},{4,12},{8,0},{12,4},{16,24},{20,28},{24,16},{28,20},{1,9},{5... | collective-permute-start | bytes 884744 | tf_op jit(solution)/shard_map/ppermute | solution.py:77
  39.8 18.2 %collective-permute-start.11 = (bf16[18,64,128]{2,1,0:T(8,128)(2,1)S(1)}, bf16[18,64,128]{2,1,0:T(8,128)(2,1)S(1)}, u32[]{:S(2)}, u32[]{:S(2)}) collective-permute-start(bf16[18,64,128]{2,1,0:T(8,128)(2,1)S(1)} %get-tuple-element.91), channel_id=1, source_target_pairs={{1,0},{2,1},{3,2},{5,4},{6,5},{7,6},{9,8},{10,9},{11,10},{13,12},{... | collective-permute-start | bytes 884744 | tf_op jit(solution)/shard_map/ppermute | solution.py:375
  41.1 16.9 %collective-permute-start.10 = (bf16[18,64,128]{2,1,0:T(8,128)(2,1)S(1)}, bf16[18,64,128]{2,1,0:T(8,128)(2,1)S(1)}, u32[]{:S(2)}, u32[]{:S(2)}) collective-permute-start(bf16[18,64,128]{2,1,0:T(8,128)(2,1)S(1)} %get-tuple-element.92), channel_id=1, source_target_pairs={{0,1},{1,2},{2,3},{4,5},{5,6},{6,7},{8,9},{9,10},{10,11},{12,13},{... | collective-permute-start | bytes 884744 | tf_op jit(solution)/shard_map/ppermute | solution.py:374
  47.3 17.6 %collective-permute-start.13 = (bf16[2,18,16,128]{3,2,1,0:T(8,128)(2,1)S(1)}, bf16[2,18,16,128]{3,2,1,0:T(8,128)(2,1)S(1)}, u32[]{:S(2)}, u32[]{:S(2)}) collective-permute-start(bf16[2,18,16,128]{3,2,1,0:T(8,128)(2,1)S(1)} %get-tuple-element.83), channel_id=1, source_target_pairs={{0,24},{4,28},{8,16},{12,20},{16,8},{20,12},{24,0},{28,4},{1,25},{... | collective-permute-start | bytes 442376 | tf_op jit(solution)/shard_map/ppermute | solution.py:77
  51.3 13.7 %collective-permute-start.14 = (bf16[2,18,16,128]{3,2,1,0:T(8,128)(2,1)S(1)}, bf16[2,18,16,128]{3,2,1,0:T(8,128)(2,1)S(1)}, u32[]{:S(2)}, u32[]{:S(2)}) collective-permute-start(bf16[2,18,16,128]{3,2,1,0:T(8,128)(2,1)S(1)} %get-tuple-element.84), channel_id=1, source_target_pairs={{0,16},{4,20},{8,24},{12,28},{16,0},{20,4},{24,8},{28,12},{1,17},{... | collective-permute-start | bytes 442376 | tf_op jit(solution)/shard_map/ppermute | solution.py:77
  51.4 13.6 %collective-permute-start.15 = (bf16[2,18,16,128]{3,2,1,0:T(8,128)(2,1)S(1)}, bf16[2,18,16,128]{3,2,1,0:T(8,128)(2,1)S(1)}, u32[]{:S(2)}, u32[]{:S(2)}) collective-permute-start(bf16[2,18,16,128]{3,2,1,0:T(8,128)(2,1)S(1)} %get-tuple-element.85), channel_id=1, source_target_pairs={{0,8},{4,12},{8,0},{12,4},{16,24},{20,28},{24,16},{28,20},{1,9},{5... | collective-permute-start | bytes 442376 | tf_op jit(solution)/shard_map/ppermute | solution.py:77
  65.0 17.6 %copy-start.2 = (f32[256]{0:T(256)S(1)}, f32[256]{0:T(256)}, u32[]{:S(2)}) copy-start(f32[256]{0:T(256)} %param.6) | copy-start | bytes 3076
  65.0 17.5 %copy-start.3 = (f32[256]{0:T(256)S(1)}, f32[256]{0:T(256)}, u32[]{:S(2)}) copy-start(f32[256]{0:T(256)} %param.7) | copy-start | bytes 3076

commit v4 on v3

--- a/solution.py
+++ b/solution.py
@@ -32,7 +32,7 @@
     return wrapped
 
 
-def on_core(body, outs, scalar, arrays, scratch=(), limit=28, specs=None):
+def on_core(body, outs, scalar, arrays, scratch=(), limit=28, specs=None, flops=0):
     mark, *given = pl.pallas_call(
         handing_on(body, len(arrays)),
         out_shape=[MARK] + outs,
@@ -40,7 +40,7 @@
         out_specs=[VMEM] + [VMEM] * len(outs),
         scratch_shapes=list(scratch),
         compiler_params=pltpu.CompilerParams(vmem_limit_bytes=limit * MIB),
-        cost_estimate=pl.CostEstimate(flops=0, bytes_accessed=0, transcendentals=0),
+        cost_estimate=pl.CostEstimate(flops=flops, bytes_accessed=0, transcendentals=0),
     )(*scalar, *arrays)
     return (scalar[0], mark), *given
 
@@ -58,8 +58,8 @@
 
 
 class Trip:
-    def __init__(self, rows, groups):
-        self.rows = rows
+    def __init__(self, rows, groups, joined=False):
+        self.rows, self.joined = rows, joined
         self.groups = [g for g in groups if g]
         self.count = 1 << sum(len(g) for g in self.groups)
         self.place = {(0, m): None for m in range(self.count)}
@@ -76,41 +76,53 @@
         for (mask, wanted), block in zip(self.leaving().items(), blocks):
             got = lax.ppermute(block, "tm", [(i, i ^ mask) for i in range(self.count)])
             for i, (source, dest) in enumerate(wanted):
-                self.place[(source ^ mask, dest ^ mask)] = (len(self.arrays), i)
+                slab = self.joined and not self.steps
+                self.place[(source ^ mask, dest ^ mask)] = (len(self.arrays), (dest ^ mask,) if slab else i)
             self.arrays.append(got)
         self.steps += 1
 
-    def step(self, me, after=()):
+    def step(self, me, flops=0):
         places = [[self.place[k] for k in wanted] for wanted in self.leaving().values()]
 
         def body(me_ref, *refs):
             for out, chosen in zip(refs[-len(places) :], places):
                 for i, (array, at) in enumerate(chosen):
-                    out[i] = refs[array][at]
+                    out[i] = self.window(me_ref[0], refs[array], at)
 
         outs = [shape((len(p),) + self.arrays[0].shape[1:], BF16) for p in places]
-        me, *blocks = on_core(body, outs, me, self.arrays + list(after), limit=24)
+        me, *blocks = on_core(body, outs, me, self.arrays, limit=24, flops=flops)
         self.swap(blocks)
         return me
 
     def gather(self, me, refs, blocks):
         for source in range(self.count):
             array, at = self.place[(source, 0)]
-            blocks[me ^ source] = refs[array][at]
-
-
-def part_body(trips, me_ref, video, *refs):
+            blocks[me ^ source] = self.window(me, refs[array], at)
+
+    def window(self, me, ref, at):
+        if not isinstance(at, tuple):
+            return ref[at]
+        half = self.count // 2
+        columns = (ref.shape[0] - 2) // half
+        return ref[pl.ds(((me ^ at[0]) & (half - 1)) * columns, columns + 2)]
+
+
+def part_body(trips, places, me_ref, video, *refs):
     *outs, wide = refs
     width = video.shape[2]
     columns = width // trips[0].count
     for i, trip in enumerate(trips):
-        cells = jnp.swapaxes(jnp.concatenate([video[:, h] for h in trip.rows], 0), 0, 1)
+        cells = jnp.swapaxes(jnp.concatenate([video[:, h] for h in places[i]], 0), 0, 1)
         edge = jnp.zeros((1,) + cells.shape[1:], BF16)
         wide[0:1] = edge
         wide[1 : width + 1] = cells
         wide[width + 1 : width + 2] = edge
-        for _, masks in trip.first:
+        for mask, masks in trip.first:
             out = outs.pop(0)
+            if mask and trip.joined:
+                other = 1 - (me_ref[0] & mask) // mask
+                out[...] = wide[pl.ds(other * (width // 2), width // 2 + 2)]
+                continue
             for place, mask in enumerate(masks):
                 out[place] = wide[pl.ds((me_ref[0] ^ mask) * columns, columns + 2)]
 
@@ -126,8 +138,13 @@
         kept = [m for m in range(count) if m not in away]
         trip.first = [(0, kept)] + [(m, [k[1] for k in wanted]) for m, wanted in leaving.items()]
         trip.place.update({(0, m): (0, i) for i, m in enumerate(kept)})
-        outs += [shape((len(masks),) + tail, BF16) for _, masks in trip.first]
-    body = functools.partial(part_body, trips)
+        slab = (width // 2 + 2,) + tail[1:]
+        outs += [shape(slab if m and trip.joined else (len(masks),) + tail, BF16) for m, masks in trip.first]
+    places = [trip.rows for trip in trips]
+    if len(trips) == 1:
+        video = jnp.concatenate([video[:, h : h + 1] for h in trips[0].rows], 1)
+        places = [(0, 1)]
+    body = functools.partial(part_body, trips, places)
     scratch = [pltpu.VMEM((width + 2, 2 * frames, channels), BF16)]
     me, *parts = on_core(body, outs, me, [video], scratch, limit=24)
     for trip in trips:
@@ -344,13 +361,15 @@
     me = (me, jnp.zeros(MARK.shape, MARK.dtype))
     bits = count.bit_length() - 1
     top, rest = bits - 1, list(range(1, bits - 1))
-    outer_trip = Trip((0, 7), [[top], [0] + rest])
+    outer_trip = Trip((0, 7), [[top], [0] + rest], joined=True)
     third_trip = Trip((2, 5), [[0], [top], rest])
     second_trip = Trip((1, 6), [rest, [0], [top]])
     inner_trip = Trip((3, 4), [[0], rest + [top]])
     trips = [outer_trip, third_trip, second_trip, inner_trip]
-    me = part_rows(me, video, trips)
-    for trip in (outer_trip, third_trip, second_trip, third_trip, second_trip):
+    me = part_rows(me, video, trips[:1])
+    me = part_rows(me, video, trips[1:])
+    me = outer_trip.step(me, flops=3 * 10**9)
+    for trip in (third_trip, second_trip, third_trip, second_trip):
         me = trip.step(me)
 
     def blocks(rows):

time: 86.3 us -> 83.7 us (0.970)
  starting transfers between devices: 24.9 us -> 23.6 us
    unnamed x8, local copies, waits for them, and re-layouts: 1.61 us -> 0.02 us
    ppermute x14, starting transfers between devices: 20.4 us -> 19.1 us  [swap(): got = lax.ppermute(block, 'tm', [(i, i ^ mask) for i in range(self.count)])]
    slice x0 -> x1, local copies, waits for them, and re-layouts: none -> 1.21 us  [part_rows(): video = jnp.concatenate([video[:, h:h + 1] for h in trips[0].rows], 1)]
    pallas_call x12 -> x13, Pallas kernels: 22.5 us -> 22.4 us  [on_core(): pl.pallas_call(handing_on(body, len(arrays)), out_shape=[MARK] + outs, in...]
  transfers between devices with their start and end apart: 16 -> 16, of which waited for: 5 -> 5; matrix products, arithmetic and copies ran while one was open for 0% -> 0% of each run, Pallas kernels for 18% -> 20%
where the time goes in v4:
time: 83.7 us; the launch traced here: 83.5 us
  Pallas kernels  26 us (31%)
  starting transfers between devices  23.6 us (28%)
  waiting for transfers between devices  20.7 us (25%)
  blocking collectives  11.5 us (14%)
  local copies, waits for them, and re-layouts  1.28 us (2%)
    pallas_call x13, Pallas kernels, on_core(): pl.pallas_call(handing_on(body, len(arrays)), out_shape=[MARK] + outs, in...  22.4 us
    ppermute x14, waiting for transfers between devices, swap(): got = lax.ppermute(block, 'tm', [(i, i ^ mask) for i in range(self.count)])  20.7 us
    ppermute x14, starting transfers between devices, swap(): got = lax.ppermute(block, 'tm', [(i, i ^ mask) for i in range(self.count)])  19.1 us
    all_to_all x1, blocking collectives, per_device(): messages = lax.all_to_all(message, ('tm', 'rows'), 0, 0, tiled=True)  11.5 us
    pallas_call x1, Pallas kernels, per_device(): pl.pallas_call(functools.partial(norm_body, float(height * columns * time...  3.57 us
    ppermute x1, starting transfers between devices, per_device(): above = lax.ppermute(plain[1], 'rows', down)  3.23 us
  transfers between devices with their start and end apart: 16, of which 5 were waited for; matrix products, arithmetic and copies ran while one was open for 0% of the time, Pallas kernels for 20%

profile of v4, /device:TPU:0, one launch (start us, length us, event | category | flops | bytes accessed | tf_op | source)
XLA Modules:
  0.0 83.5 jit_solution(5925014447074597211)
XLA Ops:
  0.0 1.2 %fusion = (bf16[8,1,128,128]{3,2,1,0:T(8,128)(2,1)S(1)}, bf16[8,1,128,128]{3,2,1,0:T(8,128)(2,1)S(1)}) fusion(bf16[8,8,128,128]{3,2,1,0:T(8,128)(2,1)} %refs_0_.5), kind=kLoop, calls=%fused_computation.3 | loop fusion | bytes 1048576 | tf_op jit(solution)/shard_map/slice | solution.py:145
  1.2 0.1 pad_maximum_fusion.refs_0_
  1.3 0.3 shard_map.46
  1.6 4.1 %collective-permute-start = (bf16[66,16,128]{2,1,0:T(8,128)(2,1)S(1)}, bf16[66,16,128]{2,1,0:T(8,128)(2,1)S(1)}, u32[]{:S(2)}, u32[]{:S(2)}) collective-permute-start(bf16[66,16,128]{2,1,0:T(8,128)(2,1)S(1)} %get-tuple-element.52), channel_id=1, source_target_pairs={{0,16},{4,20},{8,24},{12,28},{16,0},{20,4},{24,8},{28,12},{1,17},{... | collective-permute-start | bytes 811016 | tf_op jit(solution)/shard_map/ppermute | solution.py:77
  5.7 0.0 copy-done.1
  5.7 0.9 %shard_map.47 = (f32[8,128]{1,0:T(8,128)S(1)}, bf16[4,18,16,128]{3,2,1,0:T(8,128)(2,1)S(1)}, bf16[4,18,16,128]{3,2,1,0:T(8,128)(2,1)S(1)}, bf16[4,18,16,128]{3,2...) custom-call(s32[1]{0:T(128)} %bitcast.me_ref, ...), custom_call_target="tpu_custom_call" | custom-call | tf_op jit(solution)/shard_map/pallas_call | solution.py:36
  6.6 1.6 %collective-permute-start.1 = (bf16[4,18,16,128]{3,2,1,0:T(8,128)(2,1)S(1)}, bf16[4,18,16,128]{3,2,1,0:T(8,128)(2,1)S(1)}, u32[]{:S(2)}, u32[]{:S(2)}) collective-permute-start(bf16[4,18,16,128]{3,2,1,0:T(8,128)(2,1)S(1)} %get-tuple-element.55), channel_id=1, source_target_pairs={{0,4},{4,0},{8,12},{12,8},{16,20},{20,16},{24,28},{28,24},{1,5},{5... | collective-permute-start | bytes 884744 | tf_op jit(solution)/shard_map/ppermute | solution.py:77
  8.2 1.6 %collective-permute-start.2 = (bf16[4,18,16,128]{3,2,1,0:T(8,128)(2,1)S(1)}, bf16[4,18,16,128]{3,2,1,0:T(8,128)(2,1)S(1)}, u32[]{:S(2)}, u32[]{:S(2)}) collective-permute-start(bf16[4,18,16,128]{3,2,1,0:T(8,128)(2,1)S(1)} %get-tuple-element.58), channel_id=1, source_target_pairs={{0,8},{4,12},{8,0},{12,4},{16,24},{20,28},{24,16},{28,20},{1,9},{5... | collective-permute-start | bytes 884744 | tf_op jit(solution)/shard_map/ppermute | solution.py:77
  9.7 8.4 %collective-permute-done.refs_1_ = bf16[66,16,128]{2,1,0:T(8,128)(2,1)S(1)} collective-permute-done((bf16[66,16,128]{2,1,0:T(8,128)(2,1)S(1)}, bf16[66,16,128]{2,1,0:T(8,128)(2,1)S(1)}, u32[]{:S(2)}, u32[]{:S(2)}) %collective-permute-start) | collective-permute-done | bytes 270368 | tf_op jit(solution)/shard_map/ppermute | solution.py:77
  18.1 0.0 collective-permute-done.1.refs_1_.refs_3_
  18.2 0.1 collective-permute-start.3
  18.2 2.7 %collective-permute-done.2.refs_1_.refs_7_ = bf16[4,18,16,128]{3,2,1,0:T(8,128)(2,1)S(1)} collective-permute-done((bf16[4,18,16,128]{3,2,1,0:T(8,128)(2,1)S(1)}, bf16[4,18,16,128]{3,2,1,0:T(8,128)(2,1)S(1)}, u32[]{:S(2)}, u32[]{:S(2)}) %collective-permute-start.2) | collective-permute-done | bytes 294944 | tf_op jit(solution)/shard_map/ppermute | solution.py:77
  21.0 0.0 copy-start
  21.0 0.6 collective-permute-start.4
  21.7 2.2 %collective-permute-start.5 = (bf16[2,18,16,128]{3,2,1,0:T(8,128)(2,1)S(1)}, bf16[2,18,16,128]{3,2,1,0:T(8,128)(2,1)S(1)}, u32[]{:S(2)}, u32[]{:S(2)}) collective-permute-start(bf16[2,18,16,128]{3,2,1,0:T(8,128)(2,1)S(1)} %get-tuple-element.64), channel_id=1, source_target_pairs={{0,12},{4,8},{8,4},{12,0},{16,28},{20,24},{24,20},{28,16},{1,13},{... | collective-permute-start | bytes 442376 | tf_op jit(solution)/shard_map/ppermute | solution.py:77
  23.9 0.7 collective-permute-start.6
  24.6 0.8 collective-permute-start.7
  25.4 8.3 %collective-permute-done.3.refs_2_.refs_4_ = bf16[4,18,16,128]{3,2,1,0:T(8,128)(2,1)S(1)} collective-permute-done((bf16[4,18,16,128]{3,2,1,0:T(8,128)(2,1)S(1)}, bf16[4,18,16,128]{3,2,1,0:T(8,128)(2,1)S(1)}, u32[]{:S(2)}, u32[]{:S(2)}) %collective-permute-start.3) | collective-permute-done | bytes 294944 | tf_op jit(solution)/shard_map/ppermute | solution.py:77
  33.7 1.2 %collective-permute-start.8 = (bf16[4,18,16,128]{3,2,1,0:T(8,128)(2,1)S(1)}, bf16[4,18,16,128]{3,2,1,0:T(8,128)(2,1)S(1)}, u32[]{:S(2)}, u32[]{:S(2)}) collective-permute-start(bf16[4,18,16,128]{3,2,1,0:T(8,128)(2,1)S(1)} %get-tuple-element.71), channel_id=1, source_target_pairs={{0,4},{4,0},{8,12},{12,8},{16,20},{20,16},{24,28},{28,24},{1,5},{5... | collective-permute-start | bytes 884744 | tf_op jit(solution)/shard_map/ppermute | solution.py:77
  35.0 0.0 collective-permute-done.4.refs_2_.refs_8_
  35.0 0.1 collective-permute-start.12
  35.1 0.0 collective-permute-done.5.refs_2_
  35.1 1.9 %collective-permute-start.9 = (bf16[4,18,16,128]{3,2,1,0:T(8,128)(2,1)S(1)}, bf16[4,18,16,128]{3,2,1,0:T(8,128)(2,1)S(1)}, u32[]{:S(2)}, u32[]{:S(2)}) collective-permute-start(bf16[4,18,16,128]{3,2,1,0:T(8,128)(2,1)S(1)} %get-tuple-element.74), channel_id=1, source_target_pairs={{0,8},{4,12},{8,0},{12,4},{16,24},{20,28},{24,16},{28,20},{1,9},{5... | collective-permute-start | bytes 884744 | tf_op jit(solution)/shard_map/ppermute | solution.py:77
  37.0 0.0 collective-permute-done.6.refs_3_
  37.0 0.0 collective-permute-done.7.refs_4_
  37.0 0.7 shard_map.53
  37.8 1.3 %collective-permute-start.11 = (bf16[18,64,128]{2,1,0:T(8,128)(2,1)S(1)}, bf16[18,64,128]{2,1,0:T(8,128)(2,1)S(1)}, u32[]{:S(2)}, u32[]{:S(2)}) collective-permute-start(bf16[18,64,128]{2,1,0:T(8,128)(2,1)S(1)} %get-tuple-element.95), channel_id=1, source_target_pairs={{1,0},{2,1},{3,2},{5,4},{6,5},{7,6},{9,8},{10,9},{11,10},{13,12},{... | collective-permute-start | bytes 884744 | tf_op jit(solution)/shard_map/ppermute | solution.py:394
  39.1 3.2 %collective-permute-start.10 = (bf16[18,64,128]{2,1,0:T(8,128)(2,1)S(1)}, bf16[18,64,128]{2,1,0:T(8,128)(2,1)S(1)}, u32[]{:S(2)}, u32[]{:S(2)}) collective-permute-start(bf16[18,64,128]{2,1,0:T(8,128)(2,1)S(1)} %get-tuple-element.96), channel_id=1, source_target_pairs={{0,1},{1,2},{2,3},{4,5},{5,6},{6,7},{8,9},{9,10},{10,11},{12,13},{... | collective-permute-start | bytes 884744 | tf_op jit(solution)/shard_map/ppermute | solution.py:393
  42.4 2.9 %shard_map.54 = (f32[8,128]{1,0:T(8,128)S(1)}, f32[2,16,64,256]{3,2,1,0:T(8,128)S(1)}, f32[2,16,64,256]{3,2,1,0:T(8,128)S(1)}) custom-call(s32[1]{0:T(128)} %bitcast.me_ref, f32[8,128]{1,0:T(8,128)S(1)} %get-tuple-element.67.before, bf16[3,3,3,128,256]{4,3,2,1,0:T(8,128)(2,1)S(1)} %copy-done, bf16[2,18,64,384]{3,2,1,0:T(8,128)(2,1)S(1)} %get-tuple-element.68.refs_1_), custom_call_target="tpu_custom_call" | custom-call | tf_op jit(solution)/shard_map/pallas_call | solution.py:36
  45.2 0.0 collective-permute-done.8.refs_1_.refs_5_
  45.3 2.5 %collective-permute-start.13 = (bf16[2,18,16,128]{3,2,1,0:T(8,128)(2,1)S(1)}, bf16[2,18,16,128]{3,2,1,0:T(8,128)(2,1)S(1)}, u32[]{:S(2)}, u32[]{:S(2)}) collective-permute-start(bf16[2,18,16,128]{3,2,1,0:T(8,128)(2,1)S(1)} %get-tuple-element.85), channel_id=1, source_target_pairs={{0,24},{4,28},{8,16},{12,20},{16,8},{20,12},{24,0},{28,4},{1,25},{... | collective-permute-start | bytes 442376 | tf_op jit(solution)/shard_map/ppermute | solution.py:77
  47.8 1.2 %collective-permute-done.12.refs_9_ = bf16[4,18,16,128]{3,2,1,0:T(8,128)(2,1)S(1)} collective-permute-done((bf16[4,18,16,128]{3,2,1,0:T(8,128)(2,1)S(1)}, bf16[4,18,16,128]{3,2,1,0:T(8,128)(2,1)S(1)}, u32[]{:S(2)}, u32[]{:S(2)}) %collective-permute-start.12) | collective-permute-done | bytes 294944 | tf_op jit(solution)/shard_map/ppermute | solution.py:77
  49.0 0.0 collective-permute-start.14
  49.0 0.1 collective-permute-done.9.refs_5_
  49.1 1.7 %collective-permute-start.15 = (bf16[2,18,16,128]{3,2,1,0:T(8,128)(2,1)S(1)}, bf16[2,18,16,128]{3,2,1,0:T(8,128)(2,1)S(1)}, u32[]{:S(2)}, u32[]{:S(2)}) collective-permute-start(bf16[2,18,16,128]{3,2,1,0:T(8,128)(2,1)S(1)} %get-tuple-element.87), channel_id=1, source_target_pairs={{0,8},{4,12},{8,0},{12,4},{16,24},{20,28},{24,16},{28,20},{1,9},{5... | collective-permute-start | bytes 442376 | tf_op jit(solution)/shard_map/ppermute | solution.py:77
  50.8 5.0 %shard_map.56 = (f32[8,128]{1,0:T(8,128)S(1)}, f32[2,16,64,256]{3,2,1,0:T(8,128)S(1)}, f32[2,16,64,256]{3,2,1,0:T(8,128)S(1)}, f32[2,16,64,256]{3,2,1,0:T(8,128)S(1)}) custom-call(s32[1]{0:T(128)} %bitcast.me_ref, f32[8,128]{1,0:T(8,128)S(1)} %get-tuple-element.72.before, bf16[3,3,3,128,256]{4,3,2,1,0:T(8,128)(2,1)S(1)} %copy-done, ...), custom_call_target="tpu_custom_call" | custom-call | tf_op jit(solution)/shard_map/pallas_call | solution.py:36
  55.8 0.0 collective-permute-done.11.refs_2_
  55.8 0.0 collective-permute-done.10.refs_1_
  55.8 6.9 %shard_map.57 = (f32[8,128]{1,0:T(8,128)S(1)}, f32[2,16,64,256]{3,2,1,0:T(8,128)S(1)}, f32[2,16,64,256]{3,2,1,0:T(8,128)S(1)}, f32[2,16,64,256]{3,2,1,0:T(8,128)S(1)}, f32[4,2,256]{2,1,0:T(2,128)S(1)}) custom-call(s32[1]{0:T(128)} %bitcast.me_ref, f32[8,128]{1,0:T(8,128)S(1)} %get-tuple-element.75.before, bf16[3,3,3,128,256]{4,3,2,1,0:T(8,128)(2,1)S(1)} %copy-done, ...), custom_call_target="tpu_custom_call" | custom-call | tf_op jit(solution)/shard_map/pallas_call | solution.py:36
  62.7 0.0 collective-permute-done.13.refs_6_
  62.7 0.0 collective-permute-done.14.refs_7_
  62.7 0.0 collective-permute-done.15.refs_8_
  62.7 0.0 copy-start.2
  62.7 0.0 copy-start.3
  62.7 5.7 %shard_map.58 = (f32[8,128]{1,0:T(8,128)}, f32[2,16,64,256]{3,2,1,0:T(8,128)S(1)}, f32[2,16,64,256]{3,2,1,0:T(8,128)S(1)}, f32[32,1,128]{2,1,0:T(1,128)S(1)}) custom-call(s32[1]{0:T(128)} %bitcast.me_ref, f32[8,128]{1,0:T(8,128)S(1)} %get-tuple-element.81.before, bf16[3,3,3,128,256]{4,3,2,1,0:T(8,128)(2,1)S(1)} %copy-done, ...), custom_call_target="tpu_custom_call" | custom-call | tf_op jit(solution)/shard_map/pallas_call | solution.py:36
  68.4 11.5 %all_to_all.5.all_ref = f32[32,1,128]{2,1,0:T(1,128)S(1)} all-to-all(f32[32,1,128]{2,1,0:T(1,128)S(1)} %get-tuple-element.88), channel_id=1, replica_groups=mesh['tm'=8,'rows'=4] {'tm','rows'}, dimensions={0} | all-to-all | bytes 32768 | tf_op jit(solution)/shard_map/all_to_all | solution.py:418
  79.9 0.0 copy-done.3
  79.9 3.6 %shard_map.59 = bf16[4,8,64,1024]{3,2,1,0:T(8,128)(2,1)} custom-call(f32[32,1,128]{2,1,0:T(1,128)S(1)} %all_to_all.5.all_ref, f32[2,128]{1,0:T(2,128)S(1)} %bitcast.7, f32[2,128]{1,0:T(2,128)S(1)} %bitcast.8, f32[2,16,64,256]{3,2,1,0:T(8,128)S(1)} %get-tuple-element.89.refs_0_, f32[2,16,64,256]{3,2,1,0:T(8,128)S(1)} %get-tuple-element.90.refs_1_, ...), custom_call_target="tpu_custom_call" | custom-call | tf_op jit(solution)/shard_map/pallas_call | solution.py:422
  (11 shorter events, 0.2 us)
Async XLA Ops:
  0.0 5.7 %copy-start.1 = (bf16[8,8,128,128]{3,2,1,0:T(8,128)(2,1)S(1)}, bf16[8,8,128,128]{3,2,1,0:T(8,128)(2,1)}, u32[]{:S(2)}) copy-start(bf16[8,8,128,128]{3,2,1,0:T(8,128)(2,1)} %refs_0_.5) | copy-start | bytes 6291460
  1.6 16.5 %collective-permute-start = (bf16[66,16,128]{2,1,0:T(8,128)(2,1)S(1)}, bf16[66,16,128]{2,1,0:T(8,128)(2,1)S(1)}, u32[]{:S(2)}, u32[]{:S(2)}) collective-permute-start(bf16[66,16,128]{2,1,0:T(8,128)(2,1)S(1)} %get-tuple-element.52), channel_id=1, source_target_pairs={{0,16},{4,20},{8,24},{12,28},{16,0},{20,4},{24,8},{28,12},{1,17},{... | collective-permute-start | bytes 811016 | tf_op jit(solution)/shard_map/ppermute | solution.py:77
  6.6 11.5 %collective-permute-start.1 = (bf16[4,18,16,128]{3,2,1,0:T(8,128)(2,1)S(1)}, bf16[4,18,16,128]{3,2,1,0:T(8,128)(2,1)S(1)}, u32[]{:S(2)}, u32[]{:S(2)}) collective-permute-start(bf16[4,18,16,128]{3,2,1,0:T(8,128)(2,1)S(1)} %get-tuple-element.55), channel_id=1, source_target_pairs={{0,4},{4,0},{8,12},{12,8},{16,20},{20,16},{24,28},{28,24},{1,5},{5... | collective-permute-start | bytes 884744 | tf_op jit(solution)/shard_map/ppermute | solution.py:77
  8.2 12.8 %collective-permute-start.2 = (bf16[4,18,16,128]{3,2,1,0:T(8,128)(2,1)S(1)}, bf16[4,18,16,128]{3,2,1,0:T(8,128)(2,1)S(1)}, u32[]{:S(2)}, u32[]{:S(2)}) collective-permute-start(bf16[4,18,16,128]{3,2,1,0:T(8,128)(2,1)S(1)} %get-tuple-element.58), channel_id=1, source_target_pairs={{0,8},{4,12},{8,0},{12,4},{16,24},{20,28},{24,16},{28,20},{1,9},{5... | collective-permute-start | bytes 884744 | tf_op jit(solution)/shard_map/ppermute | solution.py:77
  18.2 15.5 %collective-permute-start.3 = (bf16[4,18,16,128]{3,2,1,0:T(8,128)(2,1)S(1)}, bf16[4,18,16,128]{3,2,1,0:T(8,128)(2,1)S(1)}, u32[]{:S(2)}, u32[]{:S(2)}) collective-permute-start(bf16[4,18,16,128]{3,2,1,0:T(8,128)(2,1)S(1)} %get-tuple-element.60), channel_id=1, source_target_pairs={{0,16},{4,20},{8,24},{12,28},{16,0},{20,4},{24,8},{28,12},{1,17},{... | collective-permute-start | bytes 884744 | tf_op jit(solution)/shard_map/ppermute | solution.py:77
  21.0 21.4 %copy-start = (bf16[3,3,3,128,256]{4,3,2,1,0:T(8,128)(2,1)S(1)}, bf16[3,3,3,128,256]{4,3,2,1,0:T(8,128)(2,1)}, u32[]{:S(2)}) copy-start(bf16[3,3,3,128,256]{4,3,2,1,0:T(8,128)(2,1)} %refs_0_.9) | copy-start | bytes 5308420
  21.0 13.9 %collective-permute-start.4 = (bf16[4,18,16,128]{3,2,1,0:T(8,128)(2,1)S(1)}, bf16[4,18,16,128]{3,2,1,0:T(8,128)(2,1)S(1)}, u32[]{:S(2)}, u32[]{:S(2)}) collective-permute-start(bf16[4,18,16,128]{3,2,1,0:T(8,128)(2,1)S(1)} %get-tuple-element.62), channel_id=1, source_target_pairs={{0,4},{4,0},{8,12},{12,8},{16,20},{20,16},{24,28},{28,24},{1,5},{5... | collective-permute-start | bytes 884744 | tf_op jit(solution)/shard_map/ppermute | solution.py:77
  21.7 13.4 %collective-permute-start.5 = (bf16[2,18,16,128]{3,2,1,0:T(8,128)(2,1)S(1)}, bf16[2,18,16,128]{3,2,1,0:T(8,128)(2,1)S(1)}, u32[]{:S(2)}, u32[]{:S(2)}) collective-permute-start(bf16[2,18,16,128]{3,2,1,0:T(8,128)(2,1)S(1)} %get-tuple-element.64), channel_id=1, source_target_pairs={{0,12},{4,8},{8,4},{12,0},{16,28},{20,24},{24,20},{28,16},{1,13},{... | collective-permute-start | bytes 442376 | tf_op jit(solution)/shard_map/ppermute | solution.py:77
  23.9 13.1 %collective-permute-start.6 = (bf16[2,18,16,128]{3,2,1,0:T(8,128)(2,1)S(1)}, bf16[2,18,16,128]{3,2,1,0:T(8,128)(2,1)S(1)}, u32[]{:S(2)}, u32[]{:S(2)}) collective-permute-start(bf16[2,18,16,128]{3,2,1,0:T(8,128)(2,1)S(1)} %get-tuple-element.65), channel_id=1, source_target_pairs={{0,8},{4,12},{8,0},{12,4},{16,24},{20,28},{24,16},{28,20},{1,9},{5... | collective-permute-start | bytes 442376 | tf_op jit(solution)/shard_map/ppermute | solution.py:77
  24.6 12.5 %collective-permute-start.7 = (bf16[2,18,16,128]{3,2,1,0:T(8,128)(2,1)S(1)}, bf16[2,18,16,128]{3,2,1,0:T(8,128)(2,1)S(1)}, u32[]{:S(2)}, u32[]{:S(2)}) collective-permute-start(bf16[2,18,16,128]{3,2,1,0:T(8,128)(2,1)S(1)} %get-tuple-element.66), channel_id=1, source_target_pairs={{0,4},{4,0},{8,12},{12,8},{16,20},{20,16},{24,28},{28,24},{1,5},{5... | collective-permute-start | bytes 442376 | tf_op jit(solution)/shard_map/ppermute | solution.py:77
  33.7 11.6 %collective-permute-start.8 = (bf16[4,18,16,128]{3,2,1,0:T(8,128)(2,1)S(1)}, bf16[4,18,16,128]{3,2,1,0:T(8,128)(2,1)S(1)}, u32[]{:S(2)}, u32[]{:S(2)}) collective-permute-start(bf16[4,18,16,128]{3,2,1,0:T(8,128)(2,1)S(1)} %get-tuple-element.71), channel_id=1, source_target_pairs={{0,4},{4,0},{8,12},{12,8},{16,20},{20,16},{24,28},{28,24},{1,5},{5... | collective-permute-start | bytes 884744 | tf_op jit(solution)/shard_map/ppermute | solution.py:77
  35.0 14.0 %collective-permute-start.12 = (bf16[4,18,16,128]{3,2,1,0:T(8,128)(2,1)S(1)}, bf16[4,18,16,128]{3,2,1,0:T(8,128)(2,1)S(1)}, u32[]{:S(2)}, u32[]{:S(2)}) collective-permute-start(bf16[4,18,16,128]{3,2,1,0:T(8,128)(2,1)S(1)} %get-tuple-element.80), channel_id=1, source_target_pairs={{0,16},{4,20},{8,24},{12,28},{16,0},{20,4},{24,8},{28,12},{1,17},{... | collective-permute-start | bytes 884744 | tf_op jit(solution)/shard_map/ppermute | solution.py:77
  35.1 14.0 %collective-permute-start.9 = (bf16[4,18,16,128]{3,2,1,0:T(8,128)(2,1)S(1)}, bf16[4,18,16,128]{3,2,1,0:T(8,128)(2,1)S(1)}, u32[]{:S(2)}, u32[]{:S(2)}) collective-permute-start(bf16[4,18,16,128]{3,2,1,0:T(8,128)(2,1)S(1)} %get-tuple-element.74), channel_id=1, source_target_pairs={{0,8},{4,12},{8,0},{12,4},{16,24},{20,28},{24,16},{28,20},{1,9},{5... | collective-permute-start | bytes 884744 | tf_op jit(solution)/shard_map/ppermute | solution.py:77
  37.8 18.0 %collective-permute-start.11 = (bf16[18,64,128]{2,1,0:T(8,128)(2,1)S(1)}, bf16[18,64,128]{2,1,0:T(8,128)(2,1)S(1)}, u32[]{:S(2)}, u32[]{:S(2)}) collective-permute-start(bf16[18,64,128]{2,1,0:T(8,128)(2,1)S(1)} %get-tuple-element.95), channel_id=1, source_target_pairs={{1,0},{2,1},{3,2},{5,4},{6,5},{7,6},{9,8},{10,9},{11,10},{13,12},{... | collective-permute-start | bytes 884744 | tf_op jit(solution)/shard_map/ppermute | solution.py:394
  39.1 16.7 %collective-permute-start.10 = (bf16[18,64,128]{2,1,0:T(8,128)(2,1)S(1)}, bf16[18,64,128]{2,1,0:T(8,128)(2,1)S(1)}, u32[]{:S(2)}, u32[]{:S(2)}) collective-permute-start(bf16[18,64,128]{2,1,0:T(8,128)(2,1)S(1)} %get-tuple-element.96), channel_id=1, source_target_pairs={{0,1},{1,2},{2,3},{4,5},{5,6},{6,7},{8,9},{9,10},{10,11},{12,13},{... | collective-permute-start | bytes 884744 | tf_op jit(solution)/shard_map/ppermute | solution.py:393
  45.3 17.4 %collective-permute-start.13 = (bf16[2,18,16,128]{3,2,1,0:T(8,128)(2,1)S(1)}, bf16[2,18,16,128]{3,2,1,0:T(8,128)(2,1)S(1)}, u32[]{:S(2)}, u32[]{:S(2)}) collective-permute-start(bf16[2,18,16,128]{3,2,1,0:T(8,128)(2,1)S(1)} %get-tuple-element.85), channel_id=1, source_target_pairs={{0,24},{4,28},{8,16},{12,20},{16,8},{20,12},{24,0},{28,4},{1,25},{... | collective-permute-start | bytes 442376 | tf_op jit(solution)/shard_map/ppermute | solution.py:77
  49.0 13.7 %collective-permute-start.14 = (bf16[2,18,16,128]{3,2,1,0:T(8,128)(2,1)S(1)}, bf16[2,18,16,128]{3,2,1,0:T(8,128)(2,1)S(1)}, u32[]{:S(2)}, u32[]{:S(2)}) collective-permute-start(bf16[2,18,16,128]{3,2,1,0:T(8,128)(2,1)S(1)} %get-tuple-element.86), channel_id=1, source_target_pairs={{0,16},{4,20},{8,24},{12,28},{16,0},{20,4},{24,8},{28,12},{1,17},{... | collective-permute-start | bytes 442376 | tf_op jit(solution)/shard_map/ppermute | solution.py:77
  49.1 13.6 %collective-permute-start.15 = (bf16[2,18,16,128]{3,2,1,0:T(8,128)(2,1)S(1)}, bf16[2,18,16,128]{3,2,1,0:T(8,128)(2,1)S(1)}, u32[]{:S(2)}, u32[]{:S(2)}) collective-permute-start(bf16[2,18,16,128]{3,2,1,0:T(8,128)(2,1)S(1)} %get-tuple-element.87), channel_id=1, source_target_pairs={{0,8},{4,12},{8,0},{12,4},{16,24},{20,28},{24,16},{28,20},{1,9},{5... | collective-permute-start | bytes 442376 | tf_op jit(solution)/shard_map/ppermute | solution.py:77
  62.7 17.2 %copy-start.2 = (f32[256]{0:T(256)S(1)}, f32[256]{0:T(256)}, u32[]{:S(2)}) copy-start(f32[256]{0:T(256)} %param.6) | copy-start | bytes 3076
  62.7 17.2 %copy-start.3 = (f32[256]{0:T(256)S(1)}, f32[256]{0:T(256)}, u32[]{:S(2)}) copy-start(f32[256]{0:T(256)} %param.7) | copy-start | bytes 3076

commit v5 on v4

--- a/solution.py
+++ b/solution.py
@@ -81,7 +81,7 @@
             self.arrays.append(got)
         self.steps += 1
 
-    def step(self, me, flops=0):
+    def step(self, me, flops=0, after=()):
         places = [[self.place[k] for k in wanted] for wanted in self.leaving().values()]
 
         def body(me_ref, *refs):
@@ -90,7 +90,7 @@
                     out[i] = self.window(me_ref[0], refs[array], at)
 
         outs = [shape((len(p),) + self.arrays[0].shape[1:], BF16) for p in places]
-        me, *blocks = on_core(body, outs, me, self.arrays, limit=24, flops=flops)
+        me, *blocks = on_core(body, outs, me, self.arrays + list(after), limit=24, flops=flops)
         self.swap(blocks)
         return me
 
@@ -369,7 +369,9 @@
     me = part_rows(me, video, trips[:1])
     me = part_rows(me, video, trips[1:])
     me = outer_trip.step(me, flops=3 * 10**9)
-    for trip in (third_trip, second_trip, third_trip, second_trip):
+    me = third_trip.step(me)
+    me = second_trip.step(me, after=[inner_trip.arrays[-1]])
+    for trip in (third_trip, second_trip):
         me = trip.step(me)
 
     def blocks(rows):

time: 83.7 us -> 83.1 us (level)
  waiting for transfers between devices: 20.7 us -> 19.5 us
    ppermute x14, waiting for transfers between devices: 20.7 us -> 19.5 us  [swap(): got = lax.ppermute(block, 'tm', [(i, i ^ mask) for i in range(self.count)])]
  transfers between devices with their start and end apart: 16 -> 16, of which waited for: 5 -> 7; matrix products, arithmetic and copies ran while one was open for 0% -> 0% of each run, Pallas kernels for 20% -> 20%
where the time goes in v5:
time: 83.1 us; the launch traced here: 82.9 us
  Pallas kernels  26 us (31%)
  starting transfers between devices  24.2 us (29%)
  waiting for transfers between devices  19.5 us (23%)
  blocking collectives  11.7 us (14%)
  local copies, waits for them, and re-layouts  1.28 us (2%)
    pallas_call x13, Pallas kernels, on_core(): pl.pallas_call(handing_on(body, len(arrays)), out_shape=[MARK] + outs, in...  22.5 us
    ppermute x14, starting transfers between devices, swap(): got = lax.ppermute(block, 'tm', [(i, i ^ mask) for i in range(self.count)])  19.6 us
    ppermute x14, waiting for transfers between devices, swap(): got = lax.ppermute(block, 'tm', [(i, i ^ mask) for i in range(self.count)])  19.5 us
    all_to_all x1, blocking collectives, per_device(): messages = lax.all_to_all(message, ('tm', 'rows'), 0, 0, tiled=True)  11.7 us
    pallas_call x1, Pallas kernels, per_device(): pl.pallas_call(functools.partial(norm_body, float(height * columns * time...  3.57 us
    ppermute x1, starting transfers between devices, per_device(): above = lax.ppermute(plain[1], 'rows', down)  3.23 us
  transfers between devices with their start and end apart: 16, of which 7 were waited for; matrix products, arithmetic and copies ran while one was open for 0% of the time, Pallas kernels for 20%

profile of v5, /device:TPU:0, one launch (start us, length us, event | category | flops | bytes accessed | tf_op | source)
XLA Modules:
  0.0 82.9 jit_solution(10099703217172001700)
XLA Ops:
  0.0 1.2 %fusion = (bf16[8,1,128,128]{3,2,1,0:T(8,128)(2,1)S(1)}, bf16[8,1,128,128]{3,2,1,0:T(8,128)(2,1)S(1)}) fusion(bf16[8,8,128,128]{3,2,1,0:T(8,128)(2,1)} %refs_0_.5), kind=kLoop, calls=%fused_computation.3 | loop fusion | bytes 1048576 | tf_op jit(solution)/shard_map/slice | solution.py:145
  1.2 0.1 pad_maximum_fusion.refs_0_
  1.3 0.3 shard_map.46
  1.6 4.1 %collective-permute-start = (bf16[66,16,128]{2,1,0:T(8,128)(2,1)S(1)}, bf16[66,16,128]{2,1,0:T(8,128)(2,1)S(1)}, u32[]{:S(2)}, u32[]{:S(2)}) collective-permute-start(bf16[66,16,128]{2,1,0:T(8,128)(2,1)S(1)} %get-tuple-element.52), channel_id=1, source_target_pairs={{0,16},{4,20},{8,24},{12,28},{16,0},{20,4},{24,8},{28,12},{1,17},{... | collective-permute-start | bytes 811016 | tf_op jit(solution)/shard_map/ppermute | solution.py:77
  5.7 0.9 %shard_map.47 = (f32[8,128]{1,0:T(8,128)S(1)}, bf16[4,18,16,128]{3,2,1,0:T(8,128)(2,1)S(1)}, bf16[4,18,16,128]{3,2,1,0:T(8,128)(2,1)S(1)}, bf16[4,18,16,128]{3,2...) custom-call(s32[1]{0:T(128)} %bitcast.me_ref, ...), custom_call_target="tpu_custom_call" | custom-call | tf_op jit(solution)/shard_map/pallas_call | solution.py:36
  6.6 1.6 %collective-permute-start.1 = (bf16[4,18,16,128]{3,2,1,0:T(8,128)(2,1)S(1)}, bf16[4,18,16,128]{3,2,1,0:T(8,128)(2,1)S(1)}, u32[]{:S(2)}, u32[]{:S(2)}) collective-permute-start(bf16[4,18,16,128]{3,2,1,0:T(8,128)(2,1)S(1)} %get-tuple-element.55), channel_id=1, source_target_pairs={{0,4},{4,0},{8,12},{12,8},{16,20},{20,16},{24,28},{28,24},{1,5},{5... | collective-permute-start | bytes 884744 | tf_op jit(solution)/shard_map/ppermute | solution.py:77
  8.2 1.6 %collective-permute-start.2 = (bf16[4,18,16,128]{3,2,1,0:T(8,128)(2,1)S(1)}, bf16[4,18,16,128]{3,2,1,0:T(8,128)(2,1)S(1)}, u32[]{:S(2)}, u32[]{:S(2)}) collective-permute-start(bf16[4,18,16,128]{3,2,1,0:T(8,128)(2,1)S(1)} %get-tuple-element.58), channel_id=1, source_target_pairs={{0,8},{4,12},{8,0},{12,4},{16,24},{20,28},{24,16},{28,20},{1,9},{5... | collective-permute-start | bytes 884744 | tf_op jit(solution)/shard_map/ppermute | solution.py:77
  9.7 0.5 collective-permute-start.3
  10.3 7.8 %collective-permute-done.refs_1_ = bf16[66,16,128]{2,1,0:T(8,128)(2,1)S(1)} collective-permute-done((bf16[66,16,128]{2,1,0:T(8,128)(2,1)S(1)}, bf16[66,16,128]{2,1,0:T(8,128)(2,1)S(1)}, u32[]{:S(2)}, u32[]{:S(2)}) %collective-permute-start) | collective-permute-done | bytes 270368 | tf_op jit(solution)/shard_map/ppermute | solution.py:77
  18.1 0.0 collective-permute-done.1.refs_1_.refs_3_
  18.2 0.1 collective-permute-start.4
  18.2 2.7 %collective-permute-done.2.refs_1_.refs_7_ = bf16[4,18,16,128]{3,2,1,0:T(8,128)(2,1)S(1)} collective-permute-done((bf16[4,18,16,128]{3,2,1,0:T(8,128)(2,1)S(1)}, bf16[4,18,16,128]{3,2,1,0:T(8,128)(2,1)S(1)}, u32[]{:S(2)}, u32[]{:S(2)}) %collective-permute-start.2) | collective-permute-done | bytes 294944 | tf_op jit(solution)/shard_map/ppermute | solution.py:77
  21.0 0.5 collective-permute-done.3.refs_2_.refs_1_.refs_5_
  21.5 0.0 copy-start
  21.5 1.6 %collective-permute-start.5 = (bf16[4,18,16,128]{3,2,1,0:T(8,128)(2,1)S(1)}, bf16[4,18,16,128]{3,2,1,0:T(8,128)(2,1)S(1)}, u32[]{:S(2)}, u32[]{:S(2)}) collective-permute-start(bf16[4,18,16,128]{3,2,1,0:T(8,128)(2,1)S(1)} %get-tuple-element.63), channel_id=1, source_target_pairs={{0,4},{4,0},{8,12},{12,8},{16,20},{20,16},{24,28},{28,24},{1,5},{5... | collective-permute-start | bytes 884744 | tf_op jit(solution)/shard_map/ppermute | solution.py:77
  23.0 1.5 %collective-permute-start.6 = (bf16[2,18,16,128]{3,2,1,0:T(8,128)(2,1)S(1)}, bf16[2,18,16,128]{3,2,1,0:T(8,128)(2,1)S(1)}, u32[]{:S(2)}, u32[]{:S(2)}) collective-permute-start(bf16[2,18,16,128]{3,2,1,0:T(8,128)(2,1)S(1)} %get-tuple-element.65), channel_id=1, source_target_pairs={{0,12},{4,8},{8,4},{12,0},{16,28},{20,24},{24,20},{28,16},{1,13},{... | collective-permute-start | bytes 442376 | tf_op jit(solution)/shard_map/ppermute | solution.py:77
  24.6 0.4 collective-permute-start.7
  25.0 1.5 %collective-permute-start.8 = (bf16[2,18,16,128]{3,2,1,0:T(8,128)(2,1)S(1)}, bf16[2,18,16,128]{3,2,1,0:T(8,128)(2,1)S(1)}, u32[]{:S(2)}, u32[]{:S(2)}) collective-permute-start(bf16[2,18,16,128]{3,2,1,0:T(8,128)(2,1)S(1)} %get-tuple-element.67), channel_id=1, source_target_pairs={{0,4},{4,0},{8,12},{12,8},{16,20},{20,16},{24,28},{28,24},{1,5},{5... | collective-permute-start | bytes 442376 | tf_op jit(solution)/shard_map/ppermute | solution.py:77
  26.5 7.2 %collective-permute-done.4.refs_2_.refs_4_ = bf16[4,18,16,128]{3,2,1,0:T(8,128)(2,1)S(1)} collective-permute-done((bf16[4,18,16,128]{3,2,1,0:T(8,128)(2,1)S(1)}, bf16[4,18,16,128]{3,2,1,0:T(8,128)(2,1)S(1)}, u32[]{:S(2)}, u32[]{:S(2)}) %collective-permute-start.4) | collective-permute-done | bytes 294944 | tf_op jit(solution)/shard_map/ppermute | solution.py:77
  33.7 0.1 collective-permute-done.5.refs_2_.refs_8_
  33.9 0.7 collective-permute-start.12
  34.6 1.3 %collective-permute-start.9 = (bf16[4,18,16,128]{3,2,1,0:T(8,128)(2,1)S(1)}, bf16[4,18,16,128]{3,2,1,0:T(8,128)(2,1)S(1)}, u32[]{:S(2)}, u32[]{:S(2)}) collective-permute-start(bf16[4,18,16,128]{3,2,1,0:T(8,128)(2,1)S(1)} %get-tuple-element.74), channel_id=1, source_target_pairs={{0,8},{4,12},{8,0},{12,4},{16,24},{20,28},{24,16},{28,20},{1,9},{5... | collective-permute-start | bytes 884744 | tf_op jit(solution)/shard_map/ppermute | solution.py:77
  35.9 0.0 collective-permute-done.6.refs_2_
  35.9 0.0 collective-permute-done.7.refs_3_
  35.9 0.0 collective-permute-done.8.refs_4_
  36.0 0.8 shard_map.53
  36.8 1.3 %collective-permute-start.11 = (bf16[18,64,128]{2,1,0:T(8,128)(2,1)S(1)}, bf16[18,64,128]{2,1,0:T(8,128)(2,1)S(1)}, u32[]{:S(2)}, u32[]{:S(2)}) collective-permute-start(bf16[18,64,128]{2,1,0:T(8,128)(2,1)S(1)} %get-tuple-element.95), channel_id=1, source_target_pairs={{1,0},{2,1},{3,2},{5,4},{6,5},{7,6},{9,8},{10,9},{11,10},{13,12},{... | collective-permute-start | bytes 884744 | tf_op jit(solution)/shard_map/ppermute | solution.py:396
  38.1 3.2 %collective-permute-start.10 = (bf16[18,64,128]{2,1,0:T(8,128)(2,1)S(1)}, bf16[18,64,128]{2,1,0:T(8,128)(2,1)S(1)}, u32[]{:S(2)}, u32[]{:S(2)}) collective-permute-start(bf16[18,64,128]{2,1,0:T(8,128)(2,1)S(1)} %get-tuple-element.96), channel_id=1, source_target_pairs={{0,1},{1,2},{2,3},{4,5},{5,6},{6,7},{8,9},{9,10},{10,11},{12,13},{... | collective-permute-start | bytes 884744 | tf_op jit(solution)/shard_map/ppermute | solution.py:395
  41.3 0.0 copy-done
  41.3 2.9 %shard_map.54 = (f32[8,128]{1,0:T(8,128)S(1)}, f32[2,16,64,256]{3,2,1,0:T(8,128)S(1)}, f32[2,16,64,256]{3,2,1,0:T(8,128)S(1)}) custom-call(s32[1]{0:T(128)} %bitcast.me_ref, f32[8,128]{1,0:T(8,128)S(1)} %get-tuple-element.68.before, bf16[3,3,3,128,256]{4,3,2,1,0:T(8,128)(2,1)S(1)} %copy-done, bf16[2,18,64,384]{3,2,1,0:T(8,128)(2,1)S(1)} %get-tuple-element.69.refs_1_), custom_call_target="tpu_custom_call" | custom-call | tf_op jit(solution)/shard_map/pallas_call | solution.py:36
  44.2 3.1 %collective-permute-start.13 = (bf16[2,18,16,128]{3,2,1,0:T(8,128)(2,1)S(1)}, bf16[2,18,16,128]{3,2,1,0:T(8,128)(2,1)S(1)}, u32[]{:S(2)}, u32[]{:S(2)}) collective-permute-start(bf16[2,18,16,128]{3,2,1,0:T(8,128)(2,1)S(1)} %get-tuple-element.85), channel_id=1, source_target_pairs={{0,24},{4,28},{8,16},{12,20},{16,8},{20,12},{24,0},{28,4},{1,25},{... | collective-permute-start | bytes 442376 | tf_op jit(solution)/shard_map/ppermute | solution.py:77
  47.3 1.0 %collective-permute-done.12.refs_9_ = bf16[4,18,16,128]{3,2,1,0:T(8,128)(2,1)S(1)} collective-permute-done((bf16[4,18,16,128]{3,2,1,0:T(8,128)(2,1)S(1)}, bf16[4,18,16,128]{3,2,1,0:T(8,128)(2,1)S(1)}, u32[]{:S(2)}, u32[]{:S(2)}) %collective-permute-start.12) | collective-permute-done | bytes 294944 | tf_op jit(solution)/shard_map/ppermute | solution.py:77
  48.3 0.0 collective-permute-start.14
  48.3 0.1 collective-permute-done.9.refs_5_
  48.4 1.6 %collective-permute-start.15 = (bf16[2,18,16,128]{3,2,1,0:T(8,128)(2,1)S(1)}, bf16[2,18,16,128]{3,2,1,0:T(8,128)(2,1)S(1)}, u32[]{:S(2)}, u32[]{:S(2)}) collective-permute-start(bf16[2,18,16,128]{3,2,1,0:T(8,128)(2,1)S(1)} %get-tuple-element.87), channel_id=1, source_target_pairs={{0,8},{4,12},{8,0},{12,4},{16,24},{20,28},{24,16},{28,20},{1,9},{5... | collective-permute-start | bytes 442376 | tf_op jit(solution)/shard_map/ppermute | solution.py:77
  50.0 5.0 %shard_map.56 = (f32[8,128]{1,0:T(8,128)S(1)}, f32[2,16,64,256]{3,2,1,0:T(8,128)S(1)}, f32[2,16,64,256]{3,2,1,0:T(8,128)S(1)}, f32[2,16,64,256]{3,2,1,0:T(8,128)S(1)}) custom-call(s32[1]{0:T(128)} %bitcast.me_ref, f32[8,128]{1,0:T(8,128)S(1)} %get-tuple-element.72.before, bf16[3,3,3,128,256]{4,3,2,1,0:T(8,128)(2,1)S(1)} %copy-done, ...), custom_call_target="tpu_custom_call" | custom-call | tf_op jit(solution)/shard_map/pallas_call | solution.py:36
  55.0 0.0 collective-permute-done.11.refs_2_
  55.0 0.0 collective-permute-done.10.refs_1_
  55.0 6.9 %shard_map.57 = (f32[8,128]{1,0:T(8,128)S(1)}, f32[2,16,64,256]{3,2,1,0:T(8,128)S(1)}, f32[2,16,64,256]{3,2,1,0:T(8,128)S(1)}, f32[2,16,64,256]{3,2,1,0:T(8,128)S(1)}, f32[4,2,256]{2,1,0:T(2,128)S(1)}) custom-call(s32[1]{0:T(128)} %bitcast.me_ref, f32[8,128]{1,0:T(8,128)S(1)} %get-tuple-element.75.before, bf16[3,3,3,128,256]{4,3,2,1,0:T(8,128)(2,1)S(1)} %copy-done, ...), custom_call_target="tpu_custom_call" | custom-call | tf_op jit(solution)/shard_map/pallas_call | solution.py:36
  61.9 0.0 collective-permute-done.13.refs_6_
  61.9 0.0 collective-permute-done.14.refs_7_
  61.9 0.0 collective-permute-done.15.refs_8_
  61.9 0.0 copy-start.2
  61.9 0.0 copy-start.3
  62.0 5.7 %shard_map.58 = (f32[8,128]{1,0:T(8,128)}, f32[2,16,64,256]{3,2,1,0:T(8,128)S(1)}, f32[2,16,64,256]{3,2,1,0:T(8,128)S(1)}, f32[32,1,128]{2,1,0:T(1,128)S(1)}) custom-call(s32[1]{0:T(128)} %bitcast.me_ref, f32[8,128]{1,0:T(8,128)S(1)} %get-tuple-element.81.before, bf16[3,3,3,128,256]{4,3,2,1,0:T(8,128)(2,1)S(1)} %copy-done, ...), custom_call_target="tpu_custom_call" | custom-call | tf_op jit(solution)/shard_map/pallas_call | solution.py:36
  67.6 11.7 %all_to_all.5.all_ref = f32[32,1,128]{2,1,0:T(1,128)S(1)} all-to-all(f32[32,1,128]{2,1,0:T(1,128)S(1)} %get-tuple-element.88), channel_id=1, replica_groups=mesh['tm'=8,'rows'=4] {'tm','rows'}, dimensions={0} | all-to-all | bytes 32768 | tf_op jit(solution)/shard_map/all_to_all | solution.py:420
  79.3 0.0 copy-done.2
  79.3 3.6 %shard_map.59 = bf16[4,8,64,1024]{3,2,1,0:T(8,128)(2,1)} custom-call(f32[32,1,128]{2,1,0:T(1,128)S(1)} %all_to_all.5.all_ref, f32[2,128]{1,0:T(2,128)S(1)} %bitcast.7, f32[2,128]{1,0:T(2,128)S(1)} %bitcast.8, f32[2,16,64,256]{3,2,1,0:T(8,128)S(1)} %get-tuple-element.89.refs_0_, f32[2,16,64,256]{3,2,1,0:T(8,128)S(1)} %get-tuple-element.90.refs_1_, ...), custom_call_target="tpu_custom_call" | custom-call | tf_op jit(solution)/shard_map/pallas_call | solution.py:424
  (11 shorter events, 0.2 us)
Async XLA Ops:
  0.0 5.7 %copy-start.1 = (bf16[8,8,128,128]{3,2,1,0:T(8,128)(2,1)S(1)}, bf16[8,8,128,128]{3,2,1,0:T(8,128)(2,1)}, u32[]{:S(2)}) copy-start(bf16[8,8,128,128]{3,2,1,0:T(8,128)(2,1)} %refs_0_.5) | copy-start | bytes 6291460
  1.6 16.5 %collective-permute-start = (bf16[66,16,128]{2,1,0:T(8,128)(2,1)S(1)}, bf16[66,16,128]{2,1,0:T(8,128)(2,1)S(1)}, u32[]{:S(2)}, u32[]{:S(2)}) collective-permute-start(bf16[66,16,128]{2,1,0:T(8,128)(2,1)S(1)} %get-tuple-element.52), channel_id=1, source_target_pairs={{0,16},{4,20},{8,24},{12,28},{16,0},{20,4},{24,8},{28,12},{1,17},{... | collective-permute-start | bytes 811016 | tf_op jit(solution)/shard_map/ppermute | solution.py:77
  6.6 11.5 %collective-permute-start.1 = (bf16[4,18,16,128]{3,2,1,0:T(8,128)(2,1)S(1)}, bf16[4,18,16,128]{3,2,1,0:T(8,128)(2,1)S(1)}, u32[]{:S(2)}, u32[]{:S(2)}) collective-permute-start(bf16[4,18,16,128]{3,2,1,0:T(8,128)(2,1)S(1)} %get-tuple-element.55), channel_id=1, source_target_pairs={{0,4},{4,0},{8,12},{12,8},{16,20},{20,16},{24,28},{28,24},{1,5},{5... | collective-permute-start | bytes 884744 | tf_op jit(solution)/shard_map/ppermute | solution.py:77
  8.2 12.8 %collective-permute-start.2 = (bf16[4,18,16,128]{3,2,1,0:T(8,128)(2,1)S(1)}, bf16[4,18,16,128]{3,2,1,0:T(8,128)(2,1)S(1)}, u32[]{:S(2)}, u32[]{:S(2)}) collective-permute-start(bf16[4,18,16,128]{3,2,1,0:T(8,128)(2,1)S(1)} %get-tuple-element.58), channel_id=1, source_target_pairs={{0,8},{4,12},{8,0},{12,4},{16,24},{20,28},{24,16},{28,20},{1,9},{5... | collective-permute-start | bytes 884744 | tf_op jit(solution)/shard_map/ppermute | solution.py:77
  9.7 11.7 %collective-permute-start.3 = (bf16[4,18,16,128]{3,2,1,0:T(8,128)(2,1)S(1)}, bf16[4,18,16,128]{3,2,1,0:T(8,128)(2,1)S(1)}, u32[]{:S(2)}, u32[]{:S(2)}) collective-permute-start(bf16[4,18,16,128]{3,2,1,0:T(8,128)(2,1)S(1)} %get-tuple-element.59), channel_id=1, source_target_pairs={{0,4},{4,0},{8,12},{12,8},{16,20},{20,16},{24,28},{28,24},{1,5},{5... | collective-permute-start | bytes 884744 | tf_op jit(solution)/shard_map/ppermute | solution.py:77
  18.2 15.5 %collective-permute-start.4 = (bf16[4,18,16,128]{3,2,1,0:T(8,128)(2,1)S(1)}, bf16[4,18,16,128]{3,2,1,0:T(8,128)(2,1)S(1)}, u32[]{:S(2)}, u32[]{:S(2)}) collective-permute-start(bf16[4,18,16,128]{3,2,1,0:T(8,128)(2,1)S(1)} %get-tuple-element.61), channel_id=1, source_target_pairs={{0,16},{4,20},{8,24},{12,28},{16,0},{20,4},{24,8},{28,12},{1,17},{... | collective-permute-start | bytes 884744 | tf_op jit(solution)/shard_map/ppermute | solution.py:77
  21.5 19.8 %copy-start = (bf16[3,3,3,128,256]{4,3,2,1,0:T(8,128)(2,1)S(1)}, bf16[3,3,3,128,256]{4,3,2,1,0:T(8,128)(2,1)}, u32[]{:S(2)}) copy-start(bf16[3,3,3,128,256]{4,3,2,1,0:T(8,128)(2,1)} %refs_0_.9) | copy-start | bytes 5308420
  21.5 12.4 %collective-permute-start.5 = (bf16[4,18,16,128]{3,2,1,0:T(8,128)(2,1)S(1)}, bf16[4,18,16,128]{3,2,1,0:T(8,128)(2,1)S(1)}, u32[]{:S(2)}, u32[]{:S(2)}) collective-permute-start(bf16[4,18,16,128]{3,2,1,0:T(8,128)(2,1)S(1)} %get-tuple-element.63), channel_id=1, source_target_pairs={{0,4},{4,0},{8,12},{12,8},{16,20},{20,16},{24,28},{28,24},{1,5},{5... | collective-permute-start | bytes 884744 | tf_op jit(solution)/shard_map/ppermute | solution.py:77
  23.0 12.9 %collective-permute-start.6 = (bf16[2,18,16,128]{3,2,1,0:T(8,128)(2,1)S(1)}, bf16[2,18,16,128]{3,2,1,0:T(8,128)(2,1)S(1)}, u32[]{:S(2)}, u32[]{:S(2)}) collective-permute-start(bf16[2,18,16,128]{3,2,1,0:T(8,128)(2,1)S(1)} %get-tuple-element.65), channel_id=1, source_target_pairs={{0,12},{4,8},{8,4},{12,0},{16,28},{20,24},{24,20},{28,16},{1,13},{... | collective-permute-start | bytes 442376 | tf_op jit(solution)/shard_map/ppermute | solution.py:77
  24.6 11.4 %collective-permute-start.7 = (bf16[2,18,16,128]{3,2,1,0:T(8,128)(2,1)S(1)}, bf16[2,18,16,128]{3,2,1,0:T(8,128)(2,1)S(1)}, u32[]{:S(2)}, u32[]{:S(2)}) collective-permute-start(bf16[2,18,16,128]{3,2,1,0:T(8,128)(2,1)S(1)} %get-tuple-element.66), channel_id=1, source_target_pairs={{0,8},{4,12},{8,0},{12,4},{16,24},{20,28},{24,16},{28,20},{1,9},{5... | collective-permute-start | bytes 442376 | tf_op jit(solution)/shard_map/ppermute | solution.py:77
  25.0 10.9 %collective-permute-start.8 = (bf16[2,18,16,128]{3,2,1,0:T(8,128)(2,1)S(1)}, bf16[2,18,16,128]{3,2,1,0:T(8,128)(2,1)S(1)}, u32[]{:S(2)}, u32[]{:S(2)}) collective-permute-start(bf16[2,18,16,128]{3,2,1,0:T(8,128)(2,1)S(1)} %get-tuple-element.67), channel_id=1, source_target_pairs={{0,4},{4,0},{8,12},{12,8},{16,20},{20,16},{24,28},{28,24},{1,5},{5... | collective-permute-start | bytes 442376 | tf_op jit(solution)/shard_map/ppermute | solution.py:77
  33.9 14.4 %collective-permute-start.12 = (bf16[4,18,16,128]{3,2,1,0:T(8,128)(2,1)S(1)}, bf16[4,18,16,128]{3,2,1,0:T(8,128)(2,1)S(1)}, u32[]{:S(2)}, u32[]{:S(2)}) collective-permute-start(bf16[4,18,16,128]{3,2,1,0:T(8,128)(2,1)S(1)} %get-tuple-element.80), channel_id=1, source_target_pairs={{0,16},{4,20},{8,24},{12,28},{16,0},{20,4},{24,8},{28,12},{1,17},{... | collective-permute-start | bytes 884744 | tf_op jit(solution)/shard_map/ppermute | solution.py:77
  34.6 13.8 %collective-permute-start.9 = (bf16[4,18,16,128]{3,2,1,0:T(8,128)(2,1)S(1)}, bf16[4,18,16,128]{3,2,1,0:T(8,128)(2,1)S(1)}, u32[]{:S(2)}, u32[]{:S(2)}) collective-permute-start(bf16[4,18,16,128]{3,2,1,0:T(8,128)(2,1)S(1)} %get-tuple-element.74), channel_id=1, source_target_pairs={{0,8},{4,12},{8,0},{12,4},{16,24},{20,28},{24,16},{28,20},{1,9},{5... | collective-permute-start | bytes 884744 | tf_op jit(solution)/shard_map/ppermute | solution.py:77
  36.8 18.3 %collective-permute-start.11 = (bf16[18,64,128]{2,1,0:T(8,128)(2,1)S(1)}, bf16[18,64,128]{2,1,0:T(8,128)(2,1)S(1)}, u32[]{:S(2)}, u32[]{:S(2)}) collective-permute-start(bf16[18,64,128]{2,1,0:T(8,128)(2,1)S(1)} %get-tuple-element.95), channel_id=1, source_target_pairs={{1,0},{2,1},{3,2},{5,4},{6,5},{7,6},{9,8},{10,9},{11,10},{13,12},{... | collective-permute-start | bytes 884744 | tf_op jit(solution)/shard_map/ppermute | solution.py:396
  38.1 17.0 %collective-permute-start.10 = (bf16[18,64,128]{2,1,0:T(8,128)(2,1)S(1)}, bf16[18,64,128]{2,1,0:T(8,128)(2,1)S(1)}, u32[]{:S(2)}, u32[]{:S(2)}) collective-permute-start(bf16[18,64,128]{2,1,0:T(8,128)(2,1)S(1)} %get-tuple-element.96), channel_id=1, source_target_pairs={{0,1},{1,2},{2,3},{4,5},{5,6},{6,7},{8,9},{9,10},{10,11},{12,13},{... | collective-permute-start | bytes 884744 | tf_op jit(solution)/shard_map/ppermute | solution.py:395
  44.2 17.7 %collective-permute-start.13 = (bf16[2,18,16,128]{3,2,1,0:T(8,128)(2,1)S(1)}, bf16[2,18,16,128]{3,2,1,0:T(8,128)(2,1)S(1)}, u32[]{:S(2)}, u32[]{:S(2)}) collective-permute-start(bf16[2,18,16,128]{3,2,1,0:T(8,128)(2,1)S(1)} %get-tuple-element.85), channel_id=1, source_target_pairs={{0,24},{4,28},{8,16},{12,20},{16,8},{20,12},{24,0},{28,4},{1,25},{... | collective-permute-start | bytes 442376 | tf_op jit(solution)/shard_map/ppermute | solution.py:77
  48.3 13.6 %collective-permute-start.14 = (bf16[2,18,16,128]{3,2,1,0:T(8,128)(2,1)S(1)}, bf16[2,18,16,128]{3,2,1,0:T(8,128)(2,1)S(1)}, u32[]{:S(2)}, u32[]{:S(2)}) collective-permute-start(bf16[2,18,16,128]{3,2,1,0:T(8,128)(2,1)S(1)} %get-tuple-element.86), channel_id=1, source_target_pairs={{0,16},{4,20},{8,24},{12,28},{16,0},{20,4},{24,8},{28,12},{1,17},{... | collective-permute-start | bytes 442376 | tf_op jit(solution)/shard_map/ppermute | solution.py:77
  48.4 13.5 %collective-permute-start.15 = (bf16[2,18,16,128]{3,2,1,0:T(8,128)(2,1)S(1)}, bf16[2,18,16,128]{3,2,1,0:T(8,128)(2,1)S(1)}, u32[]{:S(2)}, u32[]{:S(2)}) collective-permute-start(bf16[2,18,16,128]{3,2,1,0:T(8,128)(2,1)S(1)} %get-tuple-element.87), channel_id=1, source_target_pairs={{0,8},{4,12},{8,0},{12,4},{16,24},{20,28},{24,16},{28,20},{1,9},{5... | collective-permute-start | bytes 442376 | tf_op jit(solution)/shard_map/ppermute | solution.py:77
  61.9 17.4 %copy-start.2 = (f32[256]{0:T(256)S(1)}, f32[256]{0:T(256)}, u32[]{:S(2)}) copy-start(f32[256]{0:T(256)} %param.6) | copy-start | bytes 3076
  61.9 17.3 %copy-start.3 = (f32[256]{0:T(256)S(1)}, f32[256]{0:T(256)}, u32[]{:S(2)}) copy-start(f32[256]{0:T(256)} %param.7) | copy-start | bytes 3076
